TPU v7x, 512 devices: a whole 4x8x8 slice. The times are simulated.
512 devices in a mesh: blk: 64 (over z, y_hi, core), rhs: 8 (over y_lo, x).
Axes of the slice: x: 4, y: 8 (y_hi: 4, y_lo: 2; y = y_hi * 2 + y_lo), z: 8, core: 2. Of those that a mesh axis runs over, the one named last changes fastest.
Arguments:
- diag_inverse: float32 [64, 512, 512], P('blk', 'rhs'), may hold values from -2 to 2
- coupling: float32 [64, 512, 512], P('blk', 'rhs'), may hold values from -2 to 2
- rhs_t: float32 [512, 32768], P('rhs', 'blk'), may hold values from -2.4 to 2.4
- prior: float32 [512, 512], P('rhs'), may hold values from -6 to 6
- border_factor: float32 [2048, 32768], P('rhs', 'blk'), may hold values from -0.03125 to 0.03125
- border_rhs: float32 [512, 2048], P('rhs'), may hold values from -6 to 6
Outputs:
- solution: float32 [512, 32768], P('rhs', 'blk')
- border_out: float32 [512, 2048], P('rhs')
All inputs are finite; a program needn't handle non-finite values.
Results may differ from a plain program's by a relative error of at most 0.0003.
Values sent between devices are 32-bit elements; how exact they have to be, the bound alone decides.
No kernel may reach another device: no remote copies, remote signals or barrier semaphores. Data moves between devices by JAX's collectives and lax.ppermute only.
A program may use at most 192 MiB of HBM per device.

v0:
```python
import jax
import jax.numpy as jnp
from jax import lax
from jax.sharding import PartitionSpec as P


def passed_along(value, axis, steps):
    count = lax.axis_size(axis)
    leading, last = (max(0, -steps), min(count, count - steps))
    return lax.ppermute(value, axis, [(source, source + steps) for source in range(leading, last)])


def times_transposed(left_side, matrix):
    return lax.dot_general(
        left_side,
        matrix,
        (((1,), (1,)), ((), ())),
        precision=lax.Precision.HIGHEST,
        preferred_element_type=jnp.float32,
    )


def body(diag_inverse, coupling, rhs_t, prior, border_factor, border_rhs):
    full_inverse, full_coupling = (
        lax.all_gather(diag_inverse, "rhs", axis=1, tiled=True),
        lax.all_gather(coupling, "rhs", axis=1, tiled=True),
    )
    inv_block = full_inverse[0]
    link_block = full_coupling[0]
    position = lax.axis_index("blk")

    def advance(turn_index, carried):
        received = passed_along(carried, "blk", 1)

        def solve_here(operand):
            previous = jnp.where(turn_index == 0, prior, operand)
            coupled = times_transposed(previous, link_block)
            return times_transposed(rhs_t - coupled, inv_block)

        def keep_block(operand):
            return carried

        return lax.cond(position == turn_index, solve_here, keep_block, received)

    solved = lax.fori_loop(0, lax.axis_size("blk"), advance, jnp.zeros_like(rhs_t))
    partial_sum = times_transposed(solved, lax.all_gather(border_factor, "rhs", axis=0, tiled=True))
    summed = lax.psum(partial_sum, "blk")
    return (solved, border_rhs - summed)


def solution(mesh):
    placed = (
        P("blk", "rhs", None),
        P("blk", "rhs", None),
        P("rhs", "blk"),
        P("rhs", None),
        P("rhs", "blk"),
        P("rhs", None),
    )
    return jax.shard_map(
        body,
        mesh=mesh,
        in_specs=placed,
        out_specs=(P("rhs", "blk"), P("rhs", None)),
        check_vma=False,
    )
```

profile of v0, /device:TPU:1, one launch (start us, length us, event | category | flops | bytes accessed | tf_op | source)
XLA Modules:
  0.0 1406.2 jit_solution(3253712182647884660)
XLA Ops:
  9.4 45.3 %all-gather.4.cloned.1.call-done = f32[1,512,512]{2,1,0:T(8,128)} async-done(((f32[1,64,512]{2,1,0:T(8,128)}), f32[1,512,512]{2,1,0:T(8,128)}) %all-gather.4.cloned.1.call-update) | async-done | bytes 1048592 | tf_op jit(solution)/shard_map/all_gather | solution.py:26
  54.8 45.5 %all-gather.6.cloned.1.call-done = f32[1,512,512]{2,1,0:T(8,128)} async-done(((f32[1,64,512]{2,1,0:T(8,128)}), f32[1,512,512]{2,1,0:T(8,128)}) %all-gather.6.cloned.1.call-update) | async-done | bytes 1048592 | tf_op jit(solution)/shard_map/all_gather | solution.py:25
  100.3 594.4 %while.16 = (s32[]{:T(128)}, f32[64,512]{1,0:T(8,128)S(1)}, s32[]{:T(128)}, f32[64,512]{1,0:T(8,128)}, f32[512,512]{1,0:T(8,128)}, /*index=5*/f32[64,512]{1,0:T(8,128)}, f32[512,512]{1,0:T(8,128)}, s32[]{:T(128)}) while((s32[]{:T(128)}, f32[64,512]{1,0:T(8,128)S(1)}, s32[]{:T(128)}, f32[64,512]{1,0:T(8,128)}, f32[512,512]{1,0:T(8,128)}, ...), condition=%wide.region_3.4_spmd, body=%wide.region_0.3_spmd.sunk | while | flops 402718720 | bytes 3408085 | solution.py:45
  100.3 9.7 collective-permute-start
  131.3 10.0 collective-permute-start
  310.3 10.8 collective-permute-start
  332.0 7.4 collective-permute-start
  341.4 7.4 collective-permute-start
  350.7 7.4 collective-permute-start
  360.0 7.5 collective-permute-start
  369.3 7.4 collective-permute-start
  406.5 7.4 collective-permute-start
  425.1 7.4 collective-permute-start
  443.7 7.4 collective-permute-start
  462.3 7.4 collective-permute-start
  480.9 7.4 collective-permute-start
  499.5 7.4 collective-permute-start
  583.2 7.4 collective-permute-start
  601.7 7.4 collective-permute-start
  620.3 7.4 collective-permute-start
  638.9 7.4 collective-permute-start
  657.5 7.4 collective-permute-start
  676.1 7.4 collective-permute-start
  701.8 695.9 %all-reduce.2.cloned.1.call-done = f32[64,2048]{1,0:T(8,128)} async-done(((f32[64,2048]{1,0:T(8,128)}), f32[64,2048]{1,0:T(8,128)}) %all-reduce.2.cloned.1.call-update) | async-done | bytes 524304 | tf_op jit(solution)/shard_map/psum | solution.py:47
  (190 shorter events, 453.8 us)
Async XLA Ops:
  7.2 47.6 %all-gather.4.cloned.1.call-start = ((), (), s32[]{:S(2)}) async-start(), calls=%async_computation | async-start | bytes 1179648 | tf_op jit(solution)/shard_map/all_gather | solution.py:26
  7.9 92.4 %all-gather.6.cloned.1.call-start = ((), (), s32[]{:S(2)}) async-start(), calls=%async_computation.1 | async-start | bytes 1179648 | tf_op jit(solution)/shard_map/all_gather | solution.py:25
  8.6 686.1 %all-gather.8.cloned.1.call-start = ((), (), s32[]{:S(2)}) async-start(), calls=%async_computation.2 | async-start | bytes 4718592 | tf_op jit(solution)/shard_map/all_gather | solution.py:46
  9.4 1388.4 %all-reduce.2.cloned.1.call-start = ((), (), s32[]{:S(2)}) async-start(), calls=%async_computation.3 | async-start | bytes 1048576 | tf_op jit(solution)/shard_map/psum | solution.py:47
  100.3 11.6 collective-permute-start
  131.3 16.1 %collective-permute-start = (f32[64,512]{1,0:T(8,128)S(1)}, f32[64,512]{1,0:T(8,128)S(1)}, u32[]{:S(2)}, u32[]{:S(2)}) collective-permute-start(f32[64,512]{1,0:T(8,128)S(1)} %get-tuple-element.219), channel_id=1, source_target_pairs={{0,8},{8,16},{16,24},{24,32},{32,40},{40,48},{48,56},{56,64},{64,7... | collective-permute-start | bytes 393224 | tf_op jit(solution)/shard_map/while/body/eval_jaxpr/ppermute | solution.py:10
  147.4 10.9 collective-permute-start
  158.3 9.9 collective-permute-start
  259.8 9.7 collective-permute-start
  310.3 12.7 collective-permute-start
  332.0 9.3 collective-permute-start
  350.7 9.3 collective-permute-start
  360.0 9.4 collective-permute-start
  378.6 9.3 collective-permute-start
  397.2 9.3 collective-permute-start
  406.5 9.3 collective-permute-start
  425.1 9.3 collective-permute-start
  443.7 9.3 collective-permute-start
  462.3 9.3 collective-permute-start
  480.9 9.3 collective-permute-start
  499.5 9.3 collective-permute-start
  518.1 9.3 collective-permute-start
  536.7 9.3 collective-permute-start
  555.3 9.3 collective-permute-start
  (46 other events, 1796.4 us)
Sparse Core Ops, SparseCore 0:
  10.1 44.6 all-gather.3
  56.8 43.3 all-gather.5
  102.4 69.6 all-gather.7
  702.0 695.7 all-reduce.1
where the time goes:
time: 1410 us
  waiting for transfers between devices  929 us (66%)
  starting transfers between devices  448 us (32%)
    psum x1, waiting for transfers between devices, body(): summed = lax.psum(partial_sum, 'blk')  696 us
    ppermute x64, starting transfers between devices, passed_along(): lax.ppermute(value, axis, [(source, source + steps) for source in range(l...  448 us
    ppermute x64, waiting for transfers between devices, passed_along(): lax.ppermute(value, axis, [(source, source + steps) for source in range(l...  141 us
    all_gather x1, waiting for transfers between devices, body(): lax.all_gather(diag_inverse, 'rhs', axis=1, tiled=True)  45.5 us
    all_gather x1, waiting for transfers between devices, body(): lax.all_gather(coupling, 'rhs', axis=1, tiled=True)  45.3 us
  transfers between devices with their start and end apart: 68, of which 67 were waited for; matrix products, arithmetic and copies ran while one was open for 0% of the time, Pallas kernels for 0%

commit v1 on v0

v1 whole, which is shorter than its diff:
```python
import jax
import jax.numpy as jnp
from jax import lax
from jax.sharding import PartitionSpec as P

PLANES, CHIPS, CORES = 8, 4, 2
IN_PLANE = CHIPS * CORES
BLOCK_SHIFT = 4


def device(plane, chip, core):
    return (plane * CHIPS + chip) * CORES + core


CORE_SWAP = [(p, p ^ 1) for p in range(PLANES * IN_PLANE)]
CHIP_GROUPS = [[device(z, c, k) for c in range(CHIPS)] for z in range(PLANES) for k in range(CORES)]
PLANE_GROUPS = [[device(z, c, k) for z in range(PLANES)] for c in range(CHIPS) for k in range(CORES)]


def product(left, right):
    return lax.dot_general(left, right, (((1,), (0,)), ((), ())), precision=lax.Precision.HIGH, preferred_element_type=jnp.float32)


def product_transposed(left, right):
    return lax.dot_general(left, right, (((1,), (1,)), ((), ())), precision=lax.Precision.HIGH, preferred_element_type=jnp.float32)


def to_all(value, axis, count, groups=None):
    copies = jnp.broadcast_to(value[None], (count,) + value.shape)
    return lax.all_to_all(copies, axis, 0, 0, axis_index_groups=groups)


def exchanged(pieces, axis, groups=None):
    return lax.all_to_all(pieces, axis, 0, 0, axis_index_groups=groups)


def swapped(value):
    return lax.ppermute(value, "blk", CORE_SWAP)


def after(map_and_offset, step, shift, size):
    made = product(map_and_offset, step[:size])
    return jnp.concatenate([made[:size], made[size:] * (2.0**shift) + step[size:]], axis=0)


def body(diag_inverse, coupling, rhs_t, prior, border_factor, border_rhs):
    rows, size = rhs_t.shape
    members = lax.axis_size("rhs")
    position = lax.axis_index("blk")
    core = position % CORES
    chip = (position // CORES) % CHIPS
    plane = position // IN_PLANE
    first_core = core == 0

    own = jnp.concatenate([coupling[0], diag_inverse[0]], axis=0)
    gathered = to_all(own, "rhs", members)
    share = coupling.shape[1]
    link = gathered[:, :share].reshape(size, size)
    inverse = gathered[:, share:].reshape(size, size)

    border_factor, gathered = lax.optimization_barrier((border_factor, gathered))
    border_block = lax.all_gather(border_factor, "rhs", axis=0, tiled=True)

    block_map = lax.dot_general(link, inverse, (((0,), (1,)), ((), ())), precision=lax.Precision.HIGH, preferred_element_type=jnp.float32)
    block = jnp.concatenate([block_map * (-(2.0**-BLOCK_SHIFT)), product_transposed(rhs_t, inverse)], axis=0)

    other = swapped(block)
    pair = after(jnp.where(first_core, block, other), jnp.where(first_core, other, block), BLOCK_SHIFT, size)

    half, half_rows = size // CORES, rows // CORES
    part = jnp.concatenate(
        [lax.dynamic_slice_in_dim(pair, core * half, half, 0), lax.dynamic_slice_in_dim(pair, size + core * half_rows, half_rows, 0)], axis=0
    )
    mine = to_all(part, "blk", CHIPS, CHIP_GROUPS)
    theirs = swapped(mine)
    upper, lower = jnp.where(first_core, mine, theirs), jnp.where(first_core, theirs, mine)
    chips = [jnp.concatenate([upper[c, :half], lower[c, :half], upper[c, half:], lower[c, half:]], axis=0) for c in range(CHIPS)]

    prefixes = [chips[0]]
    for c in range(1, CHIPS):
        prefixes.append(after(prefixes[-1], chips[c], 2 * BLOCK_SHIFT, size))
    whole = prefixes[-1]

    start = prior
    for step in range(1, PLANES):
        end = product(start, whole[:size]) * (2.0 ** (BLOCK_SHIFT * IN_PLANE)) + whole[size:]
        hop = [(device(step - 1, c, k), device(step, c, k)) for c in range(CHIPS) for k in range(CORES)]
        arrived = lax.ppermute(end, "blk", hop)
        start = jnp.where(plane == step, arrived, start)

    before = jnp.where(chip == 1, prefixes[0], jnp.where(chip == 2, prefixes[1], prefixes[2]))
    even = jnp.where(chip == 0, block, after(before, block, BLOCK_SHIFT, size))
    odd = jnp.where(chip == CHIPS - 1, whole, jnp.where(chip == 0, prefixes[0], jnp.where(chip == 1, prefixes[1], prefixes[2])))
    mapped = jnp.where(first_core, even, odd)
    scales = jnp.asarray([2.0 ** (BLOCK_SHIFT * (q + 1)) for q in range(IN_PLANE)], jnp.float32)
    solved = product(start, mapped[:size]) * scales[position % IN_PLANE] + mapped[size:]

    border = border_rhs.shape[1]
    partial = product_transposed(solved, border_block)
    per_core, per_chip = border // CORES, border // CORES // CHIPS
    per_plane = rows // PLANES
    kept = lax.dynamic_slice_in_dim(partial, core * per_core, per_core, 1)
    passed = lax.dynamic_slice_in_dim(partial, (1 - core) * per_core, per_core, 1)
    total = kept + swapped(passed)
    pieces = jnp.transpose(total.reshape(rows, CHIPS, per_chip), (1, 0, 2))
    total = jnp.sum(exchanged(pieces, "blk", CHIP_GROUPS), axis=0)
    total = jnp.sum(exchanged(total.reshape(PLANES, per_plane, per_chip), "blk", PLANE_GROUPS), axis=0)
    held = lax.dynamic_slice(border_rhs, (plane * per_plane, core * per_core + chip * per_chip), (per_plane, per_chip))
    result = to_all(held - total, "blk", PLANES, PLANE_GROUPS).reshape(rows, per_chip)
    result = to_all(result, "blk", CHIPS, CHIP_GROUPS)
    result = jnp.transpose(result, (1, 0, 2)).reshape(rows, per_core)
    across = swapped(result)
    left, right = jnp.where(first_core, result, across), jnp.where(first_core, across, result)
    return solved, jnp.concatenate([left, right], axis=1)


def solution(mesh):
    placed = (
        P("blk", "rhs", None),
        P("blk", "rhs", None),
        P("rhs", "blk"),
        P("rhs", None),
        P("rhs", "blk"),
        P("rhs", None),
    )
    return jax.shard_map(
        body,
        mesh=mesh,
        in_specs=placed,
        out_specs=(P("rhs", "blk"), P("rhs", None)),
        check_vma=False,
    )
```

time: 1410 us -> 252 us (0.18)
  waiting for transfers between devices: 929 us -> 32.6 us
  starting transfers between devices: 448 us -> 40.9 us
  blocking collectives: 0 us -> 125 us
    psum x1 -> x0, waiting for transfers between devices: 696 us -> none  [body(): summed = lax.psum(partial_sum, 'blk')]
    ppermute x64 -> x11, starting transfers between devices: 448 us -> 31.5 us  [the longest x4 20.7 us: swapped(): return lax.ppermute(value, 'blk', CORE_SWAP)]
    ppermute x64 -> x11, waiting for transfers between devices: 141 us -> 11.4 us  [the longest x4 9.24 us: swapped(): return lax.ppermute(value, 'blk', CORE_SWAP)]
    all_to_all x0 -> x5, blocking collectives: none -> 125 us  [the longest x4 111 us: to_all(): return lax.all_to_all(copies, axis, 0, 0, axis_index_groups=groups)]
    all_gather x3 -> x1, waiting for transfers between devices: 90.9 us -> 14 us  [body(): border_block = lax.all_gather(border_factor, 'rhs', axis=0, tiled=True)]
  transfers between devices with their start and end apart: 68 -> 13, of which waited for: 67 -> 7; matrix products, arithmetic and copies ran while one was open for 0% -> 8% of each run, Pallas kernels for 0% -> 0%
where the time goes in v1:
time: 252 us
  blocking collectives  125 us (50%)
  starting transfers between devices  40.9 us (16%)
  waiting for transfers between devices  32.6 us (13%)
  matrix products  22.2 us (9%)
  between operations  14.7 us (6%)
  other arithmetic  10.2 us (4%)
  local copies, waits for them, and re-layouts  5.63 us (2%)
    all_to_all x4, blocking collectives, to_all(): return lax.all_to_all(copies, axis, 0, 0, axis_index_groups=groups)  111 us
    ppermute x4, starting transfers between devices, swapped(): return lax.ppermute(value, 'blk', CORE_SWAP)  20.7 us
    dot_general x13, matrix products, product(): lax.dot_general(left, right, (((1,), (0,)), ((), ())), precision=lax.Prec...  15.4 us
    all_to_all x1, blocking collectives, exchanged(): return lax.all_to_all(pieces, axis, 0, 0, axis_index_groups=groups)  14.6 us
    all_gather x1, waiting for transfers between devices, body(): border_block = lax.all_gather(border_factor, 'rhs', axis=0, tiled=True)  14 us
    ppermute x7, starting transfers between devices, body(): arrived = lax.ppermute(end, 'blk', hop)  10.8 us
    all_to_all x1, starting transfers between devices, exchanged(): return lax.all_to_all(pieces, axis, 0, 0, axis_index_groups=groups)  9.37 us
    ppermute x4, waiting for transfers between devices, swapped(): return lax.ppermute(value, 'blk', CORE_SWAP)  9.24 us
  transfers between devices with their start and end apart: 13, of which 7 were waited for; matrix products, arithmetic and copies ran while one was open for 8% of the time, Pallas kernels for 0%

profile of v1, /device:TPU:1, one launch (start us, length us, event | category | flops | bytes accessed | tf_op | source)
XLA Modules:
  0.0 251.5 jit_solution(16239671382492209108)
XLA Ops:
  8.5 28.6 %all_to_all.30 = f32[8,128,512]{2,1,0:T(8,128)S(1)} all-to-all(f32[8,128,512]{2,1,0:T(8,128)S(1)} %broadcast_in_dim.10), channel_id=1, replica_groups=mesh['blk'=64,'rhs'=8] {'rhs'}, dimensions={0} | all-to-all | bytes 4194304 | tf_op jit(solution)/shard_map/all_to_all | solution.py:30
  37.3 1.9 convolution_multiply_fusion
  40.9 7.1 %collective-permute-start = (f32[576,512]{1,0:T(8,128)}, f32[576,512]{1,0:T(8,128)S(1)}, u32[]{:S(2)}, u32[]{:S(2)}) collective-permute-start(f32[576,512]{1,0:T(8,128)} %pad_maximum_fusion), channel_id=1, source_target_pairs={{0,8},{8,0},{16,24},{24,16},{32,40},{40,32},{48,56},{56,48},{64,72... | collective-permute-start | bytes 3538952 | tf_op jit(solution)/shard_map/ppermute | solution.py:38
  48.0 2.6 %collective-permute-done = f32[576,512]{1,0:T(8,128)S(1)} collective-permute-done((f32[576,512]{1,0:T(8,128)}, f32[576,512]{1,0:T(8,128)S(1)}, u32[]{:S(2)}, u32[]{:S(2)}) %collective-permute-start) | collective-permute-done | bytes 1179680 | tf_op jit(solution)/shard_map/ppermute | solution.py:38
  52.7 60.5 %all_to_all.31 = f32[4,288,512]{2,1,0:T(8,128)} all-to-all(f32[4,288,512]{2,1,0:T(8,128)S(1)} %broadcast_in_dim.11), channel_id=1, replica_groups={{0,16,32,48},{8,24,40,56},{64,80,96,112},{72,88,104,120},{128,144,160,1..., dimensions={0} | all-to-all | bytes 4718592 | tf_op jit(solution)/shard_map/all_to_all | solution.py:30
  113.2 3.8 %collective-permute-start.1 = (f32[4,288,512]{2,1,0:T(8,128)}, f32[4,288,512]{2,1,0:T(8,128)S(1)}, u32[]{:S(2)}, u32[]{:S(2)}) collective-permute-start(f32[4,288,512]{2,1,0:T(8,128)} %all_to_all.31), channel_id=1, source_target_pairs={{0,8},{8,0},{16,24},{24,16},{32,40},{40,32},{48,56},{56,48},{64,72... | collective-permute-start | bytes 7077896 | tf_op jit(solution)/shard_map/ppermute | solution.py:38
  117.0 4.3 %collective-permute-done.1 = f32[4,288,512]{2,1,0:T(8,128)S(1)} collective-permute-done((f32[4,288,512]{2,1,0:T(8,128)}, f32[4,288,512]{2,1,0:T(8,128)S(1)}, u32[]{:S(2)}, u32[]{:S(2)}) %collective-permute-start.1) | collective-permute-done | bytes 2359328 | tf_op jit(solution)/shard_map/ppermute | solution.py:38
  121.4 2.5 broadcast_select_fusion.1
  130.1 4.6 %collective-permute-start.2 = (f32[64,512]{1,0:T(8,128)}, f32[64,512]{1,0:T(8,128)}, u32[]{:S(2)}, u32[]{:S(2)}) collective-permute-start(f32[64,512]{1,0:T(8,128)} %fusion.7), channel_id=1, source_target_pairs={{0,64},{8,72},{16,80},{24,88},{32,96},{40,104},{48,112},{56,120},{... | collective-permute-start | bytes 393224 | tf_op jit(solution)/shard_map/ppermute | solution.py:88
  134.7 2.2 collective-permute-done.2
  140.9 2.0 fusion.9
  142.8 1.4 collective-permute-start.4
  146.9 1.3 collective-permute-start.5
  148.8 1.4 fusion.11
  151.0 2.4 fusion.1
  159.1 14.0 %all-gather.2.cloned.1.call-done = f32[2048,512]{1,0:T(8,128)} async-done(((f32[256,512]{1,0:T(8,128)}), f32[2048,512]{1,0:T(8,128)}) %all-gather.2.cloned.1.call-update) | async-done | bytes 4194320 | tf_op jit(solution)/shard_map/all_gather | solution.py:62
  173.1 4.2 %fusion.52 = f32[64,2048]{1,0:T(8,128)S(1)} fusion(f32[64,512]{1,0:T(8,128)S(1)} %fusion.14, f32[2048,512]{1,0:T(8,128)} %all-gather.2.cloned.1.call-done), kind=kOutput, calls=%fused_computation.112 | convolution fusion | flops 402653184 | bytes 4849664 | tf_op jit(solution)/shard_map/dot_general | solution.py:25
  177.4 2.6 %collective-permute-start.9 = (f32[64,1024]{1,0:T(8,128)S(1)}, f32[64,1024]{1,0:T(8,128)S(1)}, u32[]{:S(2)}, u32[]{:S(2)}) collective-permute-start(f32[64,1024]{1,0:T(8,128)S(1)} %constant_dynamic-slice_fusion), channel_id=1, source_target_pairs={{0,8},{8,0},{16,24},{24,16},{32,40},{40,32},{48,56},{56,48},{64,72... | collective-permute-start | bytes 786440 | tf_op jit(solution)/shard_map/ppermute | solution.py:38
  181.2 14.6 %all_to_all.32 = f32[4,64,256]{2,1,0:T(8,128)S(1)} all-to-all(f32[4,64,256]{2,1,0:T(8,128)S(1)} %bitcast.69), channel_id=1, replica_groups={{0,16,32,48},{8,24,40,56},{64,80,96,112},{72,88,104,120},{128,144,160,1..., dimensions={0} | all-to-all | bytes 524288 | tf_op jit(solution)/shard_map/all_to_all | solution.py:34
  196.5 9.4 %all-to-all-start.3 = ((f32[8,8,256]{2,1,0:T(8,128)}), f32[8,8,256]{2,1,0:T(8,128)S(1)}, u32[]{:S(2)}, u32[]{:S(2)}) async-start(f32[8,8,256]{2,1,0:T(8,128)} %bitcast.24), calls=%async_computation.3 | async-start | bytes 131072 | tf_op jit(solution)/shard_map/all_to_all | solution.py:34
  205.8 7.2 %all-to-all-done.3 = f32[8,8,256]{2,1,0:T(8,128)S(1)} async-done(((f32[8,8,256]{2,1,0:T(8,128)}), f32[8,8,256]{2,1,0:T(8,128)S(1)}, u32[]{:S(2)}, u32[]{:S(2)}) %all-to-all-start.3) | async-done | bytes 65568 | tf_op jit(solution)/shard_map/all_to_all | solution.py:34
  213.8 9.6 %all_to_all.33 = f32[8,8,256]{2,1,0:T(8,128)S(1)} all-to-all(f32[8,8,256]{2,1,0:T(8,128)S(1)} %broadcast_in_dim.12), channel_id=1, replica_groups={{0,64,128,192,256,320,384,448},{8,72,136,200,264,328,392,456},{16,80,14..., dimensions={0} | all-to-all | bytes 131072 | tf_op jit(solution)/shard_map/all_to_all | solution.py:30
  223.4 12.0 %all_to_all.34 = f32[4,64,256]{2,1,0:T(8,128)S(1)} all-to-all(f32[4,64,256]{2,1,0:T(8,128)S(1)} %broadcast_in_dim.14), channel_id=1, replica_groups={{0,16,32,48},{8,24,40,56},{64,80,96,112},{72,88,104,120},{128,144,160,1..., dimensions={0} | all-to-all | bytes 524288 | tf_op jit(solution)/shard_map/all_to_all | solution.py:30
  235.4 7.2 %collective-permute-start.10 = (f32[64,1024]{1,0:T(8,128)S(1)}, f32[64,1024]{1,0:T(8,128)S(1)}, u32[]{:S(2)}, u32[]{:S(2)}) collective-permute-start(f32[64,1024]{1,0:T(8,128)S(1)} %bitcast.71), channel_id=1, source_target_pairs={{0,8},{8,0},{16,24},{24,16},{32,40},{40,32},{48,56},{56,48},{64,72... | collective-permute-start | bytes 786440 | tf_op jit(solution)/shard_map/ppermute | solution.py:38
  (111 shorter events, 29.3 us)
Async XLA Ops:
  7.2 32.0 %copy-start = (f32[64,512]{1,0:T(8,128)S(1)}, f32[64,512]{1,0:T(8,128)}, u32[]{:S(2)}) copy-start(f32[64,512]{1,0:T(8,128)} %param.9) | copy-start | bytes 393220
  7.2 166.0 %all-gather.2.cloned.1.call-start = ((), (), s32[]{:S(2)}) async-start(), calls=%async_computation.6 | async-start | bytes 4718592 | tf_op jit(solution)/shard_map/all_gather | solution.py:62
  39.8 11.1 %copy-start.3 = (f32[64,512]{1,0:T(8,128)}, f32[64,512]{1,0:T(8,128)S(1)}, u32[]{:S(2)}) copy-start(f32[64,512]{1,0:T(8,128)S(1)} %convolution_bitcast_fusion) | copy-start | bytes 393220
  40.9 9.7 %collective-permute-start = (f32[576,512]{1,0:T(8,128)}, f32[576,512]{1,0:T(8,128)S(1)}, u32[]{:S(2)}, u32[]{:S(2)}) collective-permute-start(f32[576,512]{1,0:T(8,128)} %pad_maximum_fusion), channel_id=1, source_target_pairs={{0,8},{8,0},{16,24},{24,16},{32,40},{40,32},{48,56},{56,48},{64,72... | collective-permute-start | bytes 3538952 | tf_op jit(solution)/shard_map/ppermute | solution.py:38
  113.2 8.2 %collective-permute-start.1 = (f32[4,288,512]{2,1,0:T(8,128)}, f32[4,288,512]{2,1,0:T(8,128)S(1)}, u32[]{:S(2)}, u32[]{:S(2)}) collective-permute-start(f32[4,288,512]{2,1,0:T(8,128)} %all_to_all.31), channel_id=1, source_target_pairs={{0,8},{8,0},{16,24},{24,16},{32,40},{40,32},{48,56},{56,48},{64,72... | collective-permute-start | bytes 7077896 | tf_op jit(solution)/shard_map/ppermute | solution.py:38
  130.1 6.8 %collective-permute-start.2 = (f32[64,512]{1,0:T(8,128)}, f32[64,512]{1,0:T(8,128)}, u32[]{:S(2)}, u32[]{:S(2)}) collective-permute-start(f32[64,512]{1,0:T(8,128)} %fusion.7), channel_id=1, source_target_pairs={{0,64},{8,72},{16,80},{24,88},{32,96},{40,104},{48,112},{56,120},{... | collective-permute-start | bytes 393224 | tf_op jit(solution)/shard_map/ppermute | solution.py:88
  139.6 1.3 collective-permute-start.3
  142.8 5.4 %copy-start.23 = (f32[8]{0:T(128)S(1)}, f32[8]{0:T(128)}, u32[]{:S(2)}) copy-start(f32[8]{0:T(128)} %constant.94.clone) | copy-start | bytes 100
  142.8 1.4 collective-permute-start.4
  146.9 1.9 collective-permute-start.5
  148.8 2.1 copy-start.2
  148.8 2.1 copy-start.6
  150.3 3.2 %collective-permute-start.6 = (f32[64,512]{1,0:T(8,128)S(1)}, f32[64,512]{1,0:T(8,128)S(1)}, u32[]{:S(2)}, u32[]{:S(2)}) collective-permute-start(f32[64,512]{1,0:T(8,128)S(1)} %fusion.11), channel_id=1, source_target_pairs={{256,320},{264,328},{272,336},{280,344},{288,352},{296,360},{304,3... | collective-permute-start | bytes 393224 | tf_op jit(solution)/shard_map/ppermute | solution.py:88
  153.4 2.5 copy-start.9
  153.5 2.4 copy-start.4
  155.0 2.0 copy-start.11
  155.1 2.0 copy-start.13
  155.1 2.0 copy-start.18
  155.1 0.9 collective-permute-start.7
  156.4 1.7 collective-permute-start.8
  159.1 18.2 %copy-start.21 = (f32[64,512]{1,0:T(8,128)}, f32[64,512]{1,0:T(8,128)S(1)}, u32[]{:S(2)}) copy-start(f32[64,512]{1,0:T(8,128)S(1)} %fusion.14) | copy-start | bytes 393220
  177.4 3.7 %collective-permute-start.9 = (f32[64,1024]{1,0:T(8,128)S(1)}, f32[64,1024]{1,0:T(8,128)S(1)}, u32[]{:S(2)}, u32[]{:S(2)}) collective-permute-start(f32[64,1024]{1,0:T(8,128)S(1)} %constant_dynamic-slice_fusion), channel_id=1, source_target_pairs={{0,8},{8,0},{16,24},{24,16},{32,40},{40,32},{48,56},{56,48},{64,72... | collective-permute-start | bytes 786440 | tf_op jit(solution)/shard_map/ppermute | solution.py:38
  196.5 16.6 %all-to-all-start.3 = ((f32[8,8,256]{2,1,0:T(8,128)}), f32[8,8,256]{2,1,0:T(8,128)S(1)}, u32[]{:S(2)}, u32[]{:S(2)}) async-start(f32[8,8,256]{2,1,0:T(8,128)} %bitcast.24), calls=%async_computation.3 | async-start | bytes 131072 | tf_op jit(solution)/shard_map/all_to_all | solution.py:34
  235.4 8.4 %collective-permute-start.10 = (f32[64,1024]{1,0:T(8,128)S(1)}, f32[64,1024]{1,0:T(8,128)S(1)}, u32[]{:S(2)}, u32[]{:S(2)}) collective-permute-start(f32[64,1024]{1,0:T(8,128)S(1)} %bitcast.71), channel_id=1, source_target_pairs={{0,8},{8,0},{16,24},{24,16},{32,40},{40,32},{48,56},{56,48},{64,72... | collective-permute-start | bytes 786440 | tf_op jit(solution)/shard_map/ppermute | solution.py:38
  (14 other events, 15.8 us)
Sparse Core Ops, SparseCore 0:
  117.2 55.9 all-gather.1

commit v2 on v1

--- a/solution.py
+++ b/solution.py
@@ -34,6 +34,10 @@
     return lax.all_to_all(pieces, axis, 0, 0, axis_index_groups=groups)
 
 
+def chip_turn(count):
+    return [(device(z, c, k), device(z, (c + count) % CHIPS, k)) for z in range(PLANES) for c in range(CHIPS) for k in range(CORES)]
+
+
 def swapped(value):
     return lax.ppermute(value, "blk", CORE_SWAP)
 
@@ -58,9 +62,6 @@
     link = gathered[:, :share].reshape(size, size)
     inverse = gathered[:, share:].reshape(size, size)
 
-    border_factor, gathered = lax.optimization_barrier((border_factor, gathered))
-    border_block = lax.all_gather(border_factor, "rhs", axis=0, tiled=True)
-
     block_map = lax.dot_general(link, inverse, (((0,), (1,)), ((), ())), precision=lax.Precision.HIGH, preferred_element_type=jnp.float32)
     block = jnp.concatenate([block_map * (-(2.0**-BLOCK_SHIFT)), product_transposed(rhs_t, inverse)], axis=0)
 
@@ -71,47 +72,80 @@
     part = jnp.concatenate(
         [lax.dynamic_slice_in_dim(pair, core * half, half, 0), lax.dynamic_slice_in_dim(pair, size + core * half_rows, half_rows, 0)], axis=0
     )
-    mine = to_all(part, "blk", CHIPS, CHIP_GROUPS)
+    mine = jnp.stack([lax.ppermute(part, "blk", chip_turn(k)) for k in range(1, CHIPS)])
     theirs = swapped(mine)
     upper, lower = jnp.where(first_core, mine, theirs), jnp.where(first_core, theirs, mine)
-    chips = [jnp.concatenate([upper[c, :half], lower[c, :half], upper[c, half:], lower[c, half:]], axis=0) for c in range(CHIPS)]
+    fetched = jnp.concatenate([upper[:, :half], lower[:, :half], upper[:, half:], lower[:, half:]], axis=1)
+    chips = jnp.concatenate([pair[None], fetched], axis=0)
 
-    prefixes = [chips[0]]
+    def chip_map(c):
+        return lax.dynamic_index_in_dim(chips, (chip - c) % CHIPS, 0, keepdims=False)
+
+    prefixes = [chip_map(0)]
     for c in range(1, CHIPS):
-        prefixes.append(after(prefixes[-1], chips[c], 2 * BLOCK_SHIFT, size))
+        prefixes.append(after(prefixes[-1], chip_map(c), 2 * BLOCK_SHIFT, size))
     whole = prefixes[-1]
-
-    start = prior
-    for step in range(1, PLANES):
-        end = product(start, whole[:size]) * (2.0 ** (BLOCK_SHIFT * IN_PLANE)) + whole[size:]
-        hop = [(device(step - 1, c, k), device(step, c, k)) for c in range(CHIPS) for k in range(CORES)]
-        arrived = lax.ppermute(end, "blk", hop)
-        start = jnp.where(plane == step, arrived, start)
 
     before = jnp.where(chip == 1, prefixes[0], jnp.where(chip == 2, prefixes[1], prefixes[2]))
     even = jnp.where(chip == 0, block, after(before, block, BLOCK_SHIFT, size))
     odd = jnp.where(chip == CHIPS - 1, whole, jnp.where(chip == 0, prefixes[0], jnp.where(chip == 1, prefixes[1], prefixes[2])))
     mapped = jnp.where(first_core, even, odd)
-    scales = jnp.asarray([2.0 ** (BLOCK_SHIFT * (q + 1)) for q in range(IN_PLANE)], jnp.float32)
-    solved = product(start, mapped[:size]) * scales[position % IN_PLANE] + mapped[size:]
+    scales = jnp.asarray([2.0 ** (BLOCK_SHIFT * (q + 1 - IN_PLANE)) for q in range(IN_PLANE)], jnp.float32)
+    own_map = mapped[:size] * scales[position % IN_PLANE]
+    own_offset = mapped[size:]
 
     border = border_rhs.shape[1]
-    partial = product_transposed(solved, border_block)
-    per_core, per_chip = border // CORES, border // CORES // CHIPS
-    per_plane = rows // PLANES
-    kept = lax.dynamic_slice_in_dim(partial, core * per_core, per_core, 1)
-    passed = lax.dynamic_slice_in_dim(partial, (1 - core) * per_core, per_core, 1)
-    total = kept + swapped(passed)
-    pieces = jnp.transpose(total.reshape(rows, CHIPS, per_chip), (1, 0, 2))
-    total = jnp.sum(exchanged(pieces, "blk", CHIP_GROUPS), axis=0)
-    total = jnp.sum(exchanged(total.reshape(PLANES, per_plane, per_chip), "blk", PLANE_GROUPS), axis=0)
-    held = lax.dynamic_slice(border_rhs, (plane * per_plane, core * per_core + chip * per_chip), (per_plane, per_chip))
-    result = to_all(held - total, "blk", PLANES, PLANE_GROUPS).reshape(rows, per_chip)
+    share = border_factor.shape[0]
+    piece = share // IN_PLANE
+
+    def gather_offsets(offset):
+        return to_all(offset, "rhs", members).reshape(rows * members, size)
+
+    def border_product(offsets):
+        made = product_transposed(border_factor, jnp.concatenate([own_map, offsets], axis=0))
+        half_share = share // CORES
+        kept = lax.dynamic_slice_in_dim(made, core * half_share, half_share, 0)
+        passed = lax.dynamic_slice_in_dim(made, (1 - core) * half_share, half_share, 0)
+        return kept + swapped(passed)
+
+    def sum_chips(made):
+        pieces = made.reshape(CHIPS, piece, made.shape[1])
+        return jnp.sum(exchanged(pieces, "blk", CHIP_GROUPS), axis=0)
+
+    def gather_border(made):
+        return to_all(made, "rhs", members).reshape(members * piece, made.shape[1])
+
+    beside = {3: gather_offsets, 4: border_product, 6: sum_chips, 7: gather_border}
+
+    start = prior
+    side = own_offset
+    for step in range(1, PLANES):
+        end = product(start, whole[:size]) * (2.0 ** (BLOCK_SHIFT * IN_PLANE)) + whole[size:]
+        if step in beside:
+            end, side = lax.optimization_barrier((end, side))
+            side = beside[step](side)
+        hop = [(device(step - 1, c, k), device(step, c, k)) for c in range(CHIPS) for k in range(CORES)]
+        arrived = lax.ppermute(end, "blk", hop)
+        if step in beside:
+            arrived, side = lax.optimization_barrier((arrived, side))
+        start = jnp.where(plane == step, arrived, start)
+
+    large = 2.0 ** (BLOCK_SHIFT * IN_PLANE)
+    solved = product(start, own_map) * large + own_offset
+
+    member = lax.axis_index("rhs")
+    chosen = (jnp.arange(rows)[:, None] + member * rows == jnp.arange(rows * members)[None, :]).astype(jnp.float32)
+    fixed = product_transposed(chosen, side[:, size:])
+    held = border_rhs.reshape(rows, members, CORES, CHIPS, piece)
+    held = lax.dynamic_slice(held, (0, 0, core, chip, 0), (rows, members, 1, 1, piece)).reshape(rows, members * piece)
+    fixed = fixed - jnp.where(plane == 0, held, 0.0)
+    result = product_transposed(start, side[:, :size]) * large + fixed
+    result = -jnp.sum(to_all(result, "blk", PLANES, PLANE_GROUPS), axis=0)
     result = to_all(result, "blk", CHIPS, CHIP_GROUPS)
-    result = jnp.transpose(result, (1, 0, 2)).reshape(rows, per_core)
     across = swapped(result)
     left, right = jnp.where(first_core, result, across), jnp.where(first_core, across, result)
-    return solved, jnp.concatenate([left, right], axis=1)
+    result = jnp.stack([left, right]).reshape(CORES, CHIPS, rows, members, piece)
+    return solved, jnp.transpose(result, (2, 3, 0, 1, 4)).reshape(rows, border)
 
 
 def solution(mesh):

time: 252 us -> 267 us (1.060)
  blocking collectives: 125 us -> 70.8 us
  waiting for transfers between devices: 32.6 us -> 76.6 us
  starting transfers between devices: 40.9 us -> 70.9 us
  between operations: 14.7 us -> 1.48 us
  local copies, waits for them, and re-layouts: 5.63 us -> 13.6 us
  other arithmetic: 10.2 us -> 12.9 us
    all_to_all x4 -> x3, blocking collectives: 111 us -> 70.8 us  [to_all(): return lax.all_to_all(copies, axis, 0, 0, axis_index_groups=groups)]
    ppermute x0 -> x3, waiting for transfers between devices: none -> 34.9 us  [body(): lax.ppermute(part, 'blk', chip_turn(k))]
    all_to_all x0 -> x2, starting transfers between devices: none -> 23 us  [to_all(): return lax.all_to_all(copies, axis, 0, 0, axis_index_groups=groups)]
    all_to_all x0 -> x2, waiting for transfers between devices: none -> 21.5 us  [to_all(): return lax.all_to_all(copies, axis, 0, 0, axis_index_groups=groups)]
    all_to_all x1 -> x0, blocking collectives: 14.6 us -> none  [exchanged(): return lax.all_to_all(pieces, axis, 0, 0, axis_index_groups=groups)]
    all_gather x1 -> x0, waiting for transfers between devices: 14 us -> none  [body(): border_block = lax.all_gather(border_factor, 'rhs', axis=0, tiled=True)]
    ppermute x0 -> x3, starting transfers between devices: none -> 12.8 us  [body(): lax.ppermute(part, 'blk', chip_turn(k))]
    unnamed x48 -> x42, local copies, waits for them, and re-layouts: 3.05 us -> 7.49 us
  transfers between devices with their start and end apart: 13 -> 17, of which waited for: 7 -> 9; matrix products, arithmetic and copies ran while one was open for 8% -> 4% of each run, Pallas kernels for 0% -> 0%
where the time goes in v2:
time: 267 us; the launch traced here: 266 us
  waiting for transfers between devices  76.6 us (29%)
  starting transfers between devices  70.9 us (27%)
  blocking collectives  70.8 us (27%)
  matrix products  19.7 us (7%)
  local copies, waits for them, and re-layouts  13.6 us (5%)
  other arithmetic  12.9 us (5%)
    all_to_all x3, blocking collectives, to_all(): return lax.all_to_all(copies, axis, 0, 0, axis_index_groups=groups)  70.8 us
    ppermute x3, waiting for transfers between devices, body(): lax.ppermute(part, 'blk', chip_turn(k))  34.9 us
    all_to_all x2, starting transfers between devices, to_all(): return lax.all_to_all(copies, axis, 0, 0, axis_index_groups=groups)  23 us
    all_to_all x2, waiting for transfers between devices, to_all(): return lax.all_to_all(copies, axis, 0, 0, axis_index_groups=groups)  21.5 us
    ppermute x4, starting transfers between devices, swapped(): return lax.ppermute(value, 'blk', CORE_SWAP)  20.3 us
    dot_general x13, matrix products, product(): lax.dot_general(left, right, (((1,), (0,)), ((), ())), precision=lax.Prec...  14.2 us
    ppermute x3, starting transfers between devices, body(): lax.ppermute(part, 'blk', chip_turn(k))  12.8 us
    all_to_all x1, waiting for transfers between devices, exchanged(): return lax.all_to_all(pieces, axis, 0, 0, axis_index_groups=groups)  10.8 us
  transfers between devices with their start and end apart: 17, of which 9 were waited for; matrix products, arithmetic and copies ran while one was open for 4% of the time, Pallas kernels for 0%

profile of v2, /device:TPU:1, one launch (start us, length us, event | category | flops | bytes accessed | tf_op | source)
XLA Modules:
  0.0 266.0 jit_solution(998563016883333206)
XLA Ops:
  2.0 28.6 %all_to_all.30 = f32[8,128,512]{2,1,0:T(8,128)S(1)} all-to-all(f32[8,128,512]{2,1,0:T(8,128)S(1)} %broadcast_in_dim.15), channel_id=1, replica_groups=mesh['blk'=64,'rhs'=8] {'rhs'}, dimensions={0} | all-to-all | bytes 4194304 | tf_op jit(solution)/shard_map/all_to_all | solution.py:30
  35.1 7.1 %collective-permute-start = (f32[576,512]{1,0:T(8,128)}, f32[576,512]{1,0:T(8,128)S(1)}, u32[]{:S(2)}, u32[]{:S(2)}) collective-permute-start(f32[576,512]{1,0:T(8,128)} %pad_maximum_fusion.2), channel_id=1, source_target_pairs={{0,8},{8,0},{16,24},{24,16},{32,40},{40,32},{48,56},{56,48},{64,72... | collective-permute-start | bytes 3538952 | tf_op jit(solution)/shard_map/ppermute | solution.py:42
  42.1 2.6 collective-permute-done
  46.5 5.1 %collective-permute-start.3 = (f32[288,512]{1,0:T(8,128)S(1)}, f32[288,512]{1,0:T(8,128)S(1)}, u32[]{:S(2)}, u32[]{:S(2)}) collective-permute-start(f32[288,512]{1,0:T(8,128)S(1)} %pad_maximum_fusion.9), channel_id=1, source_target_pairs={{0,48},{8,56},{16,0},{24,8},{32,16},{40,24},{48,32},{56,40},{64,11... | collective-permute-start | bytes 1769480 | tf_op jit(solution)/shard_map/ppermute | solution.py:75
  51.6 4.4 %collective-permute-start.2 = (f32[288,512]{1,0:T(8,128)S(1)}, f32[288,512]{1,0:T(8,128)S(1)}, u32[]{:S(2)}, u32[]{:S(2)}) collective-permute-start(f32[288,512]{1,0:T(8,128)S(1)} %pad_maximum_fusion.9), channel_id=1, source_target_pairs={{0,32},{8,40},{16,48},{24,56},{32,0},{40,8},{48,16},{56,24},{64,96... | collective-permute-start | bytes 1769480 | tf_op jit(solution)/shard_map/ppermute | solution.py:75
  56.0 3.3 %collective-permute-start.1 = (f32[288,512]{1,0:T(8,128)S(1)}, f32[288,512]{1,0:T(8,128)S(1)}, u32[]{:S(2)}, u32[]{:S(2)}) collective-permute-start(f32[288,512]{1,0:T(8,128)S(1)} %pad_maximum_fusion.9), channel_id=1, source_target_pairs={{0,16},{8,24},{16,32},{24,40},{32,48},{40,56},{48,0},{56,8},{64,80... | collective-permute-start | bytes 1769480 | tf_op jit(solution)/shard_map/ppermute | solution.py:75
  59.3 32.3 %collective-permute-done.3 = f32[288,512]{1,0:T(8,128)S(1)} collective-permute-done((f32[288,512]{1,0:T(8,128)S(1)}, f32[288,512]{1,0:T(8,128)S(1)}, u32[]{:S(2)}, u32[]{:S(2)}) %collective-permute-start.3) | collective-permute-done | bytes 589856 | tf_op jit(solution)/shard_map/ppermute | solution.py:75
  91.7 2.5 collective-permute-done.1
  95.6 3.4 %collective-permute-start.4 = (f32[3,288,512]{2,1,0:T(8,128)}, f32[3,288,512]{2,1,0:T(8,128)}, u32[]{:S(2)}, u32[]{:S(2)}) collective-permute-start(f32[3,288,512]{2,1,0:T(8,128)} %pad_maximum_fusion.1), channel_id=1, source_target_pairs={{0,8},{8,0},{16,24},{24,16},{32,40},{40,32},{48,56},{56,48},{64,72... | collective-permute-start | bytes 5308424 | tf_op jit(solution)/shard_map/ppermute | solution.py:42
  99.3 3.4 %collective-permute-done.4 = f32[3,288,512]{2,1,0:T(8,128)} collective-permute-done((f32[3,288,512]{2,1,0:T(8,128)}, f32[3,288,512]{2,1,0:T(8,128)}, u32[]{:S(2)}, u32[]{:S(2)}) %collective-permute-start.4) | collective-permute-done | bytes 1769504 | tf_op jit(solution)/shard_map/ppermute | solution.py:42
  102.7 2.0 broadcast_select_fusion.1
  112.1 4.0 %collective-permute-start.5 = (f32[64,512]{1,0:T(8,128)S(1)}, f32[64,512]{1,0:T(8,128)S(1)}, u32[]{:S(2)}, u32[]{:S(2)}) collective-permute-start(f32[64,512]{1,0:T(8,128)S(1)} %fusion.13), channel_id=1, source_target_pairs={{0,64},{8,72},{16,80},{24,88},{32,96},{40,104},{48,112},{56,120},{... | collective-permute-start | bytes 393224 | tf_op jit(solution)/shard_map/ppermute | solution.py:128
  116.2 2.4 collective-permute-done.5
  123.4 15.5 %all-to-all-start.1 = ((f32[8,64,512]{2,1,0:T(8,128)}), f32[8,64,512]{2,1,0:T(8,128)}, u32[]{:S(2)}, u32[]{:S(2)}) async-start(f32[8,64,512]{2,1,0:T(8,128)} %broadcast_in_dim.18), calls=%async_computation.1 | async-start | bytes 2097152 | tf_op jit(solution)/shard_map/all_to_all | solution.py:30
  142.2 10.9 %all-to-all-done.1 = f32[8,64,512]{2,1,0:T(8,128)} async-done(((f32[8,64,512]{2,1,0:T(8,128)}), f32[8,64,512]{2,1,0:T(8,128)}, u32[]{:S(2)}, u32[]{:S(2)}) %all-to-all-start.1) | async-done | bytes 1048608 | tf_op jit(solution)/shard_map/all_to_all | solution.py:30
  154.1 2.3 fusion
  158.3 3.6 %collective-permute-start.9 = (f32[128,1024]{0,1:T(8,128)}, f32[128,1024]{0,1:T(8,128)}, u32[]{:S(2)}, u32[]{:S(2)}) collective-permute-start(f32[128,1024]{0,1:T(8,128)} %dynamic-slice_bitcast_fusion.6), channel_id=1, source_target_pairs={{0,8},{8,0},{16,24},{24,16},{32,40},{40,32},{48,56},{56,48},{64,72... | collective-permute-start | bytes 1572872 | tf_op jit(solution)/shard_map/ppermute | solution.py:42
  171.1 5.8 %all-to-all-start.2 = ((f32[4,32,1024]{2,1,0:T(8,128)}), f32[4,32,1024]{2,1,0:T(8,128)S(1)}, u32[]{:S(2)}, u32[]{:S(2)}) async-start(f32[4,32,1024]{2,1,0:T(8,128)} %bitcast.82), calls=%async_computation.2 | async-start | bytes 1048576 | tf_op jit(solution)/shard_map/all_to_all | solution.py:34
  178.2 10.8 %all-to-all-done.2 = f32[4,32,1024]{2,1,0:T(8,128)S(1)} async-done(((f32[4,32,1024]{2,1,0:T(8,128)}), f32[4,32,1024]{2,1,0:T(8,128)S(1)}, u32[]{:S(2)}, u32[]{:S(2)}) %all-to-all-start.2) | async-done | bytes 524320 | tf_op jit(solution)/shard_map/all_to_all | solution.py:34
  192.0 7.5 %all-to-all-start.3 = ((f32[8,32,1024]{2,1,0:T(8,128)}), f32[8,32,1024]{2,1,0:T(8,128)S(1)}, u32[]{:S(2)}, u32[]{:S(2)}) async-start(f32[8,32,1024]{2,1,0:T(8,128)} %broadcast_in_dim.19), calls=%async_computation.3 | async-start | bytes 2097152 | tf_op jit(solution)/shard_map/all_to_all | solution.py:30
  202.5 10.6 %all-to-all-done.3 = f32[8,32,1024]{2,1,0:T(8,128)S(1)} async-done(((f32[8,32,1024]{2,1,0:T(8,128)}), f32[8,32,1024]{2,1,0:T(8,128)S(1)}, u32[]{:S(2)}, u32[]{:S(2)}) %all-to-all-start.3) | async-done | bytes 1048608 | tf_op jit(solution)/shard_map/all_to_all | solution.py:30
  213.8 27.6 %all_to_all.31 = f32[8,64,256]{2,1,0:T(8,128)S(1)} all-to-all(f32[8,64,256]{2,1,0:T(8,128)S(1)} %broadcast_in_dim.21), channel_id=1, replica_groups={{0,64,128,192,256,320,384,448},{8,72,136,200,264,328,392,456},{16,80,14..., dimensions={0} | all-to-all | bytes 1048576 | tf_op jit(solution)/shard_map/all_to_all | solution.py:30
  241.5 14.7 %all_to_all.32 = f32[4,64,256]{2,1,0:T(8,128)S(1)} all-to-all(f32[4,64,256]{2,1,0:T(8,128)S(1)} %broadcast_in_dim.22), channel_id=1, replica_groups={{0,16,32,48},{8,24,40,56},{64,80,96,112},{72,88,104,120},{128,144,160,1..., dimensions={0} | all-to-all | bytes 524288 | tf_op jit(solution)/shard_map/all_to_all | solution.py:30
  256.4 6.2 %collective-permute-start.13 = (f32[4,64,256]{1,2,0:T(8,128)S(1)}, f32[4,64,256]{1,2,0:T(8,128)S(1)}, u32[]{:S(2)}, u32[]{:S(2)}) collective-permute-start(f32[4,64,256]{1,2,0:T(8,128)S(1)} %copy.27), channel_id=1, source_target_pairs={{0,8},{8,0},{16,24},{24,16},{32,40},{40,32},{48,56},{56,48},{64,72... | collective-permute-start | bytes 786440 | tf_op jit(solution)/shard_map/ppermute | solution.py:42
  (124 shorter events, 47.8 us)
Async XLA Ops:
  0.6 153.5 %copy-start = (f32[256,512]{1,0:T(8,128)S(1)}, f32[256,512]{1,0:T(8,128)}, u32[]{:S(2)}) copy-start(f32[256,512]{1,0:T(8,128)} %param.11) | copy-start | bytes 1572868
  35.1 9.7 %collective-permute-start = (f32[576,512]{1,0:T(8,128)}, f32[576,512]{1,0:T(8,128)S(1)}, u32[]{:S(2)}, u32[]{:S(2)}) collective-permute-start(f32[576,512]{1,0:T(8,128)} %pad_maximum_fusion.2), channel_id=1, source_target_pairs={{0,8},{8,0},{16,24},{24,16},{32,40},{40,32},{48,56},{56,48},{64,72... | collective-permute-start | bytes 3538952 | tf_op jit(solution)/shard_map/ppermute | solution.py:42
  46.5 45.2 %collective-permute-start.3 = (f32[288,512]{1,0:T(8,128)S(1)}, f32[288,512]{1,0:T(8,128)S(1)}, u32[]{:S(2)}, u32[]{:S(2)}) collective-permute-start(f32[288,512]{1,0:T(8,128)S(1)} %pad_maximum_fusion.9), channel_id=1, source_target_pairs={{0,48},{8,56},{16,0},{24,8},{32,16},{40,24},{48,32},{56,40},{64,11... | collective-permute-start | bytes 1769480 | tf_op jit(solution)/shard_map/ppermute | solution.py:75
  51.6 40.1 %collective-permute-start.2 = (f32[288,512]{1,0:T(8,128)S(1)}, f32[288,512]{1,0:T(8,128)S(1)}, u32[]{:S(2)}, u32[]{:S(2)}) collective-permute-start(f32[288,512]{1,0:T(8,128)S(1)} %pad_maximum_fusion.9), channel_id=1, source_target_pairs={{0,32},{8,40},{16,48},{24,56},{32,0},{40,8},{48,16},{56,24},{64,96... | collective-permute-start | bytes 1769480 | tf_op jit(solution)/shard_map/ppermute | solution.py:75
  56.0 38.2 %collective-permute-start.1 = (f32[288,512]{1,0:T(8,128)S(1)}, f32[288,512]{1,0:T(8,128)S(1)}, u32[]{:S(2)}, u32[]{:S(2)}) collective-permute-start(f32[288,512]{1,0:T(8,128)S(1)} %pad_maximum_fusion.9), channel_id=1, source_target_pairs={{0,16},{8,24},{16,32},{24,40},{32,48},{40,56},{48,0},{56,8},{64,80... | collective-permute-start | bytes 1769480 | tf_op jit(solution)/shard_map/ppermute | solution.py:75
  91.7 3.9 %copy-start.4 = (f32[288,512]{1,0:T(8,128)}, f32[288,512]{1,0:T(8,128)S(1)}, u32[]{:S(2)}) copy-start(f32[288,512]{1,0:T(8,128)S(1)} %collective-permute-done.3) | copy-start | bytes 1769476
  95.6 7.1 %collective-permute-start.4 = (f32[3,288,512]{2,1,0:T(8,128)}, f32[3,288,512]{2,1,0:T(8,128)}, u32[]{:S(2)}, u32[]{:S(2)}) collective-permute-start(f32[3,288,512]{2,1,0:T(8,128)} %pad_maximum_fusion.1), channel_id=1, source_target_pairs={{0,8},{8,0},{16,24},{24,16},{32,40},{40,32},{48,56},{56,48},{64,72... | collective-permute-start | bytes 5308424 | tf_op jit(solution)/shard_map/ppermute | solution.py:42
  110.6 5.5 %copy-start.2 = (f32[576,512]{1,0:T(8,128)}, f32[576,512]{1,0:T(8,128)S(1)}, u32[]{:S(2)}) copy-start(f32[576,512]{1,0:T(8,128)S(1)} %fusion.8) | copy-start | bytes 3538948
  112.1 6.5 %collective-permute-start.5 = (f32[64,512]{1,0:T(8,128)S(1)}, f32[64,512]{1,0:T(8,128)S(1)}, u32[]{:S(2)}, u32[]{:S(2)}) collective-permute-start(f32[64,512]{1,0:T(8,128)S(1)} %fusion.13), channel_id=1, source_target_pairs={{0,64},{8,72},{16,80},{24,88},{32,96},{40,104},{48,112},{56,120},{... | collective-permute-start | bytes 393224 | tf_op jit(solution)/shard_map/ppermute | solution.py:128
  119.0 2.8 %collective-permute-start.6 = (f32[64,512]{1,0:T(8,128)S(1)}, f32[64,512]{1,0:T(8,128)S(1)}, u32[]{:S(2)}, u32[]{:S(2)}) collective-permute-start(f32[64,512]{1,0:T(8,128)S(1)} %fusion.14), channel_id=1, source_target_pairs={{64,128},{72,136},{80,144},{88,152},{96,160},{104,168},{112,176},{... | collective-permute-start | bytes 393224 | tf_op jit(solution)/shard_map/ppermute | solution.py:128
  123.4 15.5 %copy-start.19 = (f32[8]{0:T(128)S(1)}, f32[8]{0:T(128)}, u32[]{:S(2)}) copy-start(f32[8]{0:T(128)} %constant.127.clone) | copy-start | bytes 100
  123.4 29.6 %all-to-all-start.1 = ((f32[8,64,512]{2,1,0:T(8,128)}), f32[8,64,512]{2,1,0:T(8,128)}, u32[]{:S(2)}, u32[]{:S(2)}) async-start(f32[8,64,512]{2,1,0:T(8,128)} %broadcast_in_dim.18), calls=%async_computation.1 | async-start | bytes 2097152 | tf_op jit(solution)/shard_map/all_to_all | solution.py:30
  139.5 2.6 collective-permute-start.7
  142.1 14.3 %copy-start.14 = (f32[64,512]{1,0:T(8,128)}, f32[64,512]{1,0:T(8,128)S(1)}, u32[]{:S(2)}) copy-start(f32[64,512]{1,0:T(8,128)S(1)} %collective-permute-done.7) | copy-start | bytes 393220
  158.3 5.5 %collective-permute-start.9 = (f32[128,1024]{0,1:T(8,128)}, f32[128,1024]{0,1:T(8,128)}, u32[]{:S(2)}, u32[]{:S(2)}) collective-permute-start(f32[128,1024]{0,1:T(8,128)} %dynamic-slice_bitcast_fusion.6), channel_id=1, source_target_pairs={{0,8},{8,0},{16,24},{24,16},{32,40},{40,32},{48,56},{56,48},{64,72... | collective-permute-start | bytes 1572872 | tf_op jit(solution)/shard_map/ppermute | solution.py:42
  161.9 3.1 %collective-permute-start.8 = (f32[64,512]{1,0:T(8,128)}, f32[64,512]{1,0:T(8,128)S(1)}, u32[]{:S(2)}, u32[]{:S(2)}) collective-permute-start(f32[64,512]{1,0:T(8,128)} %fusion.16), channel_id=1, source_target_pairs={{192,256},{200,264},{208,272},{216,280},{224,288},{232,296},{240,3... | collective-permute-start | bytes 393224 | tf_op jit(solution)/shard_map/ppermute | solution.py:128
  166.8 0.7 collective-permute-start.10
  170.1 19.6 %copy-start.11 = (f32[64,512]{1,0:T(8,128)S(1)}, f32[64,512]{1,0:T(8,128)}, u32[]{:S(2)}) copy-start(f32[64,512]{1,0:T(8,128)} %copy-done.10) | copy-start | bytes 393220
  171.1 17.9 %all-to-all-start.2 = ((f32[4,32,1024]{2,1,0:T(8,128)}), f32[4,32,1024]{2,1,0:T(8,128)S(1)}, u32[]{:S(2)}, u32[]{:S(2)}) async-start(f32[4,32,1024]{2,1,0:T(8,128)} %bitcast.82), calls=%async_computation.2 | async-start | bytes 1048576 | tf_op jit(solution)/shard_map/all_to_all | solution.py:34
  176.9 12.8 %collective-permute-start.11 = (f32[64,512]{1,0:T(8,128)}, f32[64,512]{1,0:T(8,128)}, u32[]{:S(2)}, u32[]{:S(2)}) collective-permute-start(f32[64,512]{1,0:T(8,128)} %fusion.18), channel_id=1, source_target_pairs={{320,384},{328,392},{336,400},{344,408},{352,416},{360,424},{368,4... | collective-permute-start | bytes 393224 | tf_op jit(solution)/shard_map/ppermute | solution.py:128
  192.0 7.5 %copy-start.13 = (f32[64,2048]{1,0:T(8,128)S(1)}, f32[64,2048]{1,0:T(8,128)}, u32[]{:S(2)}) copy-start(f32[64,2048]{1,0:T(8,128)} %param.12) | copy-start | bytes 1572868
  192.0 21.1 %all-to-all-start.3 = ((f32[8,32,1024]{2,1,0:T(8,128)}), f32[8,32,1024]{2,1,0:T(8,128)S(1)}, u32[]{:S(2)}, u32[]{:S(2)}) async-start(f32[8,32,1024]{2,1,0:T(8,128)} %broadcast_in_dim.19), calls=%async_computation.3 | async-start | bytes 2097152 | tf_op jit(solution)/shard_map/all_to_all | solution.py:30
  200.8 1.7 collective-permute-start.12
  256.4 8.2 %collective-permute-start.13 = (f32[4,64,256]{1,2,0:T(8,128)S(1)}, f32[4,64,256]{1,2,0:T(8,128)S(1)}, u32[]{:S(2)}, u32[]{:S(2)}) collective-permute-start(f32[4,64,256]{1,2,0:T(8,128)S(1)} %copy.27), channel_id=1, source_target_pairs={{0,8},{8,0},{16,24},{24,16},{32,40},{40,32},{48,56},{56,48},{64,72... | collective-permute-start | bytes 786440 | tf_op jit(solution)/shard_map/ppermute | solution.py:42
  (14 other events, 29.1 us)

commit v3 on v0

v3 whole, which is shorter than its diff:
```python
import jax
import jax.numpy as jnp
from jax import lax
from jax.sharding import PartitionSpec as P

PLANES, CHIPS, CORES = 8, 4, 2
BLOCKS = PLANES * CHIPS * CORES
SHIFT = 4


def device(plane, chip, core):
    return (plane * CHIPS + chip) * CORES + core


CORE_SWAP = [(p, p ^ 1) for p in range(BLOCKS)]
TO_EVEN = [(p + 1, p) for p in range(0, BLOCKS, CORES)]
NEXT_CHIP = [(p, p + CORES) for p in range(BLOCKS - CORES)]
CORE_GROUPS = [[device(z, c, k) for z in range(PLANES) for c in range(CHIPS)] for k in range(CORES)]


def product(left, right):
    return lax.dot_general(left, right, (((1,), (0,)), ((), ())), precision=lax.Precision.HIGH, preferred_element_type=jnp.float32)


def product_transposed(left, right):
    return lax.dot_general(left, right, (((1,), (1,)), ((), ())), precision=lax.Precision.HIGH, preferred_element_type=jnp.float32)


def exchanged(pieces, axis, groups=None):
    return lax.all_to_all(pieces, axis, 0, 0, axis_index_groups=groups)


def to_all(value, axis, count, groups=None):
    return exchanged(jnp.broadcast_to(value[None], (count,) + value.shape), axis, groups)


def permuted(value, pairs):
    return lax.ppermute(value, "blk", pairs)


def body(diag_inverse, coupling, rhs_t, prior, border_factor, border_rhs):
    rows, size = rhs_t.shape
    members = lax.axis_size("rhs")
    member = lax.axis_index("rhs")
    position = lax.axis_index("blk")
    core = position % CORES
    chip = (position // CORES) % CHIPS
    plane = position // (CORES * CHIPS)
    even = core == 0

    share = coupling.shape[1]
    gathered = to_all(jnp.concatenate([coupling[0], diag_inverse[0]], axis=0), "rhs", members)
    link = gathered[:, :share].reshape(size, size)
    inverse = gathered[:, share:].reshape(size, size)

    block_map = lax.dot_general(link, inverse, (((0,), (1,)), ((), ())), precision=lax.Precision.HIGH, preferred_element_type=jnp.float32)
    block_map = block_map * (-(2.0**-SHIFT))
    offset = product_transposed(rhs_t, inverse)
    offset = jnp.where(position == 0, offset + product(prior, block_map) * 2.0**SHIFT, offset)

    block = jnp.concatenate([block_map, offset], axis=0)
    other = permuted(block, CORE_SWAP)
    first, second = jnp.where(even, block, other), jnp.where(even, other, block)
    pair = product(first, second[:size])
    chip_map = pair[:size]
    chip_offset = pair[size:] * 2.0**SHIFT + second[size:]

    state = jnp.where(even, lax.dynamic_slice_in_dim(chip_map, member * rows, rows, 0), chip_offset)
    factor = jnp.where(even, 1.0, 2.0 ** (2 * SHIFT))
    added = jnp.where(even, 0.0, chip_offset)
    for _ in range(CHIPS - 2):
        state = product(permuted(state, NEXT_CHIP), chip_map) * factor + added
    state = permuted(state, NEXT_CHIP)
    across = permuted(state, CORE_SWAP)
    window = jnp.concatenate([jnp.where(even, state, across), jnp.where(even, across, state)], axis=0)
    window = product(window, jnp.where(even, block_map, chip_map))
    own_offset = window[rows:] * jnp.where(even, 2.0**SHIFT, 2.0 ** (2 * SHIFT)) + jnp.where(even, offset, chip_offset)
    scale = jnp.where(even, 2.0 ** (SHIFT * (2 * CHIPS - 1)), 2.0 ** (SHIFT * 2 * CHIPS))

    arrived = permuted(own_offset, [(device(0, c, 1), device(1, c, 1)) for c in range(CHIPS)])
    own_map = to_all(window[:rows], "rhs", members).reshape(size, size)
    start = jnp.where(plane == 1, arrived, 0.0)
    border_block = None
    for step in range(2, PLANES):
        end = product(start, own_map) * scale + own_offset
        if step == 3:
            end, border_factor = lax.optimization_barrier((end, border_factor))
            border_block = to_all(border_factor, "rhs", members)
        arrived = permuted(end, [(device(step - 1, c, 1), device(step, c, 1)) for c in range(CHIPS)])
        start = jnp.where(plane == step, arrived, start)
    start = jnp.where(even, permuted(start, TO_EVEN), start)
    solved = product(start, own_map) * scale + own_offset

    border = border_rhs.shape[1]
    border_block = border_block.reshape(border, size)
    partial = product_transposed(solved, border_block)
    per_core, per_chip = border // CORES, border // CORES // CHIPS
    per_plane = rows // PLANES
    kept = lax.dynamic_slice_in_dim(partial, core * per_core, per_core, 1)
    passed = lax.dynamic_slice_in_dim(partial, (1 - core) * per_core, per_core, 1)
    total = kept + permuted(passed, CORE_SWAP)
    pieces = jnp.transpose(total.reshape(PLANES, per_plane, CHIPS, per_chip), (0, 2, 1, 3))
    pieces = pieces.reshape(PLANES * CHIPS, per_plane, per_chip)
    total = jnp.sum(exchanged(pieces, "blk", CORE_GROUPS), axis=0)
    held = lax.dynamic_slice(border_rhs, (plane * per_plane, core * per_core + chip * per_chip), (per_plane, per_chip))
    result = to_all(held - total, "blk", PLANES * CHIPS, CORE_GROUPS)
    result = result.reshape(PLANES, CHIPS, per_plane, per_chip)
    result = jnp.transpose(result, (0, 2, 1, 3)).reshape(rows, per_core)
    across = permuted(result, CORE_SWAP)
    return solved, jnp.concatenate([jnp.where(even, result, across), jnp.where(even, across, result)], axis=1)


def solution(mesh):
    placed = (
        P("blk", "rhs", None),
        P("blk", "rhs", None),
        P("rhs", "blk"),
        P("rhs", None),
        P("rhs", "blk"),
        P("rhs", None),
    )
    return jax.shard_map(
        body,
        mesh=mesh,
        in_specs=placed,
        out_specs=(P("rhs", "blk"), P("rhs", None)),
        check_vma=False,
    )
```

time: 1410 us -> 228 us (0.16)
  waiting for transfers between devices: 929 us -> 96 us
  starting transfers between devices: 448 us -> 86.7 us
  blocking collectives: 0 us -> 18.1 us
    psum x1 -> x0, waiting for transfers between devices: 696 us -> none  [body(): summed = lax.psum(partial_sum, 'blk')]
    ppermute x64 -> x15, starting transfers between devices: 448 us -> 50.8 us  [permuted(): return lax.ppermute(value, 'blk', pairs)]
    ppermute x64 -> x15, waiting for transfers between devices: 141 us -> 17.8 us  [permuted(): return lax.ppermute(value, 'blk', pairs)]
    all_gather x3 -> x0, waiting for transfers between devices: 90.9 us -> none  [the longest x1 45.5 us: body(): lax.all_gather(diag_inverse, 'rhs', axis=1, tiled=True)]
    all_to_all x0 -> x4, waiting for transfers between devices: none -> 78.2 us  [exchanged(): return lax.all_to_all(pieces, axis, 0, 0, axis_index_groups=groups)]
    all_to_all x0 -> x4, starting transfers between devices: none -> 36 us  [exchanged(): return lax.all_to_all(pieces, axis, 0, 0, axis_index_groups=groups)]
    all_to_all x0 -> x1, blocking collectives: none -> 18.1 us  [exchanged(): return lax.all_to_all(pieces, axis, 0, 0, axis_index_groups=groups)]
  transfers between devices with their start and end apart: 68 -> 19, of which waited for: 67 -> 13; matrix products, arithmetic and copies ran while one was open for 0% -> 1% of each run, Pallas kernels for 0% -> 0%
where the time goes in v3:
time: 228 us; the launch traced here: 227 us
  waiting for transfers between devices  96 us (42%)
  starting transfers between devices  86.7 us (38%)
  blocking collectives  18.1 us (8%)
  matrix products  13.5 us (6%)
  local copies, waits for them, and re-layouts  6.38 us (3%)
  other arithmetic  4.89 us (2%)
    all_to_all x4, waiting for transfers between devices, exchanged(): return lax.all_to_all(pieces, axis, 0, 0, axis_index_groups=groups)  78.2 us
    ppermute x15, starting transfers between devices, permuted(): return lax.ppermute(value, 'blk', pairs)  50.8 us
    all_to_all x4, starting transfers between devices, exchanged(): return lax.all_to_all(pieces, axis, 0, 0, axis_index_groups=groups)  36 us
    all_to_all x1, blocking collectives, exchanged(): return lax.all_to_all(pieces, axis, 0, 0, axis_index_groups=groups)  18.1 us
    ppermute x15, waiting for transfers between devices, permuted(): return lax.ppermute(value, 'blk', pairs)  17.8 us
    dot_general x12, matrix products, product(): lax.dot_general(left, right, (((1,), (0,)), ((), ())), precision=lax.Prec...  6.78 us
    broadcast_in_dim x4, local copies, waits for them, and re-layouts, to_all(): jnp.broadcast_to(value[None], (count,) + value.shape)  5.3 us
    dot_general x2, matrix products, product_transposed(): lax.dot_general(left, right, (((1,), (1,)), ((), ())), precision=lax.Prec...  4.82 us
  transfers between devices with their start and end apart: 19, of which 13 were waited for; matrix products, arithmetic and copies ran while one was open for 1% of the time, Pallas kernels for 0%

profile of v3, /device:TPU:1, one launch (start us, length us, event | category | flops | bytes accessed | tf_op | source)
XLA Modules:
  0.0 226.8 jit_solution(17899836281441386751)
XLA Ops:
  3.3 5.9 %all-to-all-start = ((f32[8,128,512]{2,1,0:T(8,128)}), f32[8,128,512]{2,1,0:T(8,128)S(1)}, u32[]{:S(2)}, u32[]{:S(2)}) async-start(f32[8,128,512]{2,1,0:T(8,128)} %broadcast_in_dim.14), calls=%async_computation | async-start | bytes 4194304 | tf_op jit(solution)/shard_map/all_to_all | solution.py:30
  9.1 25.1 %all-to-all-done = f32[8,128,512]{2,1,0:T(8,128)S(1)} async-done(((f32[8,128,512]{2,1,0:T(8,128)}), f32[8,128,512]{2,1,0:T(8,128)S(1)}, u32[]{:S(2)}, u32[]{:S(2)}) %all-to-all-start) | async-done | bytes 2097184 | tf_op jit(solution)/shard_map/all_to_all | solution.py:30
  38.9 3.7 %collective-permute-start = (f32[576,512]{1,0:T(8,128)}, f32[576,512]{1,0:T(8,128)S(1)}, u32[]{:S(2)}, u32[]{:S(2)}) collective-permute-start(f32[576,512]{1,0:T(8,128)} %pad_maximum_fusion), channel_id=1, source_target_pairs={{0,8},{8,0},{16,24},{24,16},{32,40},{40,32},{48,56},{56,48},{64,72... | collective-permute-start | bytes 3538952 | tf_op jit(solution)/shard_map/ppermute | solution.py:38
  42.6 2.6 %collective-permute-done = f32[576,512]{1,0:T(8,128)S(1)} collective-permute-done((f32[576,512]{1,0:T(8,128)}, f32[576,512]{1,0:T(8,128)S(1)}, u32[]{:S(2)}, u32[]{:S(2)}) %collective-permute-start) | collective-permute-done | bytes 1179680 | tf_op jit(solution)/shard_map/ppermute | solution.py:38
  45.5 2.0 fusion
  47.7 4.2 %collective-permute-start.1 = (f32[64,512]{1,0:T(8,128)S(1)}, f32[64,512]{1,0:T(8,128)S(1)}, u32[]{:S(2)}, u32[]{:S(2)}) collective-permute-start(f32[64,512]{1,0:T(8,128)S(1)} %get-tuple-element.6), channel_id=1, source_target_pairs={{0,16},{8,24},{16,32},{24,40},{32,48},{40,56},{48,64},{56,72},{64,... | collective-permute-start | bytes 393224 | tf_op jit(solution)/shard_map/ppermute | solution.py:38
  51.9 2.5 %collective-permute-done.1 = f32[64,512]{1,0:T(8,128)S(1)} collective-permute-done((f32[64,512]{1,0:T(8,128)S(1)}, f32[64,512]{1,0:T(8,128)S(1)}, u32[]{:S(2)}, u32[]{:S(2)}) %collective-permute-start.1) | collective-permute-done | bytes 131104 | tf_op jit(solution)/shard_map/ppermute | solution.py:38
  54.9 5.0 %collective-permute-start.2 = (f32[64,512]{1,0:T(8,128)S(1)}, f32[64,512]{1,0:T(8,128)S(1)}, u32[]{:S(2)}, u32[]{:S(2)}) collective-permute-start(f32[64,512]{1,0:T(8,128)S(1)} %fusion.5), channel_id=1, source_target_pairs={{0,16},{8,24},{16,32},{24,40},{32,48},{40,56},{48,64},{56,72},{64,... | collective-permute-start | bytes 393224 | tf_op jit(solution)/shard_map/ppermute | solution.py:38
  59.9 2.2 collective-permute-done.2
  62.5 5.5 %collective-permute-start.3 = (f32[64,512]{1,0:T(8,128)S(1)}, f32[64,512]{1,0:T(8,128)S(1)}, u32[]{:S(2)}, u32[]{:S(2)}) collective-permute-start(f32[64,512]{1,0:T(8,128)S(1)} %fusion.6), channel_id=1, source_target_pairs={{0,16},{8,24},{16,32},{24,40},{32,48},{40,56},{48,64},{56,72},{64,... | collective-permute-start | bytes 393224 | tf_op jit(solution)/shard_map/ppermute | solution.py:38
  68.1 4.3 %collective-permute-done.3 = f32[64,512]{1,0:T(8,128)S(1)} collective-permute-done((f32[64,512]{1,0:T(8,128)S(1)}, f32[64,512]{1,0:T(8,128)S(1)}, u32[]{:S(2)}, u32[]{:S(2)}) %collective-permute-start.3) | collective-permute-done | bytes 131104 | tf_op jit(solution)/shard_map/ppermute | solution.py:38
  72.4 6.7 %collective-permute-start.4 = (f32[64,512]{1,0:T(8,128)S(1)}, f32[64,512]{1,0:T(8,128)S(1)}, u32[]{:S(2)}, u32[]{:S(2)}) collective-permute-start(f32[64,512]{1,0:T(8,128)S(1)} %collective-permute-done.3), channel_id=1, source_target_pairs={{0,8},{8,0},{16,24},{24,16},{32,40},{40,32},{48,56},{56,48},{64,72... | collective-permute-start | bytes 393224 | tf_op jit(solution)/shard_map/ppermute | solution.py:38
  82.1 3.9 %all-to-all-start.1 = ((f32[8,64,512]{2,1,0:T(8,128)}), f32[8,64,512]{2,1,0:T(8,128)S(1)}, u32[]{:S(2)}, u32[]{:S(2)}) async-start(f32[8,64,512]{2,1,0:T(8,128)} %broadcast_in_dim.16), calls=%async_computation.1 | async-start | bytes 2097152 | tf_op jit(solution)/shard_map/all_to_all | solution.py:30
  86.0 11.1 %collective-permute-start.5 = (f32[64,512]{1,0:T(8,128)S(1)}, f32[64,512]{1,0:T(8,128)S(1)}, u32[]{:S(2)}, u32[]{:S(2)}) collective-permute-start(f32[64,512]{1,0:T(8,128)S(1)} %get-tuple-element.13), channel_id=1, source_target_pairs={{8,72},{24,88},{40,104},{56,120},{9,73},{25,89},{41,105},{57,121},... | collective-permute-start | bytes 393224 | tf_op jit(solution)/shard_map/ppermute | solution.py:38
  102.6 2.6 %broadcast_in_dim.17 = f32[8,256,512]{2,1,0:T(8,128)} broadcast(f32[256,512]{1,0:T(8,128)S(1)} %copy-done.3), dimensions={1,2} | broadcast | bytes 4718592 | tf_op jit(solution)/shard_map/broadcast_in_dim | solution.py:34
  105.1 4.6 %all-to-all-start.2 = ((f32[8,256,512]{2,1,0:T(8,128)}), f32[8,256,512]{2,1,0:T(8,128)}, u32[]{:S(2)}, u32[]{:S(2)}) async-start(f32[8,256,512]{2,1,0:T(8,128)} %broadcast_in_dim.17), calls=%async_computation.2 | async-start | bytes 8388608 | tf_op jit(solution)/shard_map/all_to_all | solution.py:30
  115.0 2.7 %collective-permute-start.12 = (f32[64,512]{1,0:T(8,128)S(1)}, f32[64,512]{1,0:T(8,128)S(1)}, u32[]{:S(2)}, u32[]{:S(2)}) collective-permute-start(f32[64,512]{1,0:T(8,128)S(1)} %broadcast_select_fusion.7), channel_id=1, source_target_pairs={{8,0},{24,16},{40,32},{56,48},{72,64},{88,80},{104,96},{120,112},{... | collective-permute-start | bytes 393224 | tf_op jit(solution)/shard_map/ppermute | solution.py:38
  119.1 39.2 %all-to-all-done.2 = f32[8,256,512]{2,1,0:T(8,128)} async-done(((f32[8,256,512]{2,1,0:T(8,128)}), f32[8,256,512]{2,1,0:T(8,128)}, u32[]{:S(2)}, u32[]{:S(2)}) %all-to-all-start.2) | async-done | bytes 4194336 | tf_op jit(solution)/shard_map/all_to_all | solution.py:30
  158.3 4.2 %fusion.36 = f32[64,2048]{1,0:T(8,128)S(1)} fusion(f32[64,512]{1,0:T(8,128)S(1)} %fusion.13, f32[2048,512]{1,0:T(8,128)} %bitcast.7), kind=kOutput, calls=%fused_computation.69 | convolution fusion | flops 402653184 | bytes 4849664 | tf_op jit(solution)/shard_map/dot_general | solution.py:26
  162.6 2.7 %collective-permute-start.13 = (f32[64,1024]{1,0:T(8,128)S(1)}, f32[64,1024]{1,0:T(8,128)S(1)}, u32[]{:S(2)}, u32[]{:S(2)}) collective-permute-start(f32[64,1024]{1,0:T(8,128)S(1)} %constant_dynamic-slice_fusion), channel_id=1, source_target_pairs={{0,8},{8,0},{16,24},{24,16},{32,40},{40,32},{48,56},{56,48},{64,72... | collective-permute-start | bytes 786440 | tf_op jit(solution)/shard_map/ppermute | solution.py:38
  167.2 21.6 %all-to-all-start.3 = ((f32[32,8,256]{2,1,0:T(8,128)}), f32[32,8,256]{2,1,0:T(8,128)S(1)}, u32[]{:S(2)}, u32[]{:S(2)}) async-start(f32[32,8,256]{2,1,0:T(8,128)} %bitcast.10), calls=%async_computation.3 | async-start | bytes 524288 | tf_op jit(solution)/shard_map/all_to_all | solution.py:30
  188.8 12.0 %all-to-all-done.3 = f32[32,8,256]{2,1,0:T(8,128)S(1)} async-done(((f32[32,8,256]{2,1,0:T(8,128)}), f32[32,8,256]{2,1,0:T(8,128)S(1)}, u32[]{:S(2)}, u32[]{:S(2)}) %all-to-all-start.3) | async-done | bytes 262176 | tf_op jit(solution)/shard_map/all_to_all | solution.py:30
  201.6 18.1 %all_to_all.25 = f32[32,8,256]{2,1,0:T(8,128)S(1)} all-to-all(f32[32,8,256]{2,1,0:T(8,128)S(1)} %broadcast_in_dim.18), channel_id=1, replica_groups={{0,16,32,48,64,80,96,112,128,144,160,176,192,208,224,240,256,272,288,30..., dimensions={0} | all-to-all | bytes 524288 | tf_op jit(solution)/shard_map/all_to_all | solution.py:30
  219.7 5.0 %collective-permute-start.14 = (f32[64,1024]{1,0:T(8,128)S(1)}, f32[64,1024]{1,0:T(8,128)S(1)}, u32[]{:S(2)}, u32[]{:S(2)}) collective-permute-start(f32[64,1024]{1,0:T(8,128)S(1)} %bitcast.53), channel_id=1, source_target_pairs={{0,8},{8,0},{16,24},{24,16},{32,40},{40,32},{48,56},{56,48},{64,72... | collective-permute-start | bytes 786440 | tf_op jit(solution)/shard_map/ppermute | solution.py:38
  (63 shorter events, 27.9 us)
Async XLA Ops:
  0.6 35.8 %copy-start = (f32[64,512]{1,0:T(8,128)S(1)}, f32[64,512]{1,0:T(8,128)}, u32[]{:S(2)}) copy-start(f32[64,512]{1,0:T(8,128)} %param.8) | copy-start | bytes 393220
  3.3 31.0 %all-to-all-start = ((f32[8,128,512]{2,1,0:T(8,128)}), f32[8,128,512]{2,1,0:T(8,128)S(1)}, u32[]{:S(2)}, u32[]{:S(2)}) async-start(f32[8,128,512]{2,1,0:T(8,128)} %broadcast_in_dim.14), calls=%async_computation | async-start | bytes 4194304 | tf_op jit(solution)/shard_map/all_to_all | solution.py:30
  36.4 0.9 copy-start.5
  37.7 7.5 %copy-start.1 = (f32[64,512]{1,0:T(8,128)}, f32[64,512]{1,0:T(8,128)S(1)}, u32[]{:S(2)}) copy-start(f32[64,512]{1,0:T(8,128)S(1)} %fusion.4) | copy-start | bytes 393220
  38.9 6.4 %collective-permute-start = (f32[576,512]{1,0:T(8,128)}, f32[576,512]{1,0:T(8,128)S(1)}, u32[]{:S(2)}, u32[]{:S(2)}) collective-permute-start(f32[576,512]{1,0:T(8,128)} %pad_maximum_fusion), channel_id=1, source_target_pairs={{0,8},{8,0},{16,24},{24,16},{32,40},{40,32},{48,56},{56,48},{64,72... | collective-permute-start | bytes 3538952 | tf_op jit(solution)/shard_map/ppermute | solution.py:38
  47.7 6.8 %collective-permute-start.1 = (f32[64,512]{1,0:T(8,128)S(1)}, f32[64,512]{1,0:T(8,128)S(1)}, u32[]{:S(2)}, u32[]{:S(2)}) collective-permute-start(f32[64,512]{1,0:T(8,128)S(1)} %get-tuple-element.6), channel_id=1, source_target_pairs={{0,16},{8,24},{16,32},{24,40},{32,48},{40,56},{48,64},{56,72},{64,... | collective-permute-start | bytes 393224 | tf_op jit(solution)/shard_map/ppermute | solution.py:38
  54.9 7.2 %collective-permute-start.2 = (f32[64,512]{1,0:T(8,128)S(1)}, f32[64,512]{1,0:T(8,128)S(1)}, u32[]{:S(2)}, u32[]{:S(2)}) collective-permute-start(f32[64,512]{1,0:T(8,128)S(1)} %fusion.5), channel_id=1, source_target_pairs={{0,16},{8,24},{16,32},{24,40},{32,48},{40,56},{48,64},{56,72},{64,... | collective-permute-start | bytes 393224 | tf_op jit(solution)/shard_map/ppermute | solution.py:38
  62.5 9.8 %collective-permute-start.3 = (f32[64,512]{1,0:T(8,128)S(1)}, f32[64,512]{1,0:T(8,128)S(1)}, u32[]{:S(2)}, u32[]{:S(2)}) collective-permute-start(f32[64,512]{1,0:T(8,128)S(1)} %fusion.6), channel_id=1, source_target_pairs={{0,16},{8,24},{16,32},{24,40},{32,48},{40,56},{48,64},{56,72},{64,... | collective-permute-start | bytes 393224 | tf_op jit(solution)/shard_map/ppermute | solution.py:38
  72.4 7.6 %collective-permute-start.4 = (f32[64,512]{1,0:T(8,128)S(1)}, f32[64,512]{1,0:T(8,128)S(1)}, u32[]{:S(2)}, u32[]{:S(2)}) collective-permute-start(f32[64,512]{1,0:T(8,128)S(1)} %collective-permute-done.3), channel_id=1, source_target_pairs={{0,8},{8,0},{16,24},{24,16},{32,40},{40,32},{48,56},{56,48},{64,72... | collective-permute-start | bytes 393224 | tf_op jit(solution)/shard_map/ppermute | solution.py:38
  82.1 18.9 %all-to-all-start.1 = ((f32[8,64,512]{2,1,0:T(8,128)}), f32[8,64,512]{2,1,0:T(8,128)S(1)}, u32[]{:S(2)}, u32[]{:S(2)}) async-start(f32[8,64,512]{2,1,0:T(8,128)} %broadcast_in_dim.16), calls=%async_computation.1 | async-start | bytes 2097152 | tf_op jit(solution)/shard_map/all_to_all | solution.py:30
  86.0 13.1 %collective-permute-start.5 = (f32[64,512]{1,0:T(8,128)S(1)}, f32[64,512]{1,0:T(8,128)S(1)}, u32[]{:S(2)}, u32[]{:S(2)}) collective-permute-start(f32[64,512]{1,0:T(8,128)S(1)} %get-tuple-element.13), channel_id=1, source_target_pairs={{8,72},{24,88},{40,104},{56,120},{9,73},{25,89},{41,105},{57,121},... | collective-permute-start | bytes 393224 | tf_op jit(solution)/shard_map/ppermute | solution.py:38
  101.0 1.6 copy-start.3
  101.4 0.7 collective-permute-start.6
  105.1 53.2 %all-to-all-start.2 = ((f32[8,256,512]{2,1,0:T(8,128)}), f32[8,256,512]{2,1,0:T(8,128)}, u32[]{:S(2)}, u32[]{:S(2)}) async-start(f32[8,256,512]{2,1,0:T(8,128)} %broadcast_in_dim.17), calls=%async_computation.2 | async-start | bytes 8388608 | tf_op jit(solution)/shard_map/all_to_all | solution.py:30
  109.7 0.7 collective-permute-start.7
  110.9 0.7 collective-permute-start.8
  112.0 0.7 collective-permute-start.9
  113.1 0.7 collective-permute-start.10
  114.3 0.7 collective-permute-start.11
  115.0 3.7 %collective-permute-start.12 = (f32[64,512]{1,0:T(8,128)S(1)}, f32[64,512]{1,0:T(8,128)S(1)}, u32[]{:S(2)}, u32[]{:S(2)}) collective-permute-start(f32[64,512]{1,0:T(8,128)S(1)} %broadcast_select_fusion.7), channel_id=1, source_target_pairs={{8,0},{24,16},{40,32},{56,48},{72,64},{88,80},{104,96},{120,112},{... | collective-permute-start | bytes 393224 | tf_op jit(solution)/shard_map/ppermute | solution.py:38
  119.1 43.4 %copy-start.4 = (f32[64,512]{1,0:T(8,128)}, f32[64,512]{1,0:T(8,128)S(1)}, u32[]{:S(2)}) copy-start(f32[64,512]{1,0:T(8,128)S(1)} %fusion.13) | copy-start | bytes 393220
  162.6 3.9 %collective-permute-start.13 = (f32[64,1024]{1,0:T(8,128)S(1)}, f32[64,1024]{1,0:T(8,128)S(1)}, u32[]{:S(2)}, u32[]{:S(2)}) collective-permute-start(f32[64,1024]{1,0:T(8,128)S(1)} %constant_dynamic-slice_fusion), channel_id=1, source_target_pairs={{0,8},{8,0},{16,24},{24,16},{32,40},{40,32},{48,56},{56,48},{64,72... | collective-permute-start | bytes 786440 | tf_op jit(solution)/shard_map/ppermute | solution.py:38
  167.2 33.6 %all-to-all-start.3 = ((f32[32,8,256]{2,1,0:T(8,128)}), f32[32,8,256]{2,1,0:T(8,128)S(1)}, u32[]{:S(2)}, u32[]{:S(2)}) async-start(f32[32,8,256]{2,1,0:T(8,128)} %bitcast.10), calls=%async_computation.3 | async-start | bytes 524288 | tf_op jit(solution)/shard_map/all_to_all | solution.py:30
  219.7 6.2 %collective-permute-start.14 = (f32[64,1024]{1,0:T(8,128)S(1)}, f32[64,1024]{1,0:T(8,128)S(1)}, u32[]{:S(2)}, u32[]{:S(2)}) collective-permute-start(f32[64,1024]{1,0:T(8,128)S(1)} %bitcast.53), channel_id=1, source_target_pairs={{0,8},{8,0},{16,24},{24,16},{32,40},{40,32},{48,56},{56,48},{64,72... | collective-permute-start | bytes 786440 | tf_op jit(solution)/shard_map/ppermute | solution.py:38
  (1 other events, 0.9 us)

commit v4 on v3

--- a/solution.py
+++ b/solution.py
@@ -79,13 +79,12 @@
 
     arrived = permuted(own_offset, [(device(0, c, 1), device(1, c, 1)) for c in range(CHIPS)])
     own_map = to_all(window[:rows], "rhs", members).reshape(size, size)
+    copies = jnp.broadcast_to(border_factor[None], (members,) + border_factor.shape)
+    arrived, copies = lax.optimization_barrier((arrived, copies))
+    border_block = exchanged(copies, "rhs")
     start = jnp.where(plane == 1, arrived, 0.0)
-    border_block = None
     for step in range(2, PLANES):
         end = product(start, own_map) * scale + own_offset
-        if step == 3:
-            end, border_factor = lax.optimization_barrier((end, border_factor))
-            border_block = to_all(border_factor, "rhs", members)
         arrived = permuted(end, [(device(step - 1, c, 1), device(step, c, 1)) for c in range(CHIPS)])
         start = jnp.where(plane == step, arrived, start)
     start = jnp.where(even, permuted(start, TO_EVEN), start)

time: 228 us -> 224 us (0.982)
    broadcast_in_dim x4 -> x3, local copies, waits for them, and re-layouts: 5.3 us -> 2.78 us  [to_all(): jnp.broadcast_to(value[None], (count,) + value.shape)]
    broadcast_in_dim x0 -> x1, local copies, waits for them, and re-layouts: none -> 2.51 us  [body(): jnp.broadcast_to(border_factor[None], (members,) + border_factor.shape)]
  transfers between devices with their start and end apart: 19 -> 19, of which waited for: 13 -> 12; matrix products, arithmetic and copies ran while one was open for 1% -> 3% of each run, Pallas kernels for 0% -> 0%
where the time goes in v4:
time: 224 us; the launch traced here: 223 us
  waiting for transfers between devices  94.2 us (42%)
  starting transfers between devices  84.6 us (38%)
  blocking collectives  18.1 us (8%)
  matrix products  13.5 us (6%)
  local copies, waits for them, and re-layouts  6.37 us (3%)
  other arithmetic  4.89 us (2%)
    all_to_all x4, waiting for transfers between devices, exchanged(): return lax.all_to_all(pieces, axis, 0, 0, axis_index_groups=groups)  76.4 us
    ppermute x15, starting transfers between devices, permuted(): return lax.ppermute(value, 'blk', pairs)  49.2 us
    all_to_all x4, starting transfers between devices, exchanged(): return lax.all_to_all(pieces, axis, 0, 0, axis_index_groups=groups)  35.5 us
    all_to_all x1, blocking collectives, exchanged(): return lax.all_to_all(pieces, axis, 0, 0, axis_index_groups=groups)  18.1 us
    ppermute x15, waiting for transfers between devices, permuted(): return lax.ppermute(value, 'blk', pairs)  17.8 us
    dot_general x12, matrix products, product(): lax.dot_general(left, right, (((1,), (0,)), ((), ())), precision=lax.Prec...  6.75 us
    dot_general x2, matrix products, product_transposed(): lax.dot_general(left, right, (((1,), (1,)), ((), ())), precision=lax.Prec...  4.82 us
  transfers between devices with their start and end apart: 19, of which 12 were waited for; matrix products, arithmetic and copies ran while one was open for 3% of the time, Pallas kernels for 0%

profile of v4, /device:TPU:1, one launch (start us, length us, event | category | flops | bytes accessed | tf_op | source)
XLA Modules:
  0.0 222.8 jit_solution(17566660038001388880)
XLA Ops:
  3.3 5.9 %all-to-all-start = ((f32[8,128,512]{2,1,0:T(8,128)}), f32[8,128,512]{2,1,0:T(8,128)S(1)}, u32[]{:S(2)}, u32[]{:S(2)}) async-start(f32[8,128,512]{2,1,0:T(8,128)} %broadcast_in_dim.13), calls=%async_computation | async-start | bytes 4194304 | tf_op jit(solution)/shard_map/all_to_all | solution.py:30
  9.1 25.1 %all-to-all-done = f32[8,128,512]{2,1,0:T(8,128)S(1)} async-done(((f32[8,128,512]{2,1,0:T(8,128)}), f32[8,128,512]{2,1,0:T(8,128)S(1)}, u32[]{:S(2)}, u32[]{:S(2)}) %all-to-all-start) | async-done | bytes 2097184 | tf_op jit(solution)/shard_map/all_to_all | solution.py:30
  38.9 3.7 %collective-permute-start = (f32[576,512]{1,0:T(8,128)}, f32[576,512]{1,0:T(8,128)S(1)}, u32[]{:S(2)}, u32[]{:S(2)}) collective-permute-start(f32[576,512]{1,0:T(8,128)} %pad_maximum_fusion), channel_id=1, source_target_pairs={{0,8},{8,0},{16,24},{24,16},{32,40},{40,32},{48,56},{56,48},{64,72... | collective-permute-start | bytes 3538952 | tf_op jit(solution)/shard_map/ppermute | solution.py:38
  42.6 2.6 %collective-permute-done = f32[576,512]{1,0:T(8,128)S(1)} collective-permute-done((f32[576,512]{1,0:T(8,128)}, f32[576,512]{1,0:T(8,128)S(1)}, u32[]{:S(2)}, u32[]{:S(2)}) %collective-permute-start) | collective-permute-done | bytes 1179680 | tf_op jit(solution)/shard_map/ppermute | solution.py:38
  45.5 2.0 fusion
  47.7 4.2 %collective-permute-start.1 = (f32[64,512]{1,0:T(8,128)S(1)}, f32[64,512]{1,0:T(8,128)S(1)}, u32[]{:S(2)}, u32[]{:S(2)}) collective-permute-start(f32[64,512]{1,0:T(8,128)S(1)} %get-tuple-element.6), channel_id=1, source_target_pairs={{0,16},{8,24},{16,32},{24,40},{32,48},{40,56},{48,64},{56,72},{64,... | collective-permute-start | bytes 393224 | tf_op jit(solution)/shard_map/ppermute | solution.py:38
  51.9 2.5 %collective-permute-done.1 = f32[64,512]{1,0:T(8,128)S(1)} collective-permute-done((f32[64,512]{1,0:T(8,128)S(1)}, f32[64,512]{1,0:T(8,128)S(1)}, u32[]{:S(2)}, u32[]{:S(2)}) %collective-permute-start.1) | collective-permute-done | bytes 131104 | tf_op jit(solution)/shard_map/ppermute | solution.py:38
  54.9 5.0 %collective-permute-start.2 = (f32[64,512]{1,0:T(8,128)S(1)}, f32[64,512]{1,0:T(8,128)S(1)}, u32[]{:S(2)}, u32[]{:S(2)}) collective-permute-start(f32[64,512]{1,0:T(8,128)S(1)} %fusion.5), channel_id=1, source_target_pairs={{0,16},{8,24},{16,32},{24,40},{32,48},{40,56},{48,64},{56,72},{64,... | collective-permute-start | bytes 393224 | tf_op jit(solution)/shard_map/ppermute | solution.py:38
  59.9 2.2 collective-permute-done.2
  62.5 5.5 %collective-permute-start.3 = (f32[64,512]{1,0:T(8,128)S(1)}, f32[64,512]{1,0:T(8,128)S(1)}, u32[]{:S(2)}, u32[]{:S(2)}) collective-permute-start(f32[64,512]{1,0:T(8,128)S(1)} %fusion.6), channel_id=1, source_target_pairs={{0,16},{8,24},{16,32},{24,40},{32,48},{40,56},{48,64},{56,72},{64,... | collective-permute-start | bytes 393224 | tf_op jit(solution)/shard_map/ppermute | solution.py:38
  68.1 4.3 %collective-permute-done.3 = f32[64,512]{1,0:T(8,128)S(1)} collective-permute-done((f32[64,512]{1,0:T(8,128)S(1)}, f32[64,512]{1,0:T(8,128)S(1)}, u32[]{:S(2)}, u32[]{:S(2)}) %collective-permute-start.3) | collective-permute-done | bytes 131104 | tf_op jit(solution)/shard_map/ppermute | solution.py:38
  72.4 6.7 %collective-permute-start.4 = (f32[64,512]{1,0:T(8,128)S(1)}, f32[64,512]{1,0:T(8,128)S(1)}, u32[]{:S(2)}, u32[]{:S(2)}) collective-permute-start(f32[64,512]{1,0:T(8,128)S(1)} %collective-permute-done.3), channel_id=1, source_target_pairs={{0,8},{8,0},{16,24},{24,16},{32,40},{40,32},{48,56},{56,48},{64,72... | collective-permute-start | bytes 393224 | tf_op jit(solution)/shard_map/ppermute | solution.py:38
  82.1 4.1 %all-to-all-start.1 = ((f32[8,64,512]{2,1,0:T(8,128)}), f32[8,64,512]{2,1,0:T(8,128)S(1)}, u32[]{:S(2)}, u32[]{:S(2)}) async-start(f32[8,64,512]{2,1,0:T(8,128)} %broadcast_in_dim.17), calls=%async_computation.1 | async-start | bytes 2097152 | tf_op jit(solution)/shard_map/all_to_all | solution.py:30
  86.2 11.1 %collective-permute-start.5 = (f32[64,512]{1,0:T(8,128)S(1)}, f32[64,512]{1,0:T(8,128)S(1)}, u32[]{:S(2)}, u32[]{:S(2)}) collective-permute-start(f32[64,512]{1,0:T(8,128)S(1)} %get-tuple-element.13), channel_id=1, source_target_pairs={{8,72},{24,88},{40,104},{56,120},{9,73},{25,89},{41,105},{57,121},... | collective-permute-start | bytes 393224 | tf_op jit(solution)/shard_map/ppermute | solution.py:38
  97.4 1.9 collective-permute-done.5
  99.3 2.5 %broadcast_in_dim.16 = f32[8,256,512]{2,1,0:T(8,128)} broadcast(f32[256,512]{1,0:T(8,128)S(1)} %copy-done.3), dimensions={1,2} | broadcast | bytes 4718592 | tf_op jit(solution)/shard_map/broadcast_in_dim | solution.py:82
  101.8 5.1 %all-to-all-start.2 = ((f32[8,256,512]{2,1,0:T(8,128)}), f32[8,256,512]{2,1,0:T(8,128)}, u32[]{:S(2)}, u32[]{:S(2)}) async-start(f32[8,256,512]{2,1,0:T(8,128)} %broadcast_in_dim.16), calls=%async_computation.2 | async-start | bytes 8388608 | tf_op jit(solution)/shard_map/all_to_all | solution.py:30
  116.8 39.3 %all-to-all-done.2 = f32[8,256,512]{2,1,0:T(8,128)} async-done(((f32[8,256,512]{2,1,0:T(8,128)}), f32[8,256,512]{2,1,0:T(8,128)}, u32[]{:S(2)}, u32[]{:S(2)}) %all-to-all-start.2) | async-done | bytes 4194336 | tf_op jit(solution)/shard_map/all_to_all | solution.py:30
  156.0 4.2 %fusion.36 = f32[64,2048]{1,0:T(8,128)S(1)} fusion(f32[64,512]{1,0:T(8,128)S(1)} %fusion.13, f32[2048,512]{1,0:T(8,128)} %bitcast.7), kind=kOutput, calls=%fused_computation.69 | convolution fusion | flops 402653184 | bytes 4849664 | tf_op jit(solution)/shard_map/dot_general | solution.py:26
  160.3 2.3 %collective-permute-start.13 = (f32[64,1024]{1,0:T(8,128)S(1)}, f32[64,1024]{1,0:T(8,128)S(1)}, u32[]{:S(2)}, u32[]{:S(2)}) collective-permute-start(f32[64,1024]{1,0:T(8,128)S(1)} %constant_dynamic-slice_fusion), channel_id=1, source_target_pairs={{0,8},{8,0},{16,24},{24,16},{32,40},{40,32},{48,56},{56,48},{64,72... | collective-permute-start | bytes 786440 | tf_op jit(solution)/shard_map/ppermute | solution.py:38
  164.5 20.4 %all-to-all-start.3 = ((f32[32,8,256]{2,1,0:T(8,128)}), f32[32,8,256]{2,1,0:T(8,128)S(1)}, u32[]{:S(2)}, u32[]{:S(2)}) async-start(f32[32,8,256]{2,1,0:T(8,128)} %bitcast.10), calls=%async_computation.3 | async-start | bytes 524288 | tf_op jit(solution)/shard_map/all_to_all | solution.py:30
  184.9 12.0 %all-to-all-done.3 = f32[32,8,256]{2,1,0:T(8,128)S(1)} async-done(((f32[32,8,256]{2,1,0:T(8,128)}), f32[32,8,256]{2,1,0:T(8,128)S(1)}, u32[]{:S(2)}, u32[]{:S(2)}) %all-to-all-start.3) | async-done | bytes 262176 | tf_op jit(solution)/shard_map/all_to_all | solution.py:30
  197.6 18.1 %all_to_all.25 = f32[32,8,256]{2,1,0:T(8,128)S(1)} all-to-all(f32[32,8,256]{2,1,0:T(8,128)S(1)} %broadcast_in_dim.18), channel_id=1, replica_groups={{0,16,32,48,64,80,96,112,128,144,160,176,192,208,224,240,256,272,288,30..., dimensions={0} | all-to-all | bytes 524288 | tf_op jit(solution)/shard_map/all_to_all | solution.py:30
  215.8 5.0 %collective-permute-start.14 = (f32[64,1024]{1,0:T(8,128)S(1)}, f32[64,1024]{1,0:T(8,128)S(1)}, u32[]{:S(2)}, u32[]{:S(2)}) collective-permute-start(f32[64,1024]{1,0:T(8,128)S(1)} %bitcast.53), channel_id=1, source_target_pairs={{0,8},{8,0},{16,24},{24,16},{32,40},{40,32},{48,56},{56,48},{64,72... | collective-permute-start | bytes 786440 | tf_op jit(solution)/shard_map/ppermute | solution.py:38
  (63 shorter events, 25.7 us)
Async XLA Ops:
  0.6 35.8 %copy-start = (f32[64,512]{1,0:T(8,128)S(1)}, f32[64,512]{1,0:T(8,128)}, u32[]{:S(2)}) copy-start(f32[64,512]{1,0:T(8,128)} %param.8) | copy-start | bytes 393220
  3.3 31.0 %all-to-all-start = ((f32[8,128,512]{2,1,0:T(8,128)}), f32[8,128,512]{2,1,0:T(8,128)S(1)}, u32[]{:S(2)}, u32[]{:S(2)}) async-start(f32[8,128,512]{2,1,0:T(8,128)} %broadcast_in_dim.13), calls=%async_computation | async-start | bytes 4194304 | tf_op jit(solution)/shard_map/all_to_all | solution.py:30
  36.4 0.9 copy-start.5
  37.7 7.5 %copy-start.1 = (f32[64,512]{1,0:T(8,128)}, f32[64,512]{1,0:T(8,128)S(1)}, u32[]{:S(2)}) copy-start(f32[64,512]{1,0:T(8,128)S(1)} %fusion.4) | copy-start | bytes 393220
  38.9 6.4 %collective-permute-start = (f32[576,512]{1,0:T(8,128)}, f32[576,512]{1,0:T(8,128)S(1)}, u32[]{:S(2)}, u32[]{:S(2)}) collective-permute-start(f32[576,512]{1,0:T(8,128)} %pad_maximum_fusion), channel_id=1, source_target_pairs={{0,8},{8,0},{16,24},{24,16},{32,40},{40,32},{48,56},{56,48},{64,72... | collective-permute-start | bytes 3538952 | tf_op jit(solution)/shard_map/ppermute | solution.py:38
  47.7 6.8 %collective-permute-start.1 = (f32[64,512]{1,0:T(8,128)S(1)}, f32[64,512]{1,0:T(8,128)S(1)}, u32[]{:S(2)}, u32[]{:S(2)}) collective-permute-start(f32[64,512]{1,0:T(8,128)S(1)} %get-tuple-element.6), channel_id=1, source_target_pairs={{0,16},{8,24},{16,32},{24,40},{32,48},{40,56},{48,64},{56,72},{64,... | collective-permute-start | bytes 393224 | tf_op jit(solution)/shard_map/ppermute | solution.py:38
  54.9 7.2 %collective-permute-start.2 = (f32[64,512]{1,0:T(8,128)S(1)}, f32[64,512]{1,0:T(8,128)S(1)}, u32[]{:S(2)}, u32[]{:S(2)}) collective-permute-start(f32[64,512]{1,0:T(8,128)S(1)} %fusion.5), channel_id=1, source_target_pairs={{0,16},{8,24},{16,32},{24,40},{32,48},{40,56},{48,64},{56,72},{64,... | collective-permute-start | bytes 393224 | tf_op jit(solution)/shard_map/ppermute | solution.py:38
  62.5 9.8 %collective-permute-start.3 = (f32[64,512]{1,0:T(8,128)S(1)}, f32[64,512]{1,0:T(8,128)S(1)}, u32[]{:S(2)}, u32[]{:S(2)}) collective-permute-start(f32[64,512]{1,0:T(8,128)S(1)} %fusion.6), channel_id=1, source_target_pairs={{0,16},{8,24},{16,32},{24,40},{32,48},{40,56},{48,64},{56,72},{64,... | collective-permute-start | bytes 393224 | tf_op jit(solution)/shard_map/ppermute | solution.py:38
  72.4 7.6 %collective-permute-start.4 = (f32[64,512]{1,0:T(8,128)S(1)}, f32[64,512]{1,0:T(8,128)S(1)}, u32[]{:S(2)}, u32[]{:S(2)}) collective-permute-start(f32[64,512]{1,0:T(8,128)S(1)} %collective-permute-done.3), channel_id=1, source_target_pairs={{0,8},{8,0},{16,24},{24,16},{32,40},{40,32},{48,56},{56,48},{64,72... | collective-permute-start | bytes 393224 | tf_op jit(solution)/shard_map/ppermute | solution.py:38
  82.1 17.2 %copy-start.3 = (f32[256,512]{1,0:T(8,128)S(1)}, f32[256,512]{1,0:T(8,128)}, u32[]{:S(2)}) copy-start(f32[256,512]{1,0:T(8,128)} %param.10) | copy-start | bytes 1572868
  82.1 19.7 %all-to-all-start.1 = ((f32[8,64,512]{2,1,0:T(8,128)}), f32[8,64,512]{2,1,0:T(8,128)S(1)}, u32[]{:S(2)}, u32[]{:S(2)}) async-start(f32[8,64,512]{2,1,0:T(8,128)} %broadcast_in_dim.17), calls=%async_computation.1 | async-start | bytes 2097152 | tf_op jit(solution)/shard_map/all_to_all | solution.py:30
  86.2 13.1 %collective-permute-start.5 = (f32[64,512]{1,0:T(8,128)S(1)}, f32[64,512]{1,0:T(8,128)S(1)}, u32[]{:S(2)}, u32[]{:S(2)}) collective-permute-start(f32[64,512]{1,0:T(8,128)S(1)} %get-tuple-element.13), channel_id=1, source_target_pairs={{8,72},{24,88},{40,104},{56,120},{9,73},{25,89},{41,105},{57,121},... | collective-permute-start | bytes 393224 | tf_op jit(solution)/shard_map/ppermute | solution.py:38
  101.8 54.2 %all-to-all-start.2 = ((f32[8,256,512]{2,1,0:T(8,128)}), f32[8,256,512]{2,1,0:T(8,128)}, u32[]{:S(2)}, u32[]{:S(2)}) async-start(f32[8,256,512]{2,1,0:T(8,128)} %broadcast_in_dim.16), calls=%async_computation.2 | async-start | bytes 8388608 | tf_op jit(solution)/shard_map/all_to_all | solution.py:30
  107.4 0.7 collective-permute-start.6
  108.5 0.7 collective-permute-start.7
  109.7 0.7 collective-permute-start.8
  110.8 0.7 collective-permute-start.9
  111.9 0.7 collective-permute-start.10
  113.1 0.7 collective-permute-start.11
  113.8 2.5 %collective-permute-start.12 = (f32[64,512]{1,0:T(8,128)S(1)}, f32[64,512]{1,0:T(8,128)S(1)}, u32[]{:S(2)}, u32[]{:S(2)}) collective-permute-start(f32[64,512]{1,0:T(8,128)S(1)} %broadcast_select_fusion.7), channel_id=1, source_target_pairs={{8,0},{24,16},{40,32},{56,48},{72,64},{88,80},{104,96},{120,112},{... | collective-permute-start | bytes 393224 | tf_op jit(solution)/shard_map/ppermute | solution.py:38
  116.7 43.5 %copy-start.4 = (f32[64,512]{1,0:T(8,128)}, f32[64,512]{1,0:T(8,128)S(1)}, u32[]{:S(2)}) copy-start(f32[64,512]{1,0:T(8,128)S(1)} %fusion.13) | copy-start | bytes 393220
  160.3 3.5 %collective-permute-start.13 = (f32[64,1024]{1,0:T(8,128)S(1)}, f32[64,1024]{1,0:T(8,128)S(1)}, u32[]{:S(2)}, u32[]{:S(2)}) collective-permute-start(f32[64,1024]{1,0:T(8,128)S(1)} %constant_dynamic-slice_fusion), channel_id=1, source_target_pairs={{0,8},{8,0},{16,24},{24,16},{32,40},{40,32},{48,56},{56,48},{64,72... | collective-permute-start | bytes 786440 | tf_op jit(solution)/shard_map/ppermute | solution.py:38
  164.5 32.4 %all-to-all-start.3 = ((f32[32,8,256]{2,1,0:T(8,128)}), f32[32,8,256]{2,1,0:T(8,128)S(1)}, u32[]{:S(2)}, u32[]{:S(2)}) async-start(f32[32,8,256]{2,1,0:T(8,128)} %bitcast.10), calls=%async_computation.3 | async-start | bytes 524288 | tf_op jit(solution)/shard_map/all_to_all | solution.py:30
  215.8 6.2 %collective-permute-start.14 = (f32[64,1024]{1,0:T(8,128)S(1)}, f32[64,1024]{1,0:T(8,128)S(1)}, u32[]{:S(2)}, u32[]{:S(2)}) collective-permute-start(f32[64,1024]{1,0:T(8,128)S(1)} %bitcast.53), channel_id=1, source_target_pairs={{0,8},{8,0},{16,24},{24,16},{32,40},{40,32},{48,56},{56,48},{64,72... | collective-permute-start | bytes 786440 | tf_op jit(solution)/shard_map/ppermute | solution.py:38
  (1 other events, 0.9 us)

commit v5 on v4

--- a/solution.py
+++ b/solution.py
@@ -60,6 +60,15 @@
 
     block = jnp.concatenate([block_map, offset], axis=0)
     other = permuted(block, CORE_SWAP)
+    border = border_rhs.shape[1]
+    half = size // 2
+
+    def border_copies(part):
+        return jnp.broadcast_to(part[None], (members,) + part.shape)
+
+    other, copies = lax.optimization_barrier((other, border_copies(border_factor[:, :half])))
+    border_left = exchanged(copies, "rhs")
+
     first, second = jnp.where(even, block, other), jnp.where(even, other, block)
     pair = product(first, second[:size])
     chip_map = pair[:size]
@@ -79,9 +88,8 @@
 
     arrived = permuted(own_offset, [(device(0, c, 1), device(1, c, 1)) for c in range(CHIPS)])
     own_map = to_all(window[:rows], "rhs", members).reshape(size, size)
-    copies = jnp.broadcast_to(border_factor[None], (members,) + border_factor.shape)
-    arrived, copies = lax.optimization_barrier((arrived, copies))
-    border_block = exchanged(copies, "rhs")
+    arrived, copies = lax.optimization_barrier((arrived, border_copies(border_factor[:, half:])))
+    border_right = exchanged(copies, "rhs")
     start = jnp.where(plane == 1, arrived, 0.0)
     for step in range(2, PLANES):
         end = product(start, own_map) * scale + own_offset
@@ -90,9 +98,8 @@
     start = jnp.where(even, permuted(start, TO_EVEN), start)
     solved = product(start, own_map) * scale + own_offset
 
-    border = border_rhs.shape[1]
-    border_block = border_block.reshape(border, size)
-    partial = product_transposed(solved, border_block)
+    partial = product_transposed(solved[:, :half], border_left.reshape(border, half))
+    partial = partial + product_transposed(solved[:, half:], border_right.reshape(border, half))
     per_core, per_chip = border // CORES, border // CORES // CHIPS
     per_plane = rows // PLANES
     kept = lax.dynamic_slice_in_dim(partial, core * per_core, per_core, 1)

time: 224 us -> 244 us (1.089)
  waiting for transfers between devices: 94.2 us -> 67.2 us
  starting transfers between devices: 84.6 us -> 106 us
  blocking collectives: 18.1 us -> 36.4 us
  matrix products: 13.5 us -> 18.8 us
    all_to_all x4, waiting for transfers between devices: 76.4 us -> 50.4 us  [exchanged(): return lax.all_to_all(pieces, axis, 0, 0, axis_index_groups=groups)]
    all_to_all x1 -> x2, blocking collectives: 18.1 us -> 36.4 us  [exchanged(): return lax.all_to_all(pieces, axis, 0, 0, axis_index_groups=groups)]
    all_to_all x4, starting transfers between devices: 35.5 us -> 50.9 us  [exchanged(): return lax.all_to_all(pieces, axis, 0, 0, axis_index_groups=groups)]
    ppermute x15, starting transfers between devices: 49.2 us -> 55.4 us  [permuted(): return lax.ppermute(value, 'blk', pairs)]
    dot_general x12, matrix products: 6.75 us -> 12.5 us  [product(): lax.dot_general(left, right, (((1,), (0,)), ((), ())), precision=lax.Prec...]
  transfers between devices with their start and end apart: 19 -> 19, of which waited for: 12 -> 13; matrix products, arithmetic and copies ran while one was open for 3% -> 6% of each run, Pallas kernels for 0% -> 0%
where the time goes in v5:
time: 244 us; the launch traced here: 243 us
  starting transfers between devices  106 us (43%)
  waiting for transfers between devices  67.2 us (28%)
  blocking collectives  36.4 us (15%)
  matrix products  18.8 us (8%)
  local copies, waits for them, and re-layouts  8.26 us (3%)
  other arithmetic  5.58 us (2%)
    ppermute x15, starting transfers between devices, permuted(): return lax.ppermute(value, 'blk', pairs)  55.4 us
    all_to_all x4, starting transfers between devices, exchanged(): return lax.all_to_all(pieces, axis, 0, 0, axis_index_groups=groups)  50.9 us
    all_to_all x4, waiting for transfers between devices, exchanged(): return lax.all_to_all(pieces, axis, 0, 0, axis_index_groups=groups)  50.4 us
    all_to_all x2, blocking collectives, exchanged(): return lax.all_to_all(pieces, axis, 0, 0, axis_index_groups=groups)  36.4 us
    ppermute x15, waiting for transfers between devices, permuted(): return lax.ppermute(value, 'blk', pairs)  16.8 us
    dot_general x12, matrix products, product(): lax.dot_general(left, right, (((1,), (0,)), ((), ())), precision=lax.Prec...  12.5 us
  transfers between devices with their start and end apart: 19, of which 13 were waited for; matrix products, arithmetic and copies ran while one was open for 6% of the time, Pallas kernels for 0%

profile of v5, /device:TPU:1, one launch (start us, length us, event | category | flops | bytes accessed | tf_op | source)
XLA Modules:
  0.0 243.4 jit_solution(17414351240769198329)
XLA Ops:
  3.3 5.9 %all-to-all-start = ((f32[8,128,512]{2,1,0:T(8,128)}), f32[8,128,512]{2,1,0:T(8,128)S(1)}, u32[]{:S(2)}, u32[]{:S(2)}) async-start(f32[8,128,512]{2,1,0:T(8,128)} %broadcast_in_dim.15), calls=%async_computation | async-start | bytes 4194304 | tf_op jit(solution)/shard_map/all_to_all | solution.py:30
  9.1 25.1 %all-to-all-done = f32[8,128,512]{2,1,0:T(8,128)S(1)} async-done(((f32[8,128,512]{2,1,0:T(8,128)}), f32[8,128,512]{2,1,0:T(8,128)S(1)}, u32[]{:S(2)}, u32[]{:S(2)}) %all-to-all-start) | async-done | bytes 2097184 | tf_op jit(solution)/shard_map/all_to_all | solution.py:30
  38.9 3.8 %collective-permute-start = (f32[576,512]{1,0:T(8,128)}, f32[576,512]{1,0:T(8,128)S(1)}, u32[]{:S(2)}, u32[]{:S(2)}) collective-permute-start(f32[576,512]{1,0:T(8,128)} %pad_maximum_fusion), channel_id=1, source_target_pairs={{0,8},{8,0},{16,24},{24,16},{32,40},{40,32},{48,56},{56,48},{64,72... | collective-permute-start | bytes 3538952 | tf_op jit(solution)/shard_map/ppermute | solution.py:38
  49.2 4.2 %collective-permute-start.1 = (f32[64,512]{1,0:T(8,128)S(1)}, f32[64,512]{1,0:T(8,128)S(1)}, u32[]{:S(2)}, u32[]{:S(2)}) collective-permute-start(f32[64,512]{1,0:T(8,128)S(1)} %get-tuple-element.10), channel_id=1, source_target_pairs={{0,16},{8,24},{16,32},{24,40},{32,48},{40,56},{48,64},{56,72},{64,... | collective-permute-start | bytes 393224 | tf_op jit(solution)/shard_map/ppermute | solution.py:38
  53.5 2.5 %collective-permute-done.1 = f32[64,512]{1,0:T(8,128)S(1)} collective-permute-done((f32[64,512]{1,0:T(8,128)S(1)}, f32[64,512]{1,0:T(8,128)S(1)}, u32[]{:S(2)}, u32[]{:S(2)}) %collective-permute-start.1) | collective-permute-done | bytes 131104 | tf_op jit(solution)/shard_map/ppermute | solution.py:38
  56.4 5.0 %collective-permute-start.2 = (f32[64,512]{1,0:T(8,128)S(1)}, f32[64,512]{1,0:T(8,128)S(1)}, u32[]{:S(2)}, u32[]{:S(2)}) collective-permute-start(f32[64,512]{1,0:T(8,128)S(1)} %fusion.5), channel_id=1, source_target_pairs={{0,16},{8,24},{16,32},{24,40},{32,48},{40,56},{48,64},{56,72},{64,... | collective-permute-start | bytes 393224 | tf_op jit(solution)/shard_map/ppermute | solution.py:38
  61.4 2.2 collective-permute-done.2
  64.1 5.5 %collective-permute-start.3 = (f32[64,512]{1,0:T(8,128)S(1)}, f32[64,512]{1,0:T(8,128)S(1)}, u32[]{:S(2)}, u32[]{:S(2)}) collective-permute-start(f32[64,512]{1,0:T(8,128)S(1)} %fusion.6), channel_id=1, source_target_pairs={{0,16},{8,24},{16,32},{24,40},{32,48},{40,56},{48,64},{56,72},{64,... | collective-permute-start | bytes 393224 | tf_op jit(solution)/shard_map/ppermute | solution.py:38
  69.6 4.3 %collective-permute-done.3 = f32[64,512]{1,0:T(8,128)S(1)} collective-permute-done((f32[64,512]{1,0:T(8,128)S(1)}, f32[64,512]{1,0:T(8,128)S(1)}, u32[]{:S(2)}, u32[]{:S(2)}) %collective-permute-start.3) | collective-permute-done | bytes 131104 | tf_op jit(solution)/shard_map/ppermute | solution.py:38
  73.9 6.7 %collective-permute-start.4 = (f32[64,512]{1,0:T(8,128)S(1)}, f32[64,512]{1,0:T(8,128)S(1)}, u32[]{:S(2)}, u32[]{:S(2)}) collective-permute-start(f32[64,512]{1,0:T(8,128)S(1)} %collective-permute-done.3), channel_id=1, source_target_pairs={{0,8},{8,0},{16,24},{24,16},{32,40},{40,32},{48,56},{56,48},{64,72... | collective-permute-start | bytes 393224 | tf_op jit(solution)/shard_map/ppermute | solution.py:38
  82.6 18.2 %all_to_all.30 = f32[8,64,512]{2,1,0:T(8,128)S(1)} all-to-all(f32[8,64,512]{2,1,0:T(8,128)S(1)} %broadcast_in_dim.20), channel_id=1, replica_groups=mesh['blk'=64,'rhs'=8] {'rhs'}, dimensions={0} | all-to-all | bytes 2097152 | tf_op jit(solution)/shard_map/all_to_all | solution.py:30
  100.8 3.6 %all-to-all-start.2 = ((f32[8,256,256]{2,1,0:T(8,128)}), f32[8,256,256]{2,1,0:T(8,128)S(1)}, u32[]{:S(2)}, u32[]{:S(2)}) async-start(f32[8,256,256]{2,1,0:T(8,128)} %broadcast_in_dim.16), calls=%async_computation.2 | async-start | bytes 4194304 | tf_op jit(solution)/shard_map/all_to_all | solution.py:30
  104.4 11.2 %collective-permute-start.5 = (f32[64,512]{1,0:T(8,128)S(1)}, f32[64,512]{1,0:T(8,128)S(1)}, u32[]{:S(2)}, u32[]{:S(2)}) collective-permute-start(f32[64,512]{1,0:T(8,128)S(1)} %get-tuple-element.19), channel_id=1, source_target_pairs={{8,72},{24,88},{40,104},{56,120},{9,73},{25,89},{41,105},{57,121},... | collective-permute-start | bytes 393224 | tf_op jit(solution)/shard_map/ppermute | solution.py:38
  117.5 2.5 %broadcast_in_dim.18 = f32[8,256,256]{2,1,0:T(8,128)} broadcast(f32[256,256]{1,0:T(8,128)} %get-tuple-element.16), dimensions={1,2} | broadcast | bytes 2359296 | tf_op jit(solution)/shard_map/broadcast_in_dim | solution.py:67
  120.0 10.5 %all-to-all-done.2 = f32[8,256,256]{2,1,0:T(8,128)S(1)} async-done(((f32[8,256,256]{2,1,0:T(8,128)}), f32[8,256,256]{2,1,0:T(8,128)S(1)}, u32[]{:S(2)}, u32[]{:S(2)}) %all-to-all-start.2) | async-done | bytes 2097184 | tf_op jit(solution)/shard_map/all_to_all | solution.py:30
  130.5 4.3 %all-to-all-start.3 = ((f32[8,256,256]{2,1,0:T(8,128)}), f32[8,256,256]{2,1,0:T(8,128)}, u32[]{:S(2)}, u32[]{:S(2)}) async-start(f32[8,256,256]{2,1,0:T(8,128)} %broadcast_in_dim.18), calls=%async_computation.3 | async-start | bytes 4194304 | tf_op jit(solution)/shard_map/all_to_all | solution.py:30
  151.7 3.4 %collective-permute-start.12 = (f32[64,512]{1,0:T(8,128)}, f32[64,512]{1,0:T(8,128)}, u32[]{:S(2)}, u32[]{:S(2)}) collective-permute-start(f32[64,512]{1,0:T(8,128)} %broadcast_select_fusion.7), channel_id=1, source_target_pairs={{8,0},{24,16},{40,32},{56,48},{72,64},{88,80},{104,96},{120,112},{... | collective-permute-start | bytes 393224 | tf_op jit(solution)/shard_map/ppermute | solution.py:38
  158.2 2.8 %all-to-all-done.3 = f32[8,256,256]{2,1,0:T(8,128)} async-done(((f32[8,256,256]{2,1,0:T(8,128)}), f32[8,256,256]{2,1,0:T(8,128)}, u32[]{:S(2)}, u32[]{:S(2)}) %all-to-all-start.3) | async-done | bytes 2097184 | tf_op jit(solution)/shard_map/all_to_all | solution.py:30
  161.0 2.7 %convolution_add_fusion = f32[64,2048]{1,0:T(8,128)S(1)} fusion(f32[64,2048]{1,0:T(8,128)S(1)} %fusion.26, f32[2048,256]{1,0:T(8,128)} %bitcast.8, f32[64,512]{1,0:T(8,128)S(1)} %fusion.13), kind=kOutput, calls=%fused_computation | convolution fusion | flops 201457664 | bytes 3211264 | tf_op jit(solution)/shard_map/dot_general | solution.py:26
  163.7 2.7 %collective-permute-start.13 = (f32[64,1024]{1,0:T(8,128)S(1)}, f32[64,1024]{1,0:T(8,128)S(1)}, u32[]{:S(2)}, u32[]{:S(2)}) collective-permute-start(f32[64,1024]{1,0:T(8,128)S(1)} %constant_dynamic-slice_fusion), channel_id=1, source_target_pairs={{0,8},{8,0},{16,24},{24,16},{32,40},{40,32},{48,56},{56,48},{64,72... | collective-permute-start | bytes 786440 | tf_op jit(solution)/shard_map/ppermute | solution.py:38
  168.4 37.1 %all-to-all-start.4 = ((f32[32,8,256]{2,1,0:T(8,128)}), f32[32,8,256]{2,1,0:T(8,128)S(1)}, u32[]{:S(2)}, u32[]{:S(2)}) async-start(f32[32,8,256]{2,1,0:T(8,128)} %bitcast.11), calls=%async_computation.4 | async-start | bytes 524288 | tf_op jit(solution)/shard_map/all_to_all | solution.py:30
  205.5 11.9 %all-to-all-done.4 = f32[32,8,256]{2,1,0:T(8,128)S(1)} async-done(((f32[32,8,256]{2,1,0:T(8,128)}), f32[32,8,256]{2,1,0:T(8,128)S(1)}, u32[]{:S(2)}, u32[]{:S(2)}) %all-to-all-start.4) | async-done | bytes 262176 | tf_op jit(solution)/shard_map/all_to_all | solution.py:30
  218.2 18.2 %all_to_all.31 = f32[32,8,256]{2,1,0:T(8,128)S(1)} all-to-all(f32[32,8,256]{2,1,0:T(8,128)S(1)} %broadcast_in_dim.21), channel_id=1, replica_groups={{0,16,32,48,64,80,96,112,128,144,160,176,192,208,224,240,256,272,288,30..., dimensions={0} | all-to-all | bytes 524288 | tf_op jit(solution)/shard_map/all_to_all | solution.py:30
  236.4 5.1 %collective-permute-start.14 = (f32[64,1024]{1,0:T(8,128)S(1)}, f32[64,1024]{1,0:T(8,128)S(1)}, u32[]{:S(2)}, u32[]{:S(2)}) collective-permute-start(f32[64,1024]{1,0:T(8,128)S(1)} %bitcast.55), channel_id=1, source_target_pairs={{0,8},{8,0},{16,24},{24,16},{32,40},{40,32},{48,56},{56,48},{64,72... | collective-permute-start | bytes 786440 | tf_op jit(solution)/shard_map/ppermute | solution.py:38
  (73 shorter events, 43.1 us)
Async XLA Ops:
  0.6 35.8 %copy-start = (f32[64,512]{1,0:T(8,128)S(1)}, f32[64,512]{1,0:T(8,128)}, u32[]{:S(2)}) copy-start(f32[64,512]{1,0:T(8,128)} %param.8) | copy-start | bytes 393220
  3.3 31.0 %all-to-all-start = ((f32[8,128,512]{2,1,0:T(8,128)}), f32[8,128,512]{2,1,0:T(8,128)S(1)}, u32[]{:S(2)}, u32[]{:S(2)}) async-start(f32[8,128,512]{2,1,0:T(8,128)} %broadcast_in_dim.15), calls=%async_computation | async-start | bytes 4194304 | tf_op jit(solution)/shard_map/all_to_all | solution.py:30
  37.7 9.1 %copy-start.1 = (f32[64,512]{1,0:T(8,128)}, f32[64,512]{1,0:T(8,128)S(1)}, u32[]{:S(2)}) copy-start(f32[64,512]{1,0:T(8,128)S(1)} %fusion.4) | copy-start | bytes 393220
  37.8 4.9 %copy-start.6 = (f32[256,512]{1,0:T(8,128)S(1)}, f32[256,512]{1,0:T(8,128)}, u32[]{:S(2)}) copy-start(f32[256,512]{1,0:T(8,128)} %param.10) | copy-start | bytes 1572868
  38.9 6.4 %collective-permute-start = (f32[576,512]{1,0:T(8,128)}, f32[576,512]{1,0:T(8,128)S(1)}, u32[]{:S(2)}, u32[]{:S(2)}) collective-permute-start(f32[576,512]{1,0:T(8,128)} %pad_maximum_fusion), channel_id=1, source_target_pairs={{0,8},{8,0},{16,24},{24,16},{32,40},{40,32},{48,56},{56,48},{64,72... | collective-permute-start | bytes 3538952 | tf_op jit(solution)/shard_map/ppermute | solution.py:38
  49.2 6.8 %collective-permute-start.1 = (f32[64,512]{1,0:T(8,128)S(1)}, f32[64,512]{1,0:T(8,128)S(1)}, u32[]{:S(2)}, u32[]{:S(2)}) collective-permute-start(f32[64,512]{1,0:T(8,128)S(1)} %get-tuple-element.10), channel_id=1, source_target_pairs={{0,16},{8,24},{16,32},{24,40},{32,48},{40,56},{48,64},{56,72},{64,... | collective-permute-start | bytes 393224 | tf_op jit(solution)/shard_map/ppermute | solution.py:38
  56.4 7.2 %collective-permute-start.2 = (f32[64,512]{1,0:T(8,128)S(1)}, f32[64,512]{1,0:T(8,128)S(1)}, u32[]{:S(2)}, u32[]{:S(2)}) collective-permute-start(f32[64,512]{1,0:T(8,128)S(1)} %fusion.5), channel_id=1, source_target_pairs={{0,16},{8,24},{16,32},{24,40},{32,48},{40,56},{48,64},{56,72},{64,... | collective-permute-start | bytes 393224 | tf_op jit(solution)/shard_map/ppermute | solution.py:38
  64.1 9.8 %collective-permute-start.3 = (f32[64,512]{1,0:T(8,128)S(1)}, f32[64,512]{1,0:T(8,128)S(1)}, u32[]{:S(2)}, u32[]{:S(2)}) collective-permute-start(f32[64,512]{1,0:T(8,128)S(1)} %fusion.6), channel_id=1, source_target_pairs={{0,16},{8,24},{16,32},{24,40},{32,48},{40,56},{48,64},{56,72},{64,... | collective-permute-start | bytes 393224 | tf_op jit(solution)/shard_map/ppermute | solution.py:38
  73.9 7.6 %collective-permute-start.4 = (f32[64,512]{1,0:T(8,128)S(1)}, f32[64,512]{1,0:T(8,128)S(1)}, u32[]{:S(2)}, u32[]{:S(2)}) collective-permute-start(f32[64,512]{1,0:T(8,128)S(1)} %collective-permute-done.3), channel_id=1, source_target_pairs={{0,8},{8,0},{16,24},{24,16},{32,40},{40,32},{48,56},{56,48},{64,72... | collective-permute-start | bytes 393224 | tf_op jit(solution)/shard_map/ppermute | solution.py:38
  100.8 29.7 %all-to-all-start.2 = ((f32[8,256,256]{2,1,0:T(8,128)}), f32[8,256,256]{2,1,0:T(8,128)S(1)}, u32[]{:S(2)}, u32[]{:S(2)}) async-start(f32[8,256,256]{2,1,0:T(8,128)} %broadcast_in_dim.16), calls=%async_computation.2 | async-start | bytes 4194304 | tf_op jit(solution)/shard_map/all_to_all | solution.py:30
  104.4 13.1 %collective-permute-start.5 = (f32[64,512]{1,0:T(8,128)S(1)}, f32[64,512]{1,0:T(8,128)S(1)}, u32[]{:S(2)}, u32[]{:S(2)}) collective-permute-start(f32[64,512]{1,0:T(8,128)S(1)} %get-tuple-element.19), channel_id=1, source_target_pairs={{8,72},{24,88},{40,104},{56,120},{9,73},{25,89},{41,105},{57,121},... | collective-permute-start | bytes 393224 | tf_op jit(solution)/shard_map/ppermute | solution.py:38
  117.5 19.8 %copy-start.5 = (f32[64,512]{1,0:T(8,128)}, f32[64,512]{1,0:T(8,128)S(1)}, u32[]{:S(2)}) copy-start(f32[64,512]{1,0:T(8,128)S(1)} %collective-permute-done.5) | copy-start | bytes 393220
  130.5 30.5 %all-to-all-start.3 = ((f32[8,256,256]{2,1,0:T(8,128)}), f32[8,256,256]{2,1,0:T(8,128)}, u32[]{:S(2)}, u32[]{:S(2)}) async-start(f32[8,256,256]{2,1,0:T(8,128)} %broadcast_in_dim.18), calls=%async_computation.3 | async-start | bytes 4194304 | tf_op jit(solution)/shard_map/all_to_all | solution.py:30
  136.0 1.3 collective-permute-start.6
  138.4 1.3 collective-permute-start.7
  140.8 1.3 collective-permute-start.8
  143.2 1.3 collective-permute-start.9
  146.3 4.7 %copy-start.4 = (f32[64,512]{1,0:T(8,128)S(1)}, f32[64,512]{1,0:T(8,128)}, u32[]{:S(2)}) copy-start(f32[64,512]{1,0:T(8,128)} %copy-done.3) | copy-start | bytes 393220
  146.3 1.4 collective-permute-start.10
  149.7 1.3 collective-permute-start.11
  151.7 4.1 %collective-permute-start.12 = (f32[64,512]{1,0:T(8,128)}, f32[64,512]{1,0:T(8,128)}, u32[]{:S(2)}, u32[]{:S(2)}) collective-permute-start(f32[64,512]{1,0:T(8,128)} %broadcast_select_fusion.7), channel_id=1, source_target_pairs={{8,0},{24,16},{40,32},{56,48},{72,64},{88,80},{104,96},{120,112},{... | collective-permute-start | bytes 393224 | tf_op jit(solution)/shard_map/ppermute | solution.py:38
  163.7 3.9 %collective-permute-start.13 = (f32[64,1024]{1,0:T(8,128)S(1)}, f32[64,1024]{1,0:T(8,128)S(1)}, u32[]{:S(2)}, u32[]{:S(2)}) collective-permute-start(f32[64,1024]{1,0:T(8,128)S(1)} %constant_dynamic-slice_fusion), channel_id=1, source_target_pairs={{0,8},{8,0},{16,24},{24,16},{32,40},{40,32},{48,56},{56,48},{64,72... | collective-permute-start | bytes 786440 | tf_op jit(solution)/shard_map/ppermute | solution.py:38
  168.4 49.0 %all-to-all-start.4 = ((f32[32,8,256]{2,1,0:T(8,128)}), f32[32,8,256]{2,1,0:T(8,128)S(1)}, u32[]{:S(2)}, u32[]{:S(2)}) async-start(f32[32,8,256]{2,1,0:T(8,128)} %bitcast.11), calls=%async_computation.4 | async-start | bytes 524288 | tf_op jit(solution)/shard_map/all_to_all | solution.py:30
  236.4 6.2 %collective-permute-start.14 = (f32[64,1024]{1,0:T(8,128)S(1)}, f32[64,1024]{1,0:T(8,128)S(1)}, u32[]{:S(2)}, u32[]{:S(2)}) collective-permute-start(f32[64,1024]{1,0:T(8,128)S(1)} %bitcast.55), channel_id=1, source_target_pairs={{0,8},{8,0},{16,24},{24,16},{32,40},{40,32},{48,56},{56,48},{64,72... | collective-permute-start | bytes 786440 | tf_op jit(solution)/shard_map/ppermute | solution.py:38
  (4 other events, 6.4 us)

commit v6 on v5

--- a/solution.py
+++ b/solution.py
@@ -79,7 +79,7 @@
     added = jnp.where(even, 0.0, chip_offset)
     for _ in range(CHIPS - 2):
         state = product(permuted(state, NEXT_CHIP), chip_map) * factor + added
-    state = permuted(state, NEXT_CHIP)
+    state, border_left = lax.optimization_barrier((permuted(state, NEXT_CHIP), border_left))
     across = permuted(state, CORE_SWAP)
     window = jnp.concatenate([jnp.where(even, state, across), jnp.where(even, across, state)], axis=0)
     window = product(window, jnp.where(even, block_map, chip_map))

time: 244 us -> 239 us (0.980)
  blocking collectives: 36.4 us -> 18.1 us
  waiting for transfers between devices: 67.2 us -> 79.7 us
    ppermute x15, waiting for transfers between devices: 16.8 us -> 37 us  [permuted(): return lax.ppermute(value, 'blk', pairs)]
    all_to_all x2 -> x1, blocking collectives: 36.4 us -> 18.1 us  [exchanged(): return lax.all_to_all(pieces, axis, 0, 0, axis_index_groups=groups)]
    all_to_all x4 -> x5, waiting for transfers between devices: 50.4 us -> 42.7 us  [exchanged(): return lax.all_to_all(pieces, axis, 0, 0, axis_index_groups=groups)]
    ppermute x15, starting transfers between devices: 55.4 us -> 52.8 us  [permuted(): return lax.ppermute(value, 'blk', pairs)]
    all_to_all x4 -> x5, starting transfers between devices: 50.9 us -> 53 us  [exchanged(): return lax.all_to_all(pieces, axis, 0, 0, axis_index_groups=groups)]
  transfers between devices with their start and end apart: 19 -> 20, of which waited for: 13 -> 13; matrix products, arithmetic and copies ran while one was open for 6% -> 7% of each run, Pallas kernels for 0% -> 0%
where the time goes in v6:
time: 239 us; the launch traced here: 238 us
  starting transfers between devices  106 us (44%)
  waiting for transfers between devices  79.7 us (33%)
  matrix products  20.4 us (9%)
  blocking collectives  18.1 us (8%)
  local copies, waits for them, and re-layouts  7.65 us (3%)
  other arithmetic  5.45 us (2%)
    all_to_all x5, starting transfers between devices, exchanged(): return lax.all_to_all(pieces, axis, 0, 0, axis_index_groups=groups)  53 us
    ppermute x15, starting transfers between devices, permuted(): return lax.ppermute(value, 'blk', pairs)  52.8 us
    all_to_all x5, waiting for transfers between devices, exchanged(): return lax.all_to_all(pieces, axis, 0, 0, axis_index_groups=groups)  42.7 us
    ppermute x15, waiting for transfers between devices, permuted(): return lax.ppermute(value, 'blk', pairs)  37 us
    all_to_all x1, blocking collectives, exchanged(): return lax.all_to_all(pieces, axis, 0, 0, axis_index_groups=groups)  18.1 us
    dot_general x12, matrix products, product(): lax.dot_general(left, right, (((1,), (0,)), ((), ())), precision=lax.Prec...  13.2 us
    dot_general x3, matrix products, product_transposed(): lax.dot_general(left, right, (((1,), (1,)), ((), ())), precision=lax.Prec...  5.27 us
  transfers between devices with their start and end apart: 20, of which 13 were waited for; matrix products, arithmetic and copies ran while one was open for 7% of the time, Pallas kernels for 0%

profile of v6, /device:TPU:1, one launch (start us, length us, event | category | flops | bytes accessed | tf_op | source)
XLA Modules:
  0.0 238.1 jit_solution(2106786490261253011)
XLA Ops:
  3.3 5.9 %all-to-all-start = ((f32[8,128,512]{2,1,0:T(8,128)}), f32[8,128,512]{2,1,0:T(8,128)S(1)}, u32[]{:S(2)}, u32[]{:S(2)}) async-start(f32[8,128,512]{2,1,0:T(8,128)} %broadcast_in_dim.15), calls=%async_computation | async-start | bytes 4194304 | tf_op jit(solution)/shard_map/all_to_all | solution.py:30
  9.2 25.1 %all-to-all-done = f32[8,128,512]{2,1,0:T(8,128)S(1)} async-done(((f32[8,128,512]{2,1,0:T(8,128)}), f32[8,128,512]{2,1,0:T(8,128)S(1)}, u32[]{:S(2)}, u32[]{:S(2)}) %all-to-all-start) | async-done | bytes 2097184 | tf_op jit(solution)/shard_map/all_to_all | solution.py:30
  37.9 3.9 %collective-permute-start = (f32[576,512]{1,0:T(8,128)S(1)}, f32[576,512]{1,0:T(8,128)S(1)}, u32[]{:S(2)}, u32[]{:S(2)}) collective-permute-start(f32[576,512]{1,0:T(8,128)S(1)} %pad_maximum_fusion), channel_id=1, source_target_pairs={{0,8},{8,0},{16,24},{24,16},{32,40},{40,32},{48,56},{56,48},{64,72... | collective-permute-start | bytes 3538952 | tf_op jit(solution)/shard_map/ppermute | solution.py:38
  45.7 4.3 %all-to-all-start.1 = ((f32[8,256,256]{2,1,0:T(8,128)}), f32[8,256,256]{2,1,0:T(8,128)}, u32[]{:S(2)}, u32[]{:S(2)}) async-start(f32[8,256,256]{2,1,0:T(8,128)} %broadcast_in_dim.16), calls=%async_computation.1 | async-start | bytes 4194304 | tf_op jit(solution)/shard_map/all_to_all | solution.py:30
  50.4 2.1 fusion
  52.5 4.2 %collective-permute-start.1 = (f32[64,512]{1,0:T(8,128)S(1)}, f32[64,512]{1,0:T(8,128)S(1)}, u32[]{:S(2)}, u32[]{:S(2)}) collective-permute-start(f32[64,512]{1,0:T(8,128)S(1)} %get-tuple-element.14), channel_id=1, source_target_pairs={{0,16},{8,24},{16,32},{24,40},{32,48},{40,56},{48,64},{56,72},{64,... | collective-permute-start | bytes 393224 | tf_op jit(solution)/shard_map/ppermute | solution.py:38
  56.8 25.8 %collective-permute-done.1 = f32[64,512]{1,0:T(8,128)S(1)} collective-permute-done((f32[64,512]{1,0:T(8,128)S(1)}, f32[64,512]{1,0:T(8,128)S(1)}, u32[]{:S(2)}, u32[]{:S(2)}) %collective-permute-start.1) | collective-permute-done | bytes 131104 | tf_op jit(solution)/shard_map/ppermute | solution.py:38
  83.0 6.5 %collective-permute-start.2 = (f32[64,512]{1,0:T(8,128)S(1)}, f32[64,512]{1,0:T(8,128)S(1)}, u32[]{:S(2)}, u32[]{:S(2)}) collective-permute-start(f32[64,512]{1,0:T(8,128)S(1)} %fusion.5), channel_id=1, source_target_pairs={{0,16},{8,24},{16,32},{24,40},{32,48},{40,56},{48,64},{56,72},{64,... | collective-permute-start | bytes 393224 | tf_op jit(solution)/shard_map/ppermute | solution.py:38
  91.9 5.4 %collective-permute-start.3 = (f32[64,512]{1,0:T(8,128)S(1)}, f32[64,512]{1,0:T(8,128)S(1)}, u32[]{:S(2)}, u32[]{:S(2)}) collective-permute-start(f32[64,512]{1,0:T(8,128)S(1)} %fusion.6), channel_id=1, source_target_pairs={{0,16},{8,24},{16,32},{24,40},{32,48},{40,56},{48,64},{56,72},{64,... | collective-permute-start | bytes 393224 | tf_op jit(solution)/shard_map/ppermute | solution.py:38
  99.2 4.5 %collective-permute-start.4 = (f32[64,512]{1,0:T(8,128)S(1)}, f32[64,512]{1,0:T(8,128)S(1)}, u32[]{:S(2)}, u32[]{:S(2)}) collective-permute-start(f32[64,512]{1,0:T(8,128)S(1)} %collective-permute-done.3), channel_id=1, source_target_pairs={{0,8},{8,0},{16,24},{24,16},{32,40},{40,32},{48,56},{56,48},{64,72... | collective-permute-start | bytes 393224 | tf_op jit(solution)/shard_map/ppermute | solution.py:38
  106.8 4.3 %all-to-all-start.2 = ((f32[8,64,512]{2,1,0:T(8,128)}), f32[8,64,512]{2,1,0:T(8,128)S(1)}, u32[]{:S(2)}, u32[]{:S(2)}) async-start(f32[8,64,512]{2,1,0:T(8,128)} %broadcast_in_dim.20), calls=%async_computation.2 | async-start | bytes 2097152 | tf_op jit(solution)/shard_map/all_to_all | solution.py:30
  111.1 10.6 %collective-permute-start.5 = (f32[64,512]{1,0:T(8,128)S(1)}, f32[64,512]{1,0:T(8,128)S(1)}, u32[]{:S(2)}, u32[]{:S(2)}) collective-permute-start(f32[64,512]{1,0:T(8,128)S(1)} %get-tuple-element.23), channel_id=1, source_target_pairs={{8,72},{24,88},{40,104},{56,120},{9,73},{25,89},{41,105},{57,121},... | collective-permute-start | bytes 393224 | tf_op jit(solution)/shard_map/ppermute | solution.py:38
  126.1 4.3 %all-to-all-start.3 = ((f32[8,256,256]{2,1,0:T(8,128)}), f32[8,256,256]{2,1,0:T(8,128)S(1)}, u32[]{:S(2)}, u32[]{:S(2)}) async-start(f32[8,256,256]{2,1,0:T(8,128)} %broadcast_in_dim.18), calls=%async_computation.3 | async-start | bytes 4194304 | tf_op jit(solution)/shard_map/all_to_all | solution.py:30
  140.6 2.0 fusion.11
  143.3 2.0 fusion.12
  147.6 2.7 %collective-permute-start.12 = (f32[64,512]{1,0:T(8,128)S(1)}, f32[64,512]{1,0:T(8,128)}, u32[]{:S(2)}, u32[]{:S(2)}) collective-permute-start(f32[64,512]{1,0:T(8,128)S(1)} %broadcast_select_fusion.7), channel_id=1, source_target_pairs={{8,0},{24,16},{40,32},{56,48},{72,64},{88,80},{104,96},{120,112},{... | collective-permute-start | bytes 393224 | tf_op jit(solution)/shard_map/ppermute | solution.py:38
  151.9 4.7 %all-to-all-done.3 = f32[8,256,256]{2,1,0:T(8,128)S(1)} async-done(((f32[8,256,256]{2,1,0:T(8,128)}), f32[8,256,256]{2,1,0:T(8,128)S(1)}, u32[]{:S(2)}, u32[]{:S(2)}) %all-to-all-start.3) | async-done | bytes 2097184 | tf_op jit(solution)/shard_map/all_to_all | solution.py:30
  156.6 2.0 fusion.25
  158.6 2.7 %convolution_add_fusion = f32[64,2048]{1,0:T(8,128)S(1)} fusion(f32[64,2048]{1,0:T(8,128)S(1)} %fusion.25, f32[2048,256]{1,0:T(8,128)} %bitcast.7, f32[64,512]{1,0:T(8,128)S(1)} %copy-done.7), kind=kOutput, calls=%fused_computation | convolution fusion | flops 201457664 | bytes 3211264 | tf_op jit(solution)/shard_map/dot_general | solution.py:26
  161.3 2.6 %collective-permute-start.13 = (f32[64,1024]{1,0:T(8,128)S(1)}, f32[64,1024]{1,0:T(8,128)S(1)}, u32[]{:S(2)}, u32[]{:S(2)}) collective-permute-start(f32[64,1024]{1,0:T(8,128)S(1)} %constant_dynamic-slice_fusion), channel_id=1, source_target_pairs={{0,8},{8,0},{16,24},{24,16},{32,40},{40,32},{48,56},{56,48},{64,72... | collective-permute-start | bytes 786440 | tf_op jit(solution)/shard_map/ppermute | solution.py:38
  165.8 34.2 %all-to-all-start.4 = ((f32[32,8,256]{2,1,0:T(8,128)}), f32[32,8,256]{2,1,0:T(8,128)S(1)}, u32[]{:S(2)}, u32[]{:S(2)}) async-start(f32[32,8,256]{2,1,0:T(8,128)} %bitcast.11), calls=%async_computation.4 | async-start | bytes 524288 | tf_op jit(solution)/shard_map/all_to_all | solution.py:30
  200.1 12.0 %all-to-all-done.4 = f32[32,8,256]{2,1,0:T(8,128)S(1)} async-done(((f32[32,8,256]{2,1,0:T(8,128)}), f32[32,8,256]{2,1,0:T(8,128)S(1)}, u32[]{:S(2)}, u32[]{:S(2)}) %all-to-all-start.4) | async-done | bytes 262176 | tf_op jit(solution)/shard_map/all_to_all | solution.py:30
  212.8 18.1 %all_to_all.30 = f32[32,8,256]{2,1,0:T(8,128)S(1)} all-to-all(f32[32,8,256]{2,1,0:T(8,128)S(1)} %broadcast_in_dim.21), channel_id=1, replica_groups={{0,16,32,48,64,80,96,112,128,144,160,176,192,208,224,240,256,272,288,30..., dimensions={0} | all-to-all | bytes 524288 | tf_op jit(solution)/shard_map/all_to_all | solution.py:30
  231.0 5.1 %collective-permute-start.14 = (f32[64,1024]{1,0:T(8,128)S(1)}, f32[64,1024]{1,0:T(8,128)S(1)}, u32[]{:S(2)}, u32[]{:S(2)}) collective-permute-start(f32[64,1024]{1,0:T(8,128)S(1)} %bitcast.55), channel_id=1, source_target_pairs={{0,8},{8,0},{16,24},{24,16},{32,40},{40,32},{48,56},{56,48},{64,72... | collective-permute-start | bytes 786440 | tf_op jit(solution)/shard_map/ppermute | solution.py:38
  (74 shorter events, 42.0 us)
Async XLA Ops:
  0.6 35.8 %copy-start = (f32[64,512]{1,0:T(8,128)S(1)}, f32[64,512]{1,0:T(8,128)}, u32[]{:S(2)}) copy-start(f32[64,512]{1,0:T(8,128)} %param.8) | copy-start | bytes 393220
  3.3 31.0 %all-to-all-start = ((f32[8,128,512]{2,1,0:T(8,128)}), f32[8,128,512]{2,1,0:T(8,128)S(1)}, u32[]{:S(2)}, u32[]{:S(2)}) async-start(f32[8,128,512]{2,1,0:T(8,128)} %broadcast_in_dim.15), calls=%async_computation | async-start | bytes 4194304 | tf_op jit(solution)/shard_map/all_to_all | solution.py:30
  37.8 12.3 %copy-start.1 = (f32[64,512]{1,0:T(8,128)}, f32[64,512]{1,0:T(8,128)S(1)}, u32[]{:S(2)}) copy-start(f32[64,512]{1,0:T(8,128)S(1)} %fusion.4) | copy-start | bytes 393220
  37.9 6.4 %collective-permute-start = (f32[576,512]{1,0:T(8,128)S(1)}, f32[576,512]{1,0:T(8,128)S(1)}, u32[]{:S(2)}, u32[]{:S(2)}) collective-permute-start(f32[576,512]{1,0:T(8,128)S(1)} %pad_maximum_fusion), channel_id=1, source_target_pairs={{0,8},{8,0},{16,24},{24,16},{32,40},{40,32},{48,56},{56,48},{64,72... | collective-permute-start | bytes 3538952 | tf_op jit(solution)/shard_map/ppermute | solution.py:38
  45.7 53.5 %all-to-all-start.1 = ((f32[8,256,256]{2,1,0:T(8,128)}), f32[8,256,256]{2,1,0:T(8,128)}, u32[]{:S(2)}, u32[]{:S(2)}) async-start(f32[8,256,256]{2,1,0:T(8,128)} %broadcast_in_dim.16), calls=%async_computation.1 | async-start | bytes 4194304 | tf_op jit(solution)/shard_map/all_to_all | solution.py:30
  52.5 30.0 %collective-permute-start.1 = (f32[64,512]{1,0:T(8,128)S(1)}, f32[64,512]{1,0:T(8,128)S(1)}, u32[]{:S(2)}, u32[]{:S(2)}) collective-permute-start(f32[64,512]{1,0:T(8,128)S(1)} %get-tuple-element.14), channel_id=1, source_target_pairs={{0,16},{8,24},{16,32},{24,40},{32,48},{40,56},{48,64},{56,72},{64,... | collective-permute-start | bytes 393224 | tf_op jit(solution)/shard_map/ppermute | solution.py:38
  83.0 8.4 %collective-permute-start.2 = (f32[64,512]{1,0:T(8,128)S(1)}, f32[64,512]{1,0:T(8,128)S(1)}, u32[]{:S(2)}, u32[]{:S(2)}) collective-permute-start(f32[64,512]{1,0:T(8,128)S(1)} %fusion.5), channel_id=1, source_target_pairs={{0,16},{8,24},{16,32},{24,40},{32,48},{40,56},{48,64},{56,72},{64,... | collective-permute-start | bytes 393224 | tf_op jit(solution)/shard_map/ppermute | solution.py:38
  91.9 7.4 %collective-permute-start.3 = (f32[64,512]{1,0:T(8,128)S(1)}, f32[64,512]{1,0:T(8,128)S(1)}, u32[]{:S(2)}, u32[]{:S(2)}) collective-permute-start(f32[64,512]{1,0:T(8,128)S(1)} %fusion.6), channel_id=1, source_target_pairs={{0,16},{8,24},{16,32},{24,40},{32,48},{40,56},{48,64},{56,72},{64,... | collective-permute-start | bytes 393224 | tf_op jit(solution)/shard_map/ppermute | solution.py:38
  99.2 5.5 %collective-permute-start.4 = (f32[64,512]{1,0:T(8,128)S(1)}, f32[64,512]{1,0:T(8,128)S(1)}, u32[]{:S(2)}, u32[]{:S(2)}) collective-permute-start(f32[64,512]{1,0:T(8,128)S(1)} %collective-permute-done.3), channel_id=1, source_target_pairs={{0,8},{8,0},{16,24},{24,16},{32,40},{40,32},{48,56},{56,48},{64,72... | collective-permute-start | bytes 393224 | tf_op jit(solution)/shard_map/ppermute | solution.py:38
  106.8 16.8 %copy-start.4 = (f32[256,256]{1,0:T(8,128)S(1)}, f32[256,256]{1,0:T(8,128)}, u32[]{:S(2)}) copy-start(f32[256,256]{1,0:T(8,128)} %get-tuple-element.20) | copy-start | bytes 786436
  106.8 19.2 %all-to-all-start.2 = ((f32[8,64,512]{2,1,0:T(8,128)}), f32[8,64,512]{2,1,0:T(8,128)S(1)}, u32[]{:S(2)}, u32[]{:S(2)}) async-start(f32[8,64,512]{2,1,0:T(8,128)} %broadcast_in_dim.20), calls=%async_computation.2 | async-start | bytes 2097152 | tf_op jit(solution)/shard_map/all_to_all | solution.py:30
  111.1 12.6 %collective-permute-start.5 = (f32[64,512]{1,0:T(8,128)S(1)}, f32[64,512]{1,0:T(8,128)S(1)}, u32[]{:S(2)}, u32[]{:S(2)}) collective-permute-start(f32[64,512]{1,0:T(8,128)S(1)} %get-tuple-element.23), channel_id=1, source_target_pairs={{8,72},{24,88},{40,104},{56,120},{9,73},{25,89},{41,105},{57,121},... | collective-permute-start | bytes 393224 | tf_op jit(solution)/shard_map/ppermute | solution.py:38
  123.7 9.1 %copy-start.3 = (f32[64,512]{1,0:T(8,128)}, f32[64,512]{1,0:T(8,128)S(1)}, u32[]{:S(2)}) copy-start(f32[64,512]{1,0:T(8,128)S(1)} %collective-permute-done.5) | copy-start | bytes 393220
  126.1 30.5 %all-to-all-start.3 = ((f32[8,256,256]{2,1,0:T(8,128)}), f32[8,256,256]{2,1,0:T(8,128)S(1)}, u32[]{:S(2)}, u32[]{:S(2)}) async-start(f32[8,256,256]{2,1,0:T(8,128)} %broadcast_in_dim.18), calls=%async_computation.3 | async-start | bytes 4194304 | tf_op jit(solution)/shard_map/all_to_all | solution.py:30
  131.4 1.3 collective-permute-start.6
  133.8 1.3 collective-permute-start.7
  136.2 1.3 collective-permute-start.8
  138.6 1.3 collective-permute-start.9
  142.6 0.7 collective-permute-start.10
  145.3 1.3 collective-permute-start.11
  147.6 3.2 %collective-permute-start.12 = (f32[64,512]{1,0:T(8,128)S(1)}, f32[64,512]{1,0:T(8,128)}, u32[]{:S(2)}, u32[]{:S(2)}) collective-permute-start(f32[64,512]{1,0:T(8,128)S(1)} %broadcast_select_fusion.7), channel_id=1, source_target_pairs={{8,0},{24,16},{40,32},{56,48},{72,64},{88,80},{104,96},{120,112},{... | collective-permute-start | bytes 393224 | tf_op jit(solution)/shard_map/ppermute | solution.py:38
  161.3 3.8 %collective-permute-start.13 = (f32[64,1024]{1,0:T(8,128)S(1)}, f32[64,1024]{1,0:T(8,128)S(1)}, u32[]{:S(2)}, u32[]{:S(2)}) collective-permute-start(f32[64,1024]{1,0:T(8,128)S(1)} %constant_dynamic-slice_fusion), channel_id=1, source_target_pairs={{0,8},{8,0},{16,24},{24,16},{32,40},{40,32},{48,56},{56,48},{64,72... | collective-permute-start | bytes 786440 | tf_op jit(solution)/shard_map/ppermute | solution.py:38
  165.8 46.3 %all-to-all-start.4 = ((f32[32,8,256]{2,1,0:T(8,128)}), f32[32,8,256]{2,1,0:T(8,128)S(1)}, u32[]{:S(2)}, u32[]{:S(2)}) async-start(f32[32,8,256]{2,1,0:T(8,128)} %bitcast.11), calls=%async_computation.4 | async-start | bytes 524288 | tf_op jit(solution)/shard_map/all_to_all | solution.py:30
  231.0 6.2 %collective-permute-start.14 = (f32[64,1024]{1,0:T(8,128)S(1)}, f32[64,1024]{1,0:T(8,128)S(1)}, u32[]{:S(2)}, u32[]{:S(2)}) collective-permute-start(f32[64,1024]{1,0:T(8,128)S(1)} %bitcast.55), channel_id=1, source_target_pairs={{0,8},{8,0},{16,24},{24,16},{32,40},{40,32},{48,56},{56,48},{64,72... | collective-permute-start | bytes 786440 | tf_op jit(solution)/shard_map/ppermute | solution.py:38
  (5 other events, 11.2 us)

commit v7 on v4

--- a/solution.py
+++ b/solution.py
@@ -16,6 +16,10 @@
 TO_EVEN = [(p + 1, p) for p in range(0, BLOCKS, CORES)]
 NEXT_CHIP = [(p, p + CORES) for p in range(BLOCKS - CORES)]
 CORE_GROUPS = [[device(z, c, k) for z in range(PLANES) for c in range(CHIPS)] for k in range(CORES)]
+
+ROW = 4
+ROW_GROUPS = [[0, 1, 2, 3], [4, 5, 6, 7]]
+ROW_SWAP = [(j, j ^ ROW) for j in range(2 * ROW)]
 
 
 def product(left, right):
@@ -60,6 +64,10 @@
 
     block = jnp.concatenate([block_map, offset], axis=0)
     other = permuted(block, CORE_SWAP)
+    copies = jnp.broadcast_to(border_factor[None], (ROW,) + border_factor.shape)
+    other, copies = lax.optimization_barrier((other, copies))
+    border_near = exchanged(copies, "rhs", ROW_GROUPS)
+
     first, second = jnp.where(even, block, other), jnp.where(even, other, block)
     pair = product(first, second[:size])
     chip_map = pair[:size]
@@ -70,7 +78,7 @@
     added = jnp.where(even, 0.0, chip_offset)
     for _ in range(CHIPS - 2):
         state = product(permuted(state, NEXT_CHIP), chip_map) * factor + added
-    state = permuted(state, NEXT_CHIP)
+    state, border_near = lax.optimization_barrier((permuted(state, NEXT_CHIP), border_near))
     across = permuted(state, CORE_SWAP)
     window = jnp.concatenate([jnp.where(even, state, across), jnp.where(even, across, state)], axis=0)
     window = product(window, jnp.where(even, block_map, chip_map))
@@ -79,9 +87,8 @@
 
     arrived = permuted(own_offset, [(device(0, c, 1), device(1, c, 1)) for c in range(CHIPS)])
     own_map = to_all(window[:rows], "rhs", members).reshape(size, size)
-    copies = jnp.broadcast_to(border_factor[None], (members,) + border_factor.shape)
-    arrived, copies = lax.optimization_barrier((arrived, copies))
-    border_block = exchanged(copies, "rhs")
+    own_map, border_near = lax.optimization_barrier((own_map, border_near))
+    border_far = lax.ppermute(border_near, "rhs", ROW_SWAP)
     start = jnp.where(plane == 1, arrived, 0.0)
     for step in range(2, PLANES):
         end = product(start, own_map) * scale + own_offset
@@ -91,13 +98,12 @@
     solved = product(start, own_map) * scale + own_offset
 
     border = border_rhs.shape[1]
-    border_block = border_block.reshape(border, size)
-    partial = product_transposed(solved, border_block)
     per_core, per_chip = border // CORES, border // CORES // CHIPS
     per_plane = rows // PLANES
-    kept = lax.dynamic_slice_in_dim(partial, core * per_core, per_core, 1)
-    passed = lax.dynamic_slice_in_dim(partial, (1 - core) * per_core, per_core, 1)
-    total = kept + permuted(passed, CORE_SWAP)
+    near = product_transposed(solved, border_near.reshape(per_core, size))
+    far = product_transposed(solved, border_far.reshape(per_core, size))
+    mine = core == member // ROW
+    total = jnp.where(mine, near, far) + permuted(jnp.where(mine, far, near), CORE_SWAP)
     pieces = jnp.transpose(total.reshape(PLANES, per_plane, CHIPS, per_chip), (0, 2, 1, 3))
     pieces = pieces.reshape(PLANES * CHIPS, per_plane, per_chip)
     total = jnp.sum(exchanged(pieces, "blk", CORE_GROUPS), axis=0)

time: 224 us -> 229 us (1.022)
  waiting for transfers between devices: 94.2 us -> 83.7 us
  starting transfers between devices: 84.6 us -> 94.2 us
  matrix products: 13.5 us -> 18.4 us
    all_to_all x4, waiting for transfers between devices: 76.4 us -> 41.8 us  [exchanged(): return lax.all_to_all(pieces, axis, 0, 0, axis_index_groups=groups)]
    ppermute x0 -> x1, waiting for transfers between devices: none -> 26.3 us  [body(): border_far = lax.ppermute(border_near, 'rhs', ROW_SWAP)]
    dot_general x12, matrix products: 6.75 us -> 12.1 us  [product(): lax.dot_general(left, right, (((1,), (0,)), ((), ())), precision=lax.Prec...]
    ppermute x15, starting transfers between devices: 49.2 us -> 53.8 us  [permuted(): return lax.ppermute(value, 'blk', pairs)]
    ppermute x0 -> x1, starting transfers between devices: none -> 3.08 us  [body(): border_far = lax.ppermute(border_near, 'rhs', ROW_SWAP)]
    ppermute x15, waiting for transfers between devices: 17.8 us -> 15.5 us  [permuted(): return lax.ppermute(value, 'blk', pairs)]
    dot_general x2 -> x3, matrix products: 4.82 us -> 4.41 us  [product_transposed(): lax.dot_general(left, right, (((1,), (1,)), ((), ())), precision=lax.Prec...]
  transfers between devices with their start and end apart: 19 -> 20, of which waited for: 12 -> 12; matrix products, arithmetic and copies ran while one was open for 3% -> 6% of each run, Pallas kernels for 0% -> 0%
where the time goes in v7:
time: 229 us; the launch traced here: 228 us
  starting transfers between devices  94.2 us (41%)
  waiting for transfers between devices  83.7 us (37%)
  matrix products  18.4 us (8%)
  blocking collectives  18.2 us (8%)
  other arithmetic  7.15 us (3%)
  local copies, waits for them, and re-layouts  5.4 us (2%)
    ppermute x15, starting transfers between devices, permuted(): return lax.ppermute(value, 'blk', pairs)  53.8 us
    all_to_all x4, waiting for transfers between devices, exchanged(): return lax.all_to_all(pieces, axis, 0, 0, axis_index_groups=groups)  41.8 us
    all_to_all x4, starting transfers between devices, exchanged(): return lax.all_to_all(pieces, axis, 0, 0, axis_index_groups=groups)  37.4 us
    ppermute x1, waiting for transfers between devices, body(): border_far = lax.ppermute(border_near, 'rhs', ROW_SWAP)  26.3 us
    all_to_all x1, blocking collectives, exchanged(): return lax.all_to_all(pieces, axis, 0, 0, axis_index_groups=groups)  18.2 us
    ppermute x15, waiting for transfers between devices, permuted(): return lax.ppermute(value, 'blk', pairs)  15.5 us
    dot_general x12, matrix products, product(): lax.dot_general(left, right, (((1,), (0,)), ((), ())), precision=lax.Prec...  12.1 us
  transfers between devices with their start and end apart: 20, of which 12 were waited for; matrix products, arithmetic and copies ran while one was open for 6% of the time, Pallas kernels for 0%

profile of v7, /device:TPU:1, one launch (start us, length us, event | category | flops | bytes accessed | tf_op | source)
XLA Modules:
  0.0 228.1 jit_solution(12509515831386475632)
XLA Ops:
  3.3 5.9 %all-to-all-start = ((f32[8,128,512]{2,1,0:T(8,128)}), f32[8,128,512]{2,1,0:T(8,128)S(1)}, u32[]{:S(2)}, u32[]{:S(2)}) async-start(f32[8,128,512]{2,1,0:T(8,128)} %broadcast_in_dim.13), calls=%async_computation | async-start | bytes 4194304 | tf_op jit(solution)/shard_map/all_to_all | solution.py:34
  9.2 25.1 %all-to-all-done = f32[8,128,512]{2,1,0:T(8,128)S(1)} async-done(((f32[8,128,512]{2,1,0:T(8,128)}), f32[8,128,512]{2,1,0:T(8,128)S(1)}, u32[]{:S(2)}, u32[]{:S(2)}) %all-to-all-start) | async-done | bytes 2097184 | tf_op jit(solution)/shard_map/all_to_all | solution.py:34
  38.9 3.7 %collective-permute-start = (f32[576,512]{1,0:T(8,128)}, f32[576,512]{1,0:T(8,128)S(1)}, u32[]{:S(2)}, u32[]{:S(2)}) collective-permute-start(f32[576,512]{1,0:T(8,128)} %pad_maximum_fusion), channel_id=1, source_target_pairs={{0,8},{8,0},{16,24},{24,16},{32,40},{40,32},{48,56},{56,48},{64,72... | collective-permute-start | bytes 3538952 | tf_op jit(solution)/shard_map/ppermute | solution.py:42
  42.7 2.6 %collective-permute-done = f32[576,512]{1,0:T(8,128)S(1)} collective-permute-done((f32[576,512]{1,0:T(8,128)}, f32[576,512]{1,0:T(8,128)S(1)}, u32[]{:S(2)}, u32[]{:S(2)}) %collective-permute-start) | collective-permute-done | bytes 1179680 | tf_op jit(solution)/shard_map/ppermute | solution.py:42
  46.9 4.4 %all-to-all-start.1 = ((f32[4,256,512]{2,1,0:T(8,128)}), f32[4,256,512]{2,1,0:T(8,128)}, u32[]{:S(2)}, u32[]{:S(2)}) async-start(f32[4,256,512]{2,1,0:T(8,128)} %broadcast_in_dim.14), calls=%async_computation.1 | async-start | bytes 4194304 | tf_op jit(solution)/shard_map/all_to_all | solution.py:34
  53.8 4.2 %collective-permute-start.1 = (f32[64,512]{1,0:T(8,128)S(1)}, f32[64,512]{1,0:T(8,128)S(1)}, u32[]{:S(2)}, u32[]{:S(2)}) collective-permute-start(f32[64,512]{1,0:T(8,128)S(1)} %get-tuple-element.14), channel_id=1, source_target_pairs={{0,16},{8,24},{16,32},{24,40},{32,48},{40,56},{48,64},{56,72},{64,... | collective-permute-start | bytes 393224 | tf_op jit(solution)/shard_map/ppermute | solution.py:42
  58.0 2.5 %collective-permute-done.1 = f32[64,512]{1,0:T(8,128)S(1)} collective-permute-done((f32[64,512]{1,0:T(8,128)S(1)}, f32[64,512]{1,0:T(8,128)S(1)}, u32[]{:S(2)}, u32[]{:S(2)}) %collective-permute-start.1) | collective-permute-done | bytes 131104 | tf_op jit(solution)/shard_map/ppermute | solution.py:42
  61.0 5.1 %collective-permute-start.2 = (f32[64,512]{1,0:T(8,128)S(1)}, f32[64,512]{1,0:T(8,128)S(1)}, u32[]{:S(2)}, u32[]{:S(2)}) collective-permute-start(f32[64,512]{1,0:T(8,128)S(1)} %fusion.5), channel_id=1, source_target_pairs={{0,16},{8,24},{16,32},{24,40},{32,48},{40,56},{48,64},{56,72},{64,... | collective-permute-start | bytes 393224 | tf_op jit(solution)/shard_map/ppermute | solution.py:42
  66.1 2.2 collective-permute-done.2
  68.7 5.5 %collective-permute-start.3 = (f32[64,512]{1,0:T(8,128)S(1)}, f32[64,512]{1,0:T(8,128)S(1)}, u32[]{:S(2)}, u32[]{:S(2)}) collective-permute-start(f32[64,512]{1,0:T(8,128)S(1)} %fusion.6), channel_id=1, source_target_pairs={{0,16},{8,24},{16,32},{24,40},{32,48},{40,56},{48,64},{56,72},{64,... | collective-permute-start | bytes 393224 | tf_op jit(solution)/shard_map/ppermute | solution.py:42
  74.1 4.2 %collective-permute-done.3 = f32[64,512]{1,0:T(8,128)S(1)} collective-permute-done((f32[64,512]{1,0:T(8,128)S(1)}, f32[64,512]{1,0:T(8,128)S(1)}, u32[]{:S(2)}, u32[]{:S(2)}) %collective-permute-start.3) | collective-permute-done | bytes 131104 | tf_op jit(solution)/shard_map/ppermute | solution.py:42
  78.4 6.9 %collective-permute-start.4 = (f32[64,512]{1,0:T(8,128)S(1)}, f32[64,512]{1,0:T(8,128)S(1)}, u32[]{:S(2)}, u32[]{:S(2)}) collective-permute-start(f32[64,512]{1,0:T(8,128)S(1)} %collective-permute-done.3), channel_id=1, source_target_pairs={{0,8},{8,0},{16,24},{24,16},{32,40},{40,32},{48,56},{56,48},{64,72... | collective-permute-start | bytes 393224 | tf_op jit(solution)/shard_map/ppermute | solution.py:42
  88.3 6.3 %all-to-all-start.2 = ((f32[8,64,512]{2,1,0:T(8,128)}), f32[8,64,512]{2,1,0:T(8,128)S(1)}, u32[]{:S(2)}, u32[]{:S(2)}) async-start(f32[8,64,512]{2,1,0:T(8,128)} %broadcast_in_dim.17), calls=%async_computation.2 | async-start | bytes 2097152 | tf_op jit(solution)/shard_map/all_to_all | solution.py:34
  94.6 10.2 %collective-permute-start.5 = (f32[64,512]{1,0:T(8,128)S(1)}, f32[64,512]{1,0:T(8,128)S(1)}, u32[]{:S(2)}, u32[]{:S(2)}) collective-permute-start(f32[64,512]{1,0:T(8,128)S(1)} %get-tuple-element.21), channel_id=1, source_target_pairs={{8,72},{24,88},{40,104},{56,120},{9,73},{25,89},{41,105},{57,121},... | collective-permute-start | bytes 393224 | tf_op jit(solution)/shard_map/ppermute | solution.py:42
  104.8 4.7 %all-to-all-done.2 = f32[8,64,512]{2,1,0:T(8,128)S(1)} async-done(((f32[8,64,512]{2,1,0:T(8,128)}), f32[8,64,512]{2,1,0:T(8,128)S(1)}, u32[]{:S(2)}, u32[]{:S(2)}) %all-to-all-start.2) | async-done | bytes 1048608 | tf_op jit(solution)/shard_map/all_to_all | solution.py:34
  114.2 3.1 %collective-permute-start.13 = (f32[4,256,512]{2,1,0:T(8,128)}, f32[4,256,512]{2,1,0:T(8,128)S(1)}, u32[]{:S(2)}, u32[]{:S(2)}) collective-permute-start(f32[4,256,512]{2,1,0:T(8,128)} %all-to-all-done.1), channel_id=1, source_target_pairs={{0,4},{1,5},{2,6},{3,7},{4,0},{5,1},{6,2},{7,3},{8,12},{9,13},{10,... | collective-permute-start | bytes 6291464 | tf_op jit(solution)/shard_map/ppermute | solution.py:91
  128.0 3.6 %collective-permute-start.12 = (f32[64,512]{1,0:T(8,128)}, f32[64,512]{1,0:T(8,128)}, u32[]{:S(2)}, u32[]{:S(2)}) collective-permute-start(f32[64,512]{1,0:T(8,128)} %broadcast_select_fusion.8), channel_id=1, source_target_pairs={{8,0},{24,16},{40,32},{56,48},{72,64},{88,80},{104,96},{120,112},{... | collective-permute-start | bytes 393224 | tf_op jit(solution)/shard_map/ppermute | solution.py:42
  133.6 2.7 %fusion.36 = f32[64,1024]{1,0:T(8,128)S(1)} fusion(f32[64,512]{1,0:T(8,128)S(1)} %fusion.13, f32[1024,512]{1,0:T(8,128)} %bitcast.7), kind=kOutput, calls=%fused_computation.69 | convolution fusion | flops 201326592 | bytes 2490368 | tf_op jit(solution)/shard_map/dot_general | solution.py:30
  136.3 26.3 %collective-permute-done.13 = f32[4,256,512]{2,1,0:T(8,128)S(1)} collective-permute-done((f32[4,256,512]{2,1,0:T(8,128)}, f32[4,256,512]{2,1,0:T(8,128)S(1)}, u32[]{:S(2)}, u32[]{:S(2)}) %collective-permute-start.13) | collective-permute-done | bytes 2097184 | tf_op jit(solution)/shard_map/ppermute | solution.py:91
  163.8 3.6 %collective-permute-start.14 = (f32[64,1024]{1,0:T(8,128)S(1)}, f32[64,1024]{1,0:T(8,128)S(1)}, u32[]{:S(2)}, u32[]{:S(2)}) collective-permute-start(f32[64,1024]{1,0:T(8,128)S(1)} %get-tuple-element.24), channel_id=1, source_target_pairs={{0,8},{8,0},{16,24},{24,16},{32,40},{40,32},{48,56},{56,48},{64,72... | collective-permute-start | bytes 786440 | tf_op jit(solution)/shard_map/ppermute | solution.py:42
  169.3 20.8 %all-to-all-start.3 = ((f32[32,8,256]{2,1,0:T(8,128)}), f32[32,8,256]{2,1,0:T(8,128)S(1)}, u32[]{:S(2)}, u32[]{:S(2)}) async-start(f32[32,8,256]{2,1,0:T(8,128)} %bitcast.11), calls=%async_computation.3 | async-start | bytes 524288 | tf_op jit(solution)/shard_map/all_to_all | solution.py:34
  190.1 12.0 %all-to-all-done.3 = f32[32,8,256]{2,1,0:T(8,128)S(1)} async-done(((f32[32,8,256]{2,1,0:T(8,128)}), f32[32,8,256]{2,1,0:T(8,128)S(1)}, u32[]{:S(2)}, u32[]{:S(2)}) %all-to-all-start.3) | async-done | bytes 262176 | tf_op jit(solution)/shard_map/all_to_all | solution.py:34
  202.8 18.2 %all_to_all.25 = f32[32,8,256]{2,1,0:T(8,128)S(1)} all-to-all(f32[32,8,256]{2,1,0:T(8,128)S(1)} %broadcast_in_dim.18), channel_id=1, replica_groups={{0,16,32,48,64,80,96,112,128,144,160,176,192,208,224,240,256,272,288,30..., dimensions={0} | all-to-all | bytes 524288 | tf_op jit(solution)/shard_map/all_to_all | solution.py:34
  221.0 5.1 %collective-permute-start.15 = (f32[64,1024]{1,0:T(8,128)S(1)}, f32[64,1024]{1,0:T(8,128)S(1)}, u32[]{:S(2)}, u32[]{:S(2)}) collective-permute-start(f32[64,1024]{1,0:T(8,128)S(1)} %bitcast.57), channel_id=1, source_target_pairs={{0,8},{8,0},{16,24},{24,16},{32,40},{40,32},{48,56},{56,48},{64,72... | collective-permute-start | bytes 786440 | tf_op jit(solution)/shard_map/ppermute | solution.py:42
  (65 shorter events, 38.1 us)
Async XLA Ops:
  0.6 35.8 %copy-start = (f32[64,512]{1,0:T(8,128)S(1)}, f32[64,512]{1,0:T(8,128)}, u32[]{:S(2)}) copy-start(f32[64,512]{1,0:T(8,128)} %param.8) | copy-start | bytes 393220
  3.3 31.0 %all-to-all-start = ((f32[8,128,512]{2,1,0:T(8,128)}), f32[8,128,512]{2,1,0:T(8,128)S(1)}, u32[]{:S(2)}, u32[]{:S(2)}) async-start(f32[8,128,512]{2,1,0:T(8,128)} %broadcast_in_dim.13), calls=%async_computation | async-start | bytes 4194304 | tf_op jit(solution)/shard_map/all_to_all | solution.py:34
  37.8 13.6 %copy-start.1 = (f32[64,512]{1,0:T(8,128)}, f32[64,512]{1,0:T(8,128)S(1)}, u32[]{:S(2)}) copy-start(f32[64,512]{1,0:T(8,128)S(1)} %fusion.4) | copy-start | bytes 393220
  37.8 7.5 %copy-start.4 = (f32[256,512]{1,0:T(8,128)S(1)}, f32[256,512]{1,0:T(8,128)}, u32[]{:S(2)}) copy-start(f32[256,512]{1,0:T(8,128)} %param.10) | copy-start | bytes 1572868
  38.9 6.4 %collective-permute-start = (f32[576,512]{1,0:T(8,128)}, f32[576,512]{1,0:T(8,128)S(1)}, u32[]{:S(2)}, u32[]{:S(2)}) collective-permute-start(f32[576,512]{1,0:T(8,128)} %pad_maximum_fusion), channel_id=1, source_target_pairs={{0,8},{8,0},{16,24},{24,16},{32,40},{40,32},{48,56},{56,48},{64,72... | collective-permute-start | bytes 3538952 | tf_op jit(solution)/shard_map/ppermute | solution.py:42
  46.9 31.5 %all-to-all-start.1 = ((f32[4,256,512]{2,1,0:T(8,128)}), f32[4,256,512]{2,1,0:T(8,128)}, u32[]{:S(2)}, u32[]{:S(2)}) async-start(f32[4,256,512]{2,1,0:T(8,128)} %broadcast_in_dim.14), calls=%async_computation.1 | async-start | bytes 4194304 | tf_op jit(solution)/shard_map/all_to_all | solution.py:34
  53.8 6.8 %collective-permute-start.1 = (f32[64,512]{1,0:T(8,128)S(1)}, f32[64,512]{1,0:T(8,128)S(1)}, u32[]{:S(2)}, u32[]{:S(2)}) collective-permute-start(f32[64,512]{1,0:T(8,128)S(1)} %get-tuple-element.14), channel_id=1, source_target_pairs={{0,16},{8,24},{16,32},{24,40},{32,48},{40,56},{48,64},{56,72},{64,... | collective-permute-start | bytes 393224 | tf_op jit(solution)/shard_map/ppermute | solution.py:42
  61.0 7.3 %collective-permute-start.2 = (f32[64,512]{1,0:T(8,128)S(1)}, f32[64,512]{1,0:T(8,128)S(1)}, u32[]{:S(2)}, u32[]{:S(2)}) collective-permute-start(f32[64,512]{1,0:T(8,128)S(1)} %fusion.5), channel_id=1, source_target_pairs={{0,16},{8,24},{16,32},{24,40},{32,48},{40,56},{48,64},{56,72},{64,... | collective-permute-start | bytes 393224 | tf_op jit(solution)/shard_map/ppermute | solution.py:42
  68.7 9.7 %collective-permute-start.3 = (f32[64,512]{1,0:T(8,128)S(1)}, f32[64,512]{1,0:T(8,128)S(1)}, u32[]{:S(2)}, u32[]{:S(2)}) collective-permute-start(f32[64,512]{1,0:T(8,128)S(1)} %fusion.6), channel_id=1, source_target_pairs={{0,16},{8,24},{16,32},{24,40},{32,48},{40,56},{48,64},{56,72},{64,... | collective-permute-start | bytes 393224 | tf_op jit(solution)/shard_map/ppermute | solution.py:42
  78.4 7.8 %collective-permute-start.4 = (f32[64,512]{1,0:T(8,128)S(1)}, f32[64,512]{1,0:T(8,128)S(1)}, u32[]{:S(2)}, u32[]{:S(2)}) collective-permute-start(f32[64,512]{1,0:T(8,128)S(1)} %collective-permute-done.3), channel_id=1, source_target_pairs={{0,8},{8,0},{16,24},{24,16},{32,40},{40,32},{48,56},{56,48},{64,72... | collective-permute-start | bytes 393224 | tf_op jit(solution)/shard_map/ppermute | solution.py:42
  88.3 21.2 %all-to-all-start.2 = ((f32[8,64,512]{2,1,0:T(8,128)}), f32[8,64,512]{2,1,0:T(8,128)S(1)}, u32[]{:S(2)}, u32[]{:S(2)}) async-start(f32[8,64,512]{2,1,0:T(8,128)} %broadcast_in_dim.17), calls=%async_computation.2 | async-start | bytes 2097152 | tf_op jit(solution)/shard_map/all_to_all | solution.py:34
  94.6 15.0 %collective-permute-start.5 = (f32[64,512]{1,0:T(8,128)S(1)}, f32[64,512]{1,0:T(8,128)S(1)}, u32[]{:S(2)}, u32[]{:S(2)}) collective-permute-start(f32[64,512]{1,0:T(8,128)S(1)} %get-tuple-element.21), channel_id=1, source_target_pairs={{8,72},{24,88},{40,104},{56,120},{9,73},{25,89},{41,105},{57,121},... | collective-permute-start | bytes 393224 | tf_op jit(solution)/shard_map/ppermute | solution.py:42
  110.0 0.7 collective-permute-start.6
  111.1 0.7 collective-permute-start.7
  112.9 4.4 %collective-permute-start.8 = (f32[64,512]{1,0:T(8,128)}, f32[64,512]{1,0:T(8,128)}, u32[]{:S(2)}, u32[]{:S(2)}) collective-permute-start(f32[64,512]{1,0:T(8,128)} %fusion.9), channel_id=1, source_target_pairs={{200,264},{216,280},{232,296},{248,312},{201,265},{217,281},{233,2... | collective-permute-start | bytes 393224 | tf_op jit(solution)/shard_map/ppermute | solution.py:42
  114.2 48.4 %collective-permute-start.13 = (f32[4,256,512]{2,1,0:T(8,128)}, f32[4,256,512]{2,1,0:T(8,128)S(1)}, u32[]{:S(2)}, u32[]{:S(2)}) collective-permute-start(f32[4,256,512]{2,1,0:T(8,128)} %all-to-all-done.1), channel_id=1, source_target_pairs={{0,4},{1,5},{2,6},{3,7},{4,0},{5,1},{6,2},{7,3},{8,12},{9,13},{10,... | collective-permute-start | bytes 6291464 | tf_op jit(solution)/shard_map/ppermute | solution.py:91
  118.4 1.3 collective-permute-start.9
  122.4 0.7 collective-permute-start.10
  125.1 1.3 collective-permute-start.11
  128.0 4.3 %collective-permute-start.12 = (f32[64,512]{1,0:T(8,128)}, f32[64,512]{1,0:T(8,128)}, u32[]{:S(2)}, u32[]{:S(2)}) collective-permute-start(f32[64,512]{1,0:T(8,128)} %broadcast_select_fusion.8), channel_id=1, source_target_pairs={{8,0},{24,16},{40,32},{56,48},{72,64},{88,80},{104,96},{120,112},{... | collective-permute-start | bytes 393224 | tf_op jit(solution)/shard_map/ppermute | solution.py:42
  133.6 29.1 %copy-start.3 = (f32[64,512]{1,0:T(8,128)}, f32[64,512]{1,0:T(8,128)S(1)}, u32[]{:S(2)}) copy-start(f32[64,512]{1,0:T(8,128)S(1)} %fusion.13) | copy-start | bytes 393220
  163.8 4.7 %collective-permute-start.14 = (f32[64,1024]{1,0:T(8,128)S(1)}, f32[64,1024]{1,0:T(8,128)S(1)}, u32[]{:S(2)}, u32[]{:S(2)}) collective-permute-start(f32[64,1024]{1,0:T(8,128)S(1)} %get-tuple-element.24), channel_id=1, source_target_pairs={{0,8},{8,0},{16,24},{24,16},{32,40},{40,32},{48,56},{56,48},{64,72... | collective-permute-start | bytes 786440 | tf_op jit(solution)/shard_map/ppermute | solution.py:42
  169.3 32.8 %all-to-all-start.3 = ((f32[32,8,256]{2,1,0:T(8,128)}), f32[32,8,256]{2,1,0:T(8,128)S(1)}, u32[]{:S(2)}, u32[]{:S(2)}) async-start(f32[32,8,256]{2,1,0:T(8,128)} %bitcast.11), calls=%async_computation.3 | async-start | bytes 524288 | tf_op jit(solution)/shard_map/all_to_all | solution.py:34
  221.0 6.2 %collective-permute-start.15 = (f32[64,1024]{1,0:T(8,128)S(1)}, f32[64,1024]{1,0:T(8,128)S(1)}, u32[]{:S(2)}, u32[]{:S(2)}) collective-permute-start(f32[64,1024]{1,0:T(8,128)S(1)} %bitcast.57), channel_id=1, source_target_pairs={{0,8},{8,0},{16,24},{24,16},{32,40},{40,32},{48,56},{56,48},{64,72... | collective-permute-start | bytes 786440 | tf_op jit(solution)/shard_map/ppermute | solution.py:42
  (2 other events, 1.8 us)

commit v8 on v7

--- a/solution.py
+++ b/solution.py
@@ -52,8 +52,11 @@
     plane = position // (CORES * CHIPS)
     even = core == 0
 
+    border_across = lax.ppermute(border_factor, "rhs", ROW_SWAP)
+
     share = coupling.shape[1]
     gathered = to_all(jnp.concatenate([coupling[0], diag_inverse[0]], axis=0), "rhs", members)
+    gathered, border_across = lax.optimization_barrier((gathered, border_across))
     link = gathered[:, :share].reshape(size, size)
     inverse = gathered[:, share:].reshape(size, size)
 
@@ -87,12 +90,14 @@
 
     arrived = permuted(own_offset, [(device(0, c, 1), device(1, c, 1)) for c in range(CHIPS)])
     own_map = to_all(window[:rows], "rhs", members).reshape(size, size)
-    own_map, border_near = lax.optimization_barrier((own_map, border_near))
-    border_far = lax.ppermute(border_near, "rhs", ROW_SWAP)
+    own_map, copies = lax.optimization_barrier((own_map, jnp.broadcast_to(border_across[None], (ROW,) + border_across.shape)))
+    border_far = exchanged(copies, "rhs", ROW_GROUPS)
     start = jnp.where(plane == 1, arrived, 0.0)
     for step in range(2, PLANES):
         end = product(start, own_map) * scale + own_offset
         arrived = permuted(end, [(device(step - 1, c, 1), device(step, c, 1)) for c in range(CHIPS)])
+        if step == PLANES - 1:
+            arrived, border_far = lax.optimization_barrier((arrived, border_far))
         start = jnp.where(plane == step, arrived, start)
     start = jnp.where(even, permuted(start, TO_EVEN), start)
     solved = product(start, own_map) * scale + own_offset

time: 229 us -> 228 us (level)
  waiting for transfers between devices: 83.7 us -> 71 us
  starting transfers between devices: 94.2 us -> 104 us
    all_to_all x4 -> x5, waiting for transfers between devices: 41.8 us -> 30.1 us  [exchanged(): return lax.all_to_all(pieces, axis, 0, 0, axis_index_groups=groups)]
    ppermute x15, starting transfers between devices: 53.8 us -> 58.8 us  [permuted(): return lax.ppermute(value, 'blk', pairs)]
    all_to_all x4 -> x5, starting transfers between devices: 37.4 us -> 42 us  [exchanged(): return lax.all_to_all(pieces, axis, 0, 0, axis_index_groups=groups)]
    ppermute x15, waiting for transfers between devices: 15.5 us -> 12.6 us  [permuted(): return lax.ppermute(value, 'blk', pairs)]
  transfers between devices with their start and end apart: 20 -> 21, of which waited for: 12 -> 13; matrix products, arithmetic and copies ran while one was open for 6% -> 5% of each run, Pallas kernels for 0% -> 0%
where the time goes in v8:
time: 228 us; the launch traced here: 227 us
  starting transfers between devices  104 us (46%)
  waiting for transfers between devices  71 us (31%)
  matrix products  18.4 us (8%)
  blocking collectives  18.1 us (8%)
  local copies, waits for them, and re-layouts  7.62 us (3%)
  other arithmetic  6.53 us (3%)
    ppermute x15, starting transfers between devices, permuted(): return lax.ppermute(value, 'blk', pairs)  58.8 us
    all_to_all x5, starting transfers between devices, exchanged(): return lax.all_to_all(pieces, axis, 0, 0, axis_index_groups=groups)  42 us
    all_to_all x5, waiting for transfers between devices, exchanged(): return lax.all_to_all(pieces, axis, 0, 0, axis_index_groups=groups)  30.1 us
    ppermute x1, waiting for transfers between devices, body(): border_across = lax.ppermute(border_factor, 'rhs', ROW_SWAP)  28.3 us
    all_to_all x1, blocking collectives, exchanged(): return lax.all_to_all(pieces, axis, 0, 0, axis_index_groups=groups)  18.1 us
    ppermute x15, waiting for transfers between devices, permuted(): return lax.ppermute(value, 'blk', pairs)  12.6 us
    dot_general x12, matrix products, product(): lax.dot_general(left, right, (((1,), (0,)), ((), ())), precision=lax.Prec...  12.1 us
  transfers between devices with their start and end apart: 21, of which 13 were waited for; matrix products, arithmetic and copies ran while one was open for 5% of the time, Pallas kernels for 0%

profile of v8, /device:TPU:1, one launch (start us, length us, event | category | flops | bytes accessed | tf_op | source)
XLA Modules:
  0.0 226.9 jit_solution(18288769335467116746)
XLA Ops:
  3.3 6.0 %all-to-all-start = ((f32[8,128,512]{2,1,0:T(8,128)}), f32[8,128,512]{2,1,0:T(8,128)S(1)}, u32[]{:S(2)}, u32[]{:S(2)}) async-start(f32[8,128,512]{2,1,0:T(8,128)} %broadcast_in_dim.15), calls=%async_computation | async-start | bytes 4194304 | tf_op jit(solution)/shard_map/all_to_all | solution.py:34
  9.3 3.4 %collective-permute-start = (f32[256,512]{1,0:T(8,128)S(1)}, f32[256,512]{1,0:T(8,128)S(1)}, u32[]{:S(2)}, u32[]{:S(2)}) collective-permute-start(f32[256,512]{1,0:T(8,128)S(1)} %copy-done.5), channel_id=1, source_target_pairs={{0,4},{1,5},{2,6},{3,7},{4,0},{5,1},{6,2},{7,3},{8,12},{9,13},{10,... | collective-permute-start | bytes 1572872 | tf_op jit(solution)/shard_map/ppermute | solution.py:55
  12.7 28.3 %collective-permute-done = f32[256,512]{1,0:T(8,128)S(1)} collective-permute-done((f32[256,512]{1,0:T(8,128)S(1)}, f32[256,512]{1,0:T(8,128)S(1)}, u32[]{:S(2)}, u32[]{:S(2)}) %collective-permute-start) | collective-permute-done | bytes 524320 | tf_op jit(solution)/shard_map/ppermute | solution.py:55
  46.2 7.3 %collective-permute-start.1 = (f32[576,512]{1,0:T(8,128)}, f32[576,512]{1,0:T(8,128)S(1)}, u32[]{:S(2)}, u32[]{:S(2)}) collective-permute-start(f32[576,512]{1,0:T(8,128)} %pad_maximum_fusion), channel_id=1, source_target_pairs={{0,8},{8,0},{16,24},{24,16},{32,40},{40,32},{48,56},{56,48},{64,72... | collective-permute-start | bytes 3538952 | tf_op jit(solution)/shard_map/ppermute | solution.py:42
  53.5 2.6 %collective-permute-done.1 = f32[576,512]{1,0:T(8,128)S(1)} collective-permute-done((f32[576,512]{1,0:T(8,128)}, f32[576,512]{1,0:T(8,128)S(1)}, u32[]{:S(2)}, u32[]{:S(2)}) %collective-permute-start.1) | collective-permute-done | bytes 1179680 | tf_op jit(solution)/shard_map/ppermute | solution.py:42
  57.7 4.4 %all-to-all-start.1 = ((f32[4,256,512]{2,1,0:T(8,128)}), f32[4,256,512]{2,1,0:T(8,128)}, u32[]{:S(2)}, u32[]{:S(2)}) async-start(f32[4,256,512]{2,1,0:T(8,128)} %broadcast_in_dim.16), calls=%async_computation.1 | async-start | bytes 4194304 | tf_op jit(solution)/shard_map/all_to_all | solution.py:34
  62.4 2.0 fusion
  64.6 4.2 %collective-permute-start.2 = (f32[64,512]{1,0:T(8,128)S(1)}, f32[64,512]{1,0:T(8,128)S(1)}, u32[]{:S(2)}, u32[]{:S(2)}) collective-permute-start(f32[64,512]{1,0:T(8,128)S(1)} %get-tuple-element.22), channel_id=1, source_target_pairs={{0,16},{8,24},{16,32},{24,40},{32,48},{40,56},{48,64},{56,72},{64,... | collective-permute-start | bytes 393224 | tf_op jit(solution)/shard_map/ppermute | solution.py:42
  68.8 2.4 %collective-permute-done.2 = f32[64,512]{1,0:T(8,128)S(1)} collective-permute-done((f32[64,512]{1,0:T(8,128)S(1)}, f32[64,512]{1,0:T(8,128)S(1)}, u32[]{:S(2)}, u32[]{:S(2)}) %collective-permute-start.2) | collective-permute-done | bytes 131104 | tf_op jit(solution)/shard_map/ppermute | solution.py:42
  71.7 6.5 %collective-permute-start.3 = (f32[64,512]{1,0:T(8,128)S(1)}, f32[64,512]{1,0:T(8,128)S(1)}, u32[]{:S(2)}, u32[]{:S(2)}) collective-permute-start(f32[64,512]{1,0:T(8,128)S(1)} %fusion.5), channel_id=1, source_target_pairs={{0,16},{8,24},{16,32},{24,40},{32,48},{40,56},{48,64},{56,72},{64,... | collective-permute-start | bytes 393224 | tf_op jit(solution)/shard_map/ppermute | solution.py:42
  80.6 5.6 %collective-permute-start.4 = (f32[64,512]{1,0:T(8,128)S(1)}, f32[64,512]{1,0:T(8,128)S(1)}, u32[]{:S(2)}, u32[]{:S(2)}) collective-permute-start(f32[64,512]{1,0:T(8,128)S(1)} %fusion.6), channel_id=1, source_target_pairs={{0,16},{8,24},{16,32},{24,40},{32,48},{40,56},{48,64},{56,72},{64,... | collective-permute-start | bytes 393224 | tf_op jit(solution)/shard_map/ppermute | solution.py:42
  88.3 5.9 %collective-permute-start.5 = (f32[64,512]{1,0:T(8,128)S(1)}, f32[64,512]{1,0:T(8,128)S(1)}, u32[]{:S(2)}, u32[]{:S(2)}) collective-permute-start(f32[64,512]{1,0:T(8,128)S(1)} %collective-permute-done.4), channel_id=1, source_target_pairs={{0,8},{8,0},{16,24},{24,16},{32,40},{40,32},{48,56},{56,48},{64,72... | collective-permute-start | bytes 393224 | tf_op jit(solution)/shard_map/ppermute | solution.py:42
  97.3 6.4 %all-to-all-start.2 = ((f32[8,64,512]{2,1,0:T(8,128)}), f32[8,64,512]{2,1,0:T(8,128)S(1)}, u32[]{:S(2)}, u32[]{:S(2)}) async-start(f32[8,64,512]{2,1,0:T(8,128)} %broadcast_in_dim.18), calls=%async_computation.2 | async-start | bytes 2097152 | tf_op jit(solution)/shard_map/all_to_all | solution.py:34
  103.7 11.0 %collective-permute-start.6 = (f32[64,512]{1,0:T(8,128)S(1)}, f32[64,512]{1,0:T(8,128)S(1)}, u32[]{:S(2)}, u32[]{:S(2)}) collective-permute-start(f32[64,512]{1,0:T(8,128)S(1)} %get-tuple-element.29), channel_id=1, source_target_pairs={{8,72},{24,88},{40,104},{56,120},{9,73},{25,89},{41,105},{57,121},... | collective-permute-start | bytes 393224 | tf_op jit(solution)/shard_map/ppermute | solution.py:42
  114.8 3.9 %all-to-all-done.2 = f32[8,64,512]{2,1,0:T(8,128)S(1)} async-done(((f32[8,64,512]{2,1,0:T(8,128)}), f32[8,64,512]{2,1,0:T(8,128)S(1)}, u32[]{:S(2)}, u32[]{:S(2)}) %all-to-all-start.2) | async-done | bytes 1048608 | tf_op jit(solution)/shard_map/all_to_all | solution.py:34
  123.2 3.6 %all-to-all-start.3 = ((f32[4,256,512]{2,1,0:T(8,128)}), f32[4,256,512]{2,1,0:T(8,128)S(1)}, u32[]{:S(2)}, u32[]{:S(2)}) async-start(f32[4,256,512]{2,1,0:T(8,128)} %broadcast_in_dim.20), calls=%async_computation.3 | async-start | bytes 4194304 | tf_op jit(solution)/shard_map/all_to_all | solution.py:34
  138.3 14.0 %all-to-all-done.3 = f32[4,256,512]{2,1,0:T(8,128)S(1)} async-done(((f32[4,256,512]{2,1,0:T(8,128)}), f32[4,256,512]{2,1,0:T(8,128)S(1)}, u32[]{:S(2)}, u32[]{:S(2)}) %all-to-all-start.3) | async-done | bytes 2097184 | tf_op jit(solution)/shard_map/all_to_all | solution.py:34
  153.3 4.3 %collective-permute-start.13 = (f32[64,512]{1,0:T(8,128)S(1)}, f32[64,512]{1,0:T(8,128)}, u32[]{:S(2)}, u32[]{:S(2)}) collective-permute-start(f32[64,512]{1,0:T(8,128)S(1)} %broadcast_select_fusion.8), channel_id=1, source_target_pairs={{8,0},{24,16},{40,32},{56,48},{72,64},{88,80},{104,96},{120,112},{... | collective-permute-start | bytes 393224 | tf_op jit(solution)/shard_map/ppermute | solution.py:42
  159.3 2.7 %fusion.36 = f32[64,1024]{1,0:T(8,128)S(1)} fusion(f32[64,512]{1,0:T(8,128)S(1)} %fusion.13, f32[1024,512]{1,0:T(8,128)} %bitcast.7), kind=kOutput, calls=%fused_computation.69 | convolution fusion | flops 201326592 | bytes 2490368 | tf_op jit(solution)/shard_map/dot_general | solution.py:30
  163.1 2.3 collective-permute-start.14
  167.3 21.6 %all-to-all-start.4 = ((f32[32,8,256]{2,1,0:T(8,128)}), f32[32,8,256]{2,1,0:T(8,128)S(1)}, u32[]{:S(2)}, u32[]{:S(2)}) async-start(f32[32,8,256]{2,1,0:T(8,128)} %bitcast.11), calls=%async_computation.4 | async-start | bytes 524288 | tf_op jit(solution)/shard_map/all_to_all | solution.py:34
  188.9 12.0 %all-to-all-done.4 = f32[32,8,256]{2,1,0:T(8,128)S(1)} async-done(((f32[32,8,256]{2,1,0:T(8,128)}), f32[32,8,256]{2,1,0:T(8,128)S(1)}, u32[]{:S(2)}, u32[]{:S(2)}) %all-to-all-start.4) | async-done | bytes 262176 | tf_op jit(solution)/shard_map/all_to_all | solution.py:34
  201.7 18.1 %all_to_all.30 = f32[32,8,256]{2,1,0:T(8,128)S(1)} all-to-all(f32[32,8,256]{2,1,0:T(8,128)S(1)} %broadcast_in_dim.21), channel_id=1, replica_groups={{0,16,32,48,64,80,96,112,128,144,160,176,192,208,224,240,256,272,288,30..., dimensions={0} | all-to-all | bytes 524288 | tf_op jit(solution)/shard_map/all_to_all | solution.py:34
  219.8 5.1 %collective-permute-start.15 = (f32[64,1024]{1,0:T(8,128)S(1)}, f32[64,1024]{1,0:T(8,128)S(1)}, u32[]{:S(2)}, u32[]{:S(2)}) collective-permute-start(f32[64,1024]{1,0:T(8,128)S(1)} %bitcast.57), channel_id=1, source_target_pairs={{0,8},{8,0},{16,24},{24,16},{32,40},{40,32},{48,56},{56,48},{64,72... | collective-permute-start | bytes 786440 | tf_op jit(solution)/shard_map/ppermute | solution.py:42
  (80 shorter events, 42.1 us)
Async XLA Ops:
  0.6 43.1 %copy-start = (f32[64,512]{1,0:T(8,128)S(1)}, f32[64,512]{1,0:T(8,128)}, u32[]{:S(2)}) copy-start(f32[64,512]{1,0:T(8,128)} %param.8) | copy-start | bytes 393220
  3.3 37.7 %all-to-all-start = ((f32[8,128,512]{2,1,0:T(8,128)}), f32[8,128,512]{2,1,0:T(8,128)S(1)}, u32[]{:S(2)}, u32[]{:S(2)}) async-start(f32[8,128,512]{2,1,0:T(8,128)} %broadcast_in_dim.15), calls=%async_computation | async-start | bytes 4194304 | tf_op jit(solution)/shard_map/all_to_all | solution.py:34
  9.3 31.7 %collective-permute-start = (f32[256,512]{1,0:T(8,128)S(1)}, f32[256,512]{1,0:T(8,128)S(1)}, u32[]{:S(2)}, u32[]{:S(2)}) collective-permute-start(f32[256,512]{1,0:T(8,128)S(1)} %copy-done.5), channel_id=1, source_target_pairs={{0,4},{1,5},{2,6},{3,7},{4,0},{5,1},{6,2},{7,3},{8,12},{9,13},{10,... | collective-permute-start | bytes 1572872 | tf_op jit(solution)/shard_map/ppermute | solution.py:55
  45.1 17.1 %copy-start.1 = (f32[64,512]{1,0:T(8,128)}, f32[64,512]{1,0:T(8,128)S(1)}, u32[]{:S(2)}) copy-start(f32[64,512]{1,0:T(8,128)S(1)} %fusion.4) | copy-start | bytes 393220
  46.2 9.9 %collective-permute-start.1 = (f32[576,512]{1,0:T(8,128)}, f32[576,512]{1,0:T(8,128)S(1)}, u32[]{:S(2)}, u32[]{:S(2)}) collective-permute-start(f32[576,512]{1,0:T(8,128)} %pad_maximum_fusion), channel_id=1, source_target_pairs={{0,8},{8,0},{16,24},{24,16},{32,40},{40,32},{48,56},{56,48},{64,72... | collective-permute-start | bytes 3538952 | tf_op jit(solution)/shard_map/ppermute | solution.py:42
  57.7 30.6 %all-to-all-start.1 = ((f32[4,256,512]{2,1,0:T(8,128)}), f32[4,256,512]{2,1,0:T(8,128)}, u32[]{:S(2)}, u32[]{:S(2)}) async-start(f32[4,256,512]{2,1,0:T(8,128)} %broadcast_in_dim.16), calls=%async_computation.1 | async-start | bytes 4194304 | tf_op jit(solution)/shard_map/all_to_all | solution.py:34
  64.6 6.6 %collective-permute-start.2 = (f32[64,512]{1,0:T(8,128)S(1)}, f32[64,512]{1,0:T(8,128)S(1)}, u32[]{:S(2)}, u32[]{:S(2)}) collective-permute-start(f32[64,512]{1,0:T(8,128)S(1)} %get-tuple-element.22), channel_id=1, source_target_pairs={{0,16},{8,24},{16,32},{24,40},{32,48},{40,56},{48,64},{56,72},{64,... | collective-permute-start | bytes 393224 | tf_op jit(solution)/shard_map/ppermute | solution.py:42
  71.7 8.5 %collective-permute-start.3 = (f32[64,512]{1,0:T(8,128)S(1)}, f32[64,512]{1,0:T(8,128)S(1)}, u32[]{:S(2)}, u32[]{:S(2)}) collective-permute-start(f32[64,512]{1,0:T(8,128)S(1)} %fusion.5), channel_id=1, source_target_pairs={{0,16},{8,24},{16,32},{24,40},{32,48},{40,56},{48,64},{56,72},{64,... | collective-permute-start | bytes 393224 | tf_op jit(solution)/shard_map/ppermute | solution.py:42
  80.6 7.6 %collective-permute-start.4 = (f32[64,512]{1,0:T(8,128)S(1)}, f32[64,512]{1,0:T(8,128)S(1)}, u32[]{:S(2)}, u32[]{:S(2)}) collective-permute-start(f32[64,512]{1,0:T(8,128)S(1)} %fusion.6), channel_id=1, source_target_pairs={{0,16},{8,24},{16,32},{24,40},{32,48},{40,56},{48,64},{56,72},{64,... | collective-permute-start | bytes 393224 | tf_op jit(solution)/shard_map/ppermute | solution.py:42
  88.3 6.9 %collective-permute-start.5 = (f32[64,512]{1,0:T(8,128)S(1)}, f32[64,512]{1,0:T(8,128)S(1)}, u32[]{:S(2)}, u32[]{:S(2)}) collective-permute-start(f32[64,512]{1,0:T(8,128)S(1)} %collective-permute-done.4), channel_id=1, source_target_pairs={{0,8},{8,0},{16,24},{24,16},{32,40},{40,32},{48,56},{56,48},{64,72... | collective-permute-start | bytes 393224 | tf_op jit(solution)/shard_map/ppermute | solution.py:42
  97.3 21.4 %copy-start.7 = (f32[256,512]{1,0:T(8,128)S(1)}, f32[256,512]{1,0:T(8,128)}, u32[]{:S(2)}) copy-start(f32[256,512]{1,0:T(8,128)} %copy-done.6) | copy-start | bytes 1572868
  97.3 21.4 %all-to-all-start.2 = ((f32[8,64,512]{2,1,0:T(8,128)}), f32[8,64,512]{2,1,0:T(8,128)S(1)}, u32[]{:S(2)}, u32[]{:S(2)}) async-start(f32[8,64,512]{2,1,0:T(8,128)} %broadcast_in_dim.18), calls=%async_computation.2 | async-start | bytes 2097152 | tf_op jit(solution)/shard_map/all_to_all | solution.py:34
  103.7 16.6 %collective-permute-start.6 = (f32[64,512]{1,0:T(8,128)S(1)}, f32[64,512]{1,0:T(8,128)S(1)}, u32[]{:S(2)}, u32[]{:S(2)}) collective-permute-start(f32[64,512]{1,0:T(8,128)S(1)} %get-tuple-element.29), channel_id=1, source_target_pairs={{8,72},{24,88},{40,104},{56,120},{9,73},{25,89},{41,105},{57,121},... | collective-permute-start | bytes 393224 | tf_op jit(solution)/shard_map/ppermute | solution.py:42
  120.7 0.7 collective-permute-start.7
  121.8 4.9 %collective-permute-start.8 = (f32[64,512]{1,0:T(8,128)S(1)}, f32[64,512]{1,0:T(8,128)}, u32[]{:S(2)}, u32[]{:S(2)}) collective-permute-start(f32[64,512]{1,0:T(8,128)S(1)} %fusion.8), channel_id=1, source_target_pairs={{136,200},{152,216},{168,232},{184,248},{137,201},{153,217},{169,2... | collective-permute-start | bytes 393224 | tf_op jit(solution)/shard_map/ppermute | solution.py:42
  123.2 29.2 %all-to-all-start.3 = ((f32[4,256,512]{2,1,0:T(8,128)}), f32[4,256,512]{2,1,0:T(8,128)S(1)}, u32[]{:S(2)}, u32[]{:S(2)}) async-start(f32[4,256,512]{2,1,0:T(8,128)} %broadcast_in_dim.20), calls=%async_computation.3 | async-start | bytes 4194304 | tf_op jit(solution)/shard_map/all_to_all | solution.py:34
  127.9 1.3 collective-permute-start.9
  130.3 1.3 collective-permute-start.10
  134.3 0.7 collective-permute-start.11
  137.0 1.3 collective-permute-start.12
  153.3 4.7 %collective-permute-start.13 = (f32[64,512]{1,0:T(8,128)S(1)}, f32[64,512]{1,0:T(8,128)}, u32[]{:S(2)}, u32[]{:S(2)}) collective-permute-start(f32[64,512]{1,0:T(8,128)S(1)} %broadcast_select_fusion.8), channel_id=1, source_target_pairs={{8,0},{24,16},{40,32},{56,48},{72,64},{88,80},{104,96},{120,112},{... | collective-permute-start | bytes 393224 | tf_op jit(solution)/shard_map/ppermute | solution.py:42
  163.1 3.4 %collective-permute-start.14 = (f32[64,1024]{1,0:T(8,128)S(1)}, f32[64,1024]{1,0:T(8,128)S(1)}, u32[]{:S(2)}, u32[]{:S(2)}) collective-permute-start(f32[64,1024]{1,0:T(8,128)S(1)} %get-tuple-element.32), channel_id=1, source_target_pairs={{0,8},{8,0},{16,24},{24,16},{32,40},{40,32},{48,56},{56,48},{64,72... | collective-permute-start | bytes 786440 | tf_op jit(solution)/shard_map/ppermute | solution.py:42
  167.3 33.6 %all-to-all-start.4 = ((f32[32,8,256]{2,1,0:T(8,128)}), f32[32,8,256]{2,1,0:T(8,128)S(1)}, u32[]{:S(2)}, u32[]{:S(2)}) async-start(f32[32,8,256]{2,1,0:T(8,128)} %bitcast.11), calls=%async_computation.4 | async-start | bytes 524288 | tf_op jit(solution)/shard_map/all_to_all | solution.py:34
  219.8 6.2 %collective-permute-start.15 = (f32[64,1024]{1,0:T(8,128)S(1)}, f32[64,1024]{1,0:T(8,128)S(1)}, u32[]{:S(2)}, u32[]{:S(2)}) collective-permute-start(f32[64,1024]{1,0:T(8,128)S(1)} %bitcast.57), channel_id=1, source_target_pairs={{0,8},{8,0},{16,24},{24,16},{32,40},{40,32},{48,56},{56,48},{64,72... | collective-permute-start | bytes 786440 | tf_op jit(solution)/shard_map/ppermute | solution.py:42
  (9 other events, 23.6 us)

commit v9 on v7

--- a/solution.py
+++ b/solution.py
@@ -64,10 +64,6 @@
 
     block = jnp.concatenate([block_map, offset], axis=0)
     other = permuted(block, CORE_SWAP)
-    copies = jnp.broadcast_to(border_factor[None], (ROW,) + border_factor.shape)
-    other, copies = lax.optimization_barrier((other, copies))
-    border_near = exchanged(copies, "rhs", ROW_GROUPS)
-
     first, second = jnp.where(even, block, other), jnp.where(even, other, block)
     pair = product(first, second[:size])
     chip_map = pair[:size]
@@ -78,7 +74,7 @@
     added = jnp.where(even, 0.0, chip_offset)
     for _ in range(CHIPS - 2):
         state = product(permuted(state, NEXT_CHIP), chip_map) * factor + added
-    state, border_near = lax.optimization_barrier((permuted(state, NEXT_CHIP), border_near))
+    state = permuted(state, NEXT_CHIP)
     across = permuted(state, CORE_SWAP)
     window = jnp.concatenate([jnp.where(even, state, across), jnp.where(even, across, state)], axis=0)
     window = product(window, jnp.where(even, block_map, chip_map))
@@ -87,12 +83,14 @@
 
     arrived = permuted(own_offset, [(device(0, c, 1), device(1, c, 1)) for c in range(CHIPS)])
     own_map = to_all(window[:rows], "rhs", members).reshape(size, size)
-    own_map, border_near = lax.optimization_barrier((own_map, border_near))
-    border_far = lax.ppermute(border_near, "rhs", ROW_SWAP)
+    own_map, copies = lax.optimization_barrier((own_map, jnp.broadcast_to(border_factor[None], (ROW,) + border_factor.shape)))
+    border_near = exchanged(copies, "rhs", ROW_GROUPS)
     start = jnp.where(plane == 1, arrived, 0.0)
     for step in range(2, PLANES):
         end = product(start, own_map) * scale + own_offset
         arrived = permuted(end, [(device(step - 1, c, 1), device(step, c, 1)) for c in range(CHIPS)])
+        if step == PLANES - 1:
+            arrived, border_near = lax.optimization_barrier((arrived, border_near))
         start = jnp.where(plane == step, arrived, start)
     start = jnp.where(even, permuted(start, TO_EVEN), start)
     solved = product(start, own_map) * scale + own_offset
@@ -100,8 +98,10 @@
     border = border_rhs.shape[1]
     per_core, per_chip = border // CORES, border // CORES // CHIPS
     per_plane = rows // PLANES
-    near = product_transposed(solved, border_near.reshape(per_core, size))
-    far = product_transposed(solved, border_far.reshape(per_core, size))
+    border_near = border_near.reshape(per_core, size)
+    solved_across = lax.ppermute(solved, "rhs", ROW_SWAP)
+    near = product_transposed(solved, border_near)
+    far = lax.ppermute(product_transposed(solved_across, border_near), "rhs", ROW_SWAP)
     mine = core == member // ROW
     total = jnp.where(mine, near, far) + permuted(jnp.where(mine, far, near), CORE_SWAP)
     pieces = jnp.transpose(total.reshape(PLANES, per_plane, CHIPS, per_chip), (0, 2, 1, 3))

time: 229 us -> 225 us (0.983)
  waiting for transfers between devices: 83.7 us -> 79.7 us
  starting transfers between devices: 94.2 us -> 97.1 us
  matrix products: 18.4 us -> 15.9 us
    ppermute x1 -> x2, waiting for transfers between devices: 26.3 us -> 8.9 us  [the longest x1 5.38 us: body(): lax.ppermute(product_transposed(solved_across, border_near), 'rhs', ROW_S...]
    all_to_all x4, waiting for transfers between devices: 41.8 us -> 54.9 us  [exchanged(): return lax.all_to_all(pieces, axis, 0, 0, axis_index_groups=groups)]
    ppermute x1 -> x2, starting transfers between devices: 3.08 us -> 6.18 us  [the longest x1 3.09 us: body(): solved_across = lax.ppermute(solved, 'rhs', ROW_SWAP)]
  transfers between devices with their start and end apart: 20 -> 21, of which waited for: 12 -> 14; matrix products, arithmetic and copies ran while one was open for 6% -> 4% of each run, Pallas kernels for 0% -> 0%
where the time goes in v9:
time: 225 us; the launch traced here: 224 us
  starting transfers between devices  97.1 us (43%)
  waiting for transfers between devices  79.7 us (35%)
  blocking collectives  18.2 us (8%)
  matrix products  15.9 us (7%)
  other arithmetic  6.51 us (3%)
  local copies, waits for them, and re-layouts  5.41 us (2%)
    ppermute x15, starting transfers between devices, permuted(): return lax.ppermute(value, 'blk', pairs)  55.5 us
    all_to_all x4, waiting for transfers between devices, exchanged(): return lax.all_to_all(pieces, axis, 0, 0, axis_index_groups=groups)  54.9 us
    all_to_all x4, starting transfers between devices, exchanged(): return lax.all_to_all(pieces, axis, 0, 0, axis_index_groups=groups)  35.4 us
    all_to_all x1, blocking collectives, exchanged(): return lax.all_to_all(pieces, axis, 0, 0, axis_index_groups=groups)  18.2 us
    ppermute x15, waiting for transfers between devices, permuted(): return lax.ppermute(value, 'blk', pairs)  15.9 us
    dot_general x12, matrix products, product(): lax.dot_general(left, right, (((1,), (0,)), ((), ())), precision=lax.Prec...  11.2 us
    ppermute x1, waiting for transfers between devices, body(): lax.ppermute(product_transposed(solved_across, border_near), 'rhs', ROW_S...  5.38 us
  transfers between devices with their start and end apart: 21, of which 14 were waited for; matrix products, arithmetic and copies ran while one was open for 4% of the time, Pallas kernels for 0%

profile of v9, /device:TPU:1, one launch (start us, length us, event | category | flops | bytes accessed | tf_op | source)
XLA Modules:
  0.0 223.9 jit_solution(8782958194114342702)
XLA Ops:
  3.3 5.9 %all-to-all-start = ((f32[8,128,512]{2,1,0:T(8,128)}), f32[8,128,512]{2,1,0:T(8,128)S(1)}, u32[]{:S(2)}, u32[]{:S(2)}) async-start(f32[8,128,512]{2,1,0:T(8,128)} %broadcast_in_dim.13), calls=%async_computation | async-start | bytes 4194304 | tf_op jit(solution)/shard_map/all_to_all | solution.py:34
  9.1 25.1 %all-to-all-done = f32[8,128,512]{2,1,0:T(8,128)S(1)} async-done(((f32[8,128,512]{2,1,0:T(8,128)}), f32[8,128,512]{2,1,0:T(8,128)S(1)}, u32[]{:S(2)}, u32[]{:S(2)}) %all-to-all-start) | async-done | bytes 2097184 | tf_op jit(solution)/shard_map/all_to_all | solution.py:34
  38.9 3.7 %collective-permute-start = (f32[576,512]{1,0:T(8,128)}, f32[576,512]{1,0:T(8,128)S(1)}, u32[]{:S(2)}, u32[]{:S(2)}) collective-permute-start(f32[576,512]{1,0:T(8,128)} %pad_maximum_fusion), channel_id=1, source_target_pairs={{0,8},{8,0},{16,24},{24,16},{32,40},{40,32},{48,56},{56,48},{64,72... | collective-permute-start | bytes 3538952 | tf_op jit(solution)/shard_map/ppermute | solution.py:42
  42.6 2.6 %collective-permute-done = f32[576,512]{1,0:T(8,128)S(1)} collective-permute-done((f32[576,512]{1,0:T(8,128)}, f32[576,512]{1,0:T(8,128)S(1)}, u32[]{:S(2)}, u32[]{:S(2)}) %collective-permute-start) | collective-permute-done | bytes 1179680 | tf_op jit(solution)/shard_map/ppermute | solution.py:42
  47.7 4.2 %collective-permute-start.1 = (f32[64,512]{1,0:T(8,128)S(1)}, f32[64,512]{1,0:T(8,128)S(1)}, u32[]{:S(2)}, u32[]{:S(2)}) collective-permute-start(f32[64,512]{1,0:T(8,128)S(1)} %get-tuple-element.10), channel_id=1, source_target_pairs={{0,16},{8,24},{16,32},{24,40},{32,48},{40,56},{48,64},{56,72},{64,... | collective-permute-start | bytes 393224 | tf_op jit(solution)/shard_map/ppermute | solution.py:42
  54.9 5.0 %collective-permute-start.2 = (f32[64,512]{1,0:T(8,128)S(1)}, f32[64,512]{1,0:T(8,128)S(1)}, u32[]{:S(2)}, u32[]{:S(2)}) collective-permute-start(f32[64,512]{1,0:T(8,128)S(1)} %fusion.5), channel_id=1, source_target_pairs={{0,16},{8,24},{16,32},{24,40},{32,48},{40,56},{48,64},{56,72},{64,... | collective-permute-start | bytes 393224 | tf_op jit(solution)/shard_map/ppermute | solution.py:42
  62.5 5.5 %collective-permute-start.3 = (f32[64,512]{1,0:T(8,128)S(1)}, f32[64,512]{1,0:T(8,128)S(1)}, u32[]{:S(2)}, u32[]{:S(2)}) collective-permute-start(f32[64,512]{1,0:T(8,128)S(1)} %fusion.6), channel_id=1, source_target_pairs={{0,16},{8,24},{16,32},{24,40},{32,48},{40,56},{48,64},{56,72},{64,... | collective-permute-start | bytes 393224 | tf_op jit(solution)/shard_map/ppermute | solution.py:42
  68.1 4.3 %collective-permute-done.3 = f32[64,512]{1,0:T(8,128)S(1)} collective-permute-done((f32[64,512]{1,0:T(8,128)S(1)}, f32[64,512]{1,0:T(8,128)S(1)}, u32[]{:S(2)}, u32[]{:S(2)}) %collective-permute-start.3) | collective-permute-done | bytes 131104 | tf_op jit(solution)/shard_map/ppermute | solution.py:42
  72.4 6.7 %collective-permute-start.4 = (f32[64,512]{1,0:T(8,128)S(1)}, f32[64,512]{1,0:T(8,128)S(1)}, u32[]{:S(2)}, u32[]{:S(2)}) collective-permute-start(f32[64,512]{1,0:T(8,128)S(1)} %collective-permute-done.3), channel_id=1, source_target_pairs={{0,8},{8,0},{16,24},{24,16},{32,40},{40,32},{48,56},{56,48},{64,72... | collective-permute-start | bytes 393224 | tf_op jit(solution)/shard_map/ppermute | solution.py:42
  82.1 4.1 %all-to-all-start.1 = ((f32[8,64,512]{2,1,0:T(8,128)}), f32[8,64,512]{2,1,0:T(8,128)S(1)}, u32[]{:S(2)}, u32[]{:S(2)}) async-start(f32[8,64,512]{2,1,0:T(8,128)} %broadcast_in_dim.16), calls=%async_computation.1 | async-start | bytes 2097152 | tf_op jit(solution)/shard_map/all_to_all | solution.py:34
  86.2 11.2 %collective-permute-start.5 = (f32[64,512]{1,0:T(8,128)S(1)}, f32[64,512]{1,0:T(8,128)S(1)}, u32[]{:S(2)}, u32[]{:S(2)}) collective-permute-start(f32[64,512]{1,0:T(8,128)S(1)} %get-tuple-element.17), channel_id=1, source_target_pairs={{8,72},{24,88},{40,104},{56,120},{9,73},{25,89},{41,105},{57,121},... | collective-permute-start | bytes 393224 | tf_op jit(solution)/shard_map/ppermute | solution.py:42
  97.4 3.8 %all-to-all-done.1 = f32[8,64,512]{2,1,0:T(8,128)S(1)} async-done(((f32[8,64,512]{2,1,0:T(8,128)}), f32[8,64,512]{2,1,0:T(8,128)S(1)}, u32[]{:S(2)}, u32[]{:S(2)}) %all-to-all-start.1) | async-done | bytes 1048608 | tf_op jit(solution)/shard_map/all_to_all | solution.py:34
  105.7 3.6 %all-to-all-start.2 = ((f32[4,256,512]{2,1,0:T(8,128)}), f32[4,256,512]{2,1,0:T(8,128)S(1)}, u32[]{:S(2)}, u32[]{:S(2)}) async-start(f32[4,256,512]{2,1,0:T(8,128)} %broadcast_in_dim.17), calls=%async_computation.2 | async-start | bytes 4194304 | tf_op jit(solution)/shard_map/all_to_all | solution.py:34
  120.8 14.0 %all-to-all-done.2 = f32[4,256,512]{2,1,0:T(8,128)S(1)} async-done(((f32[4,256,512]{2,1,0:T(8,128)}), f32[4,256,512]{2,1,0:T(8,128)S(1)}, u32[]{:S(2)}, u32[]{:S(2)}) %all-to-all-start.2) | async-done | bytes 2097184 | tf_op jit(solution)/shard_map/all_to_all | solution.py:34
  135.8 3.6 %collective-permute-start.12 = (f32[64,512]{1,0:T(8,128)S(1)}, f32[64,512]{1,0:T(8,128)S(1)}, u32[]{:S(2)}, u32[]{:S(2)}) collective-permute-start(f32[64,512]{1,0:T(8,128)S(1)} %broadcast_select_fusion.8), channel_id=1, source_target_pairs={{8,0},{24,16},{40,32},{56,48},{72,64},{88,80},{104,96},{120,112},{... | collective-permute-start | bytes 393224 | tf_op jit(solution)/shard_map/ppermute | solution.py:42
  140.8 3.1 %collective-permute-start.13 = (f32[64,512]{1,0:T(8,128)S(1)}, f32[64,512]{1,0:T(8,128)S(1)}, u32[]{:S(2)}, u32[]{:S(2)}) collective-permute-start(f32[64,512]{1,0:T(8,128)S(1)} %fusion.13), channel_id=1, source_target_pairs={{0,4},{1,5},{2,6},{3,7},{4,0},{5,1},{6,2},{7,3},{8,12},{9,13},{10,... | collective-permute-start | bytes 393224 | tf_op jit(solution)/shard_map/ppermute | solution.py:102
  143.9 3.5 %collective-permute-done.13 = f32[64,512]{1,0:T(8,128)S(1)} collective-permute-done((f32[64,512]{1,0:T(8,128)S(1)}, f32[64,512]{1,0:T(8,128)S(1)}, u32[]{:S(2)}, u32[]{:S(2)}) %collective-permute-start.13) | collective-permute-done | bytes 131104 | tf_op jit(solution)/shard_map/ppermute | solution.py:102
  148.5 3.1 %collective-permute-start.14 = (f32[64,1024]{1,0:T(8,128)S(1)}, f32[64,1024]{1,0:T(8,128)S(1)}, u32[]{:S(2)}, u32[]{:S(2)}) collective-permute-start(f32[64,1024]{1,0:T(8,128)S(1)} %fusion.36), channel_id=1, source_target_pairs={{0,4},{1,5},{2,6},{3,7},{4,0},{5,1},{6,2},{7,3},{8,12},{9,13},{10,... | collective-permute-start | bytes 786440 | tf_op jit(solution)/shard_map/ppermute | solution.py:104
  151.6 5.4 %collective-permute-done.14 = f32[64,1024]{1,0:T(8,128)S(1)} collective-permute-done((f32[64,1024]{1,0:T(8,128)S(1)}, f32[64,1024]{1,0:T(8,128)S(1)}, u32[]{:S(2)}, u32[]{:S(2)}) %collective-permute-start.14) | collective-permute-done | bytes 262176 | tf_op jit(solution)/shard_map/ppermute | solution.py:104
  158.1 4.0 %collective-permute-start.15 = (f32[64,1024]{1,0:T(8,128)S(1)}, f32[64,1024]{1,0:T(8,128)S(1)}, u32[]{:S(2)}, u32[]{:S(2)}) collective-permute-start(f32[64,1024]{1,0:T(8,128)S(1)} %get-tuple-element.20), channel_id=1, source_target_pairs={{0,8},{8,0},{16,24},{24,16},{32,40},{40,32},{48,56},{56,48},{64,72... | collective-permute-start | bytes 786440 | tf_op jit(solution)/shard_map/ppermute | solution.py:42
  164.0 21.9 %all-to-all-start.3 = ((f32[32,8,256]{2,1,0:T(8,128)}), f32[32,8,256]{2,1,0:T(8,128)S(1)}, u32[]{:S(2)}, u32[]{:S(2)}) async-start(f32[32,8,256]{2,1,0:T(8,128)} %bitcast.10), calls=%async_computation.3 | async-start | bytes 524288 | tf_op jit(solution)/shard_map/all_to_all | solution.py:34
  185.9 11.9 %all-to-all-done.3 = f32[32,8,256]{2,1,0:T(8,128)S(1)} async-done(((f32[32,8,256]{2,1,0:T(8,128)}), f32[32,8,256]{2,1,0:T(8,128)S(1)}, u32[]{:S(2)}, u32[]{:S(2)}) %all-to-all-start.3) | async-done | bytes 262176 | tf_op jit(solution)/shard_map/all_to_all | solution.py:34
  198.7 18.2 %all_to_all.25 = f32[32,8,256]{2,1,0:T(8,128)S(1)} all-to-all(f32[32,8,256]{2,1,0:T(8,128)S(1)} %broadcast_in_dim.18), channel_id=1, replica_groups={{0,16,32,48,64,80,96,112,128,144,160,176,192,208,224,240,256,272,288,30..., dimensions={0} | all-to-all | bytes 524288 | tf_op jit(solution)/shard_map/all_to_all | solution.py:34
  216.8 5.0 %collective-permute-start.16 = (f32[64,1024]{1,0:T(8,128)S(1)}, f32[64,1024]{1,0:T(8,128)S(1)}, u32[]{:S(2)}, u32[]{:S(2)}) collective-permute-start(f32[64,1024]{1,0:T(8,128)S(1)} %bitcast.57), channel_id=1, source_target_pairs={{0,8},{8,0},{16,24},{24,16},{32,40},{40,32},{48,56},{56,48},{64,72... | collective-permute-start | bytes 786440 | tf_op jit(solution)/shard_map/ppermute | solution.py:42
  (71 shorter events, 43.3 us)
Async XLA Ops:
  0.6 35.8 %copy-start = (f32[64,512]{1,0:T(8,128)S(1)}, f32[64,512]{1,0:T(8,128)}, u32[]{:S(2)}) copy-start(f32[64,512]{1,0:T(8,128)} %param.8) | copy-start | bytes 393220
  3.3 31.0 %all-to-all-start = ((f32[8,128,512]{2,1,0:T(8,128)}), f32[8,128,512]{2,1,0:T(8,128)S(1)}, u32[]{:S(2)}, u32[]{:S(2)}) async-start(f32[8,128,512]{2,1,0:T(8,128)} %broadcast_in_dim.13), calls=%async_computation | async-start | bytes 4194304 | tf_op jit(solution)/shard_map/all_to_all | solution.py:34
  38.9 6.4 %collective-permute-start = (f32[576,512]{1,0:T(8,128)}, f32[576,512]{1,0:T(8,128)S(1)}, u32[]{:S(2)}, u32[]{:S(2)}) collective-permute-start(f32[576,512]{1,0:T(8,128)} %pad_maximum_fusion), channel_id=1, source_target_pairs={{0,8},{8,0},{16,24},{24,16},{32,40},{40,32},{48,56},{56,48},{64,72... | collective-permute-start | bytes 3538952 | tf_op jit(solution)/shard_map/ppermute | solution.py:42
  47.7 6.8 %collective-permute-start.1 = (f32[64,512]{1,0:T(8,128)S(1)}, f32[64,512]{1,0:T(8,128)S(1)}, u32[]{:S(2)}, u32[]{:S(2)}) collective-permute-start(f32[64,512]{1,0:T(8,128)S(1)} %get-tuple-element.10), channel_id=1, source_target_pairs={{0,16},{8,24},{16,32},{24,40},{32,48},{40,56},{48,64},{56,72},{64,... | collective-permute-start | bytes 393224 | tf_op jit(solution)/shard_map/ppermute | solution.py:42
  54.9 7.2 %collective-permute-start.2 = (f32[64,512]{1,0:T(8,128)S(1)}, f32[64,512]{1,0:T(8,128)S(1)}, u32[]{:S(2)}, u32[]{:S(2)}) collective-permute-start(f32[64,512]{1,0:T(8,128)S(1)} %fusion.5), channel_id=1, source_target_pairs={{0,16},{8,24},{16,32},{24,40},{32,48},{40,56},{48,64},{56,72},{64,... | collective-permute-start | bytes 393224 | tf_op jit(solution)/shard_map/ppermute | solution.py:42
  62.5 9.8 %collective-permute-start.3 = (f32[64,512]{1,0:T(8,128)S(1)}, f32[64,512]{1,0:T(8,128)S(1)}, u32[]{:S(2)}, u32[]{:S(2)}) collective-permute-start(f32[64,512]{1,0:T(8,128)S(1)} %fusion.6), channel_id=1, source_target_pairs={{0,16},{8,24},{16,32},{24,40},{32,48},{40,56},{48,64},{56,72},{64,... | collective-permute-start | bytes 393224 | tf_op jit(solution)/shard_map/ppermute | solution.py:42
  72.4 7.6 %collective-permute-start.4 = (f32[64,512]{1,0:T(8,128)S(1)}, f32[64,512]{1,0:T(8,128)S(1)}, u32[]{:S(2)}, u32[]{:S(2)}) collective-permute-start(f32[64,512]{1,0:T(8,128)S(1)} %collective-permute-done.3), channel_id=1, source_target_pairs={{0,8},{8,0},{16,24},{24,16},{32,40},{40,32},{48,56},{56,48},{64,72... | collective-permute-start | bytes 393224 | tf_op jit(solution)/shard_map/ppermute | solution.py:42
  82.1 19.0 %copy-start.4 = (f32[256,512]{1,0:T(8,128)S(1)}, f32[256,512]{1,0:T(8,128)}, u32[]{:S(2)}) copy-start(f32[256,512]{1,0:T(8,128)} %param.10) | copy-start | bytes 1572868
  82.1 19.0 %all-to-all-start.1 = ((f32[8,64,512]{2,1,0:T(8,128)}), f32[8,64,512]{2,1,0:T(8,128)S(1)}, u32[]{:S(2)}, u32[]{:S(2)}) async-start(f32[8,64,512]{2,1,0:T(8,128)} %broadcast_in_dim.16), calls=%async_computation.1 | async-start | bytes 2097152 | tf_op jit(solution)/shard_map/all_to_all | solution.py:34
  86.2 16.6 %collective-permute-start.5 = (f32[64,512]{1,0:T(8,128)S(1)}, f32[64,512]{1,0:T(8,128)S(1)}, u32[]{:S(2)}, u32[]{:S(2)}) collective-permute-start(f32[64,512]{1,0:T(8,128)S(1)} %get-tuple-element.17), channel_id=1, source_target_pairs={{8,72},{24,88},{40,104},{56,120},{9,73},{25,89},{41,105},{57,121},... | collective-permute-start | bytes 393224 | tf_op jit(solution)/shard_map/ppermute | solution.py:42
  103.2 0.7 collective-permute-start.6
  104.3 4.9 %collective-permute-start.7 = (f32[64,512]{1,0:T(8,128)S(1)}, f32[64,512]{1,0:T(8,128)}, u32[]{:S(2)}, u32[]{:S(2)}) collective-permute-start(f32[64,512]{1,0:T(8,128)S(1)} %fusion.8), channel_id=1, source_target_pairs={{136,200},{152,216},{168,232},{184,248},{137,201},{153,217},{169,2... | collective-permute-start | bytes 393224 | tf_op jit(solution)/shard_map/ppermute | solution.py:42
  105.7 29.2 %all-to-all-start.2 = ((f32[4,256,512]{2,1,0:T(8,128)}), f32[4,256,512]{2,1,0:T(8,128)S(1)}, u32[]{:S(2)}, u32[]{:S(2)}) async-start(f32[4,256,512]{2,1,0:T(8,128)} %broadcast_in_dim.17), calls=%async_computation.2 | async-start | bytes 4194304 | tf_op jit(solution)/shard_map/all_to_all | solution.py:34
  110.4 1.3 collective-permute-start.8
  112.8 1.3 collective-permute-start.9
  116.8 0.7 collective-permute-start.10
  119.5 1.3 collective-permute-start.11
  135.8 4.6 %collective-permute-start.12 = (f32[64,512]{1,0:T(8,128)S(1)}, f32[64,512]{1,0:T(8,128)S(1)}, u32[]{:S(2)}, u32[]{:S(2)}) collective-permute-start(f32[64,512]{1,0:T(8,128)S(1)} %broadcast_select_fusion.8), channel_id=1, source_target_pairs={{8,0},{24,16},{40,32},{56,48},{72,64},{88,80},{104,96},{120,112},{... | collective-permute-start | bytes 393224 | tf_op jit(solution)/shard_map/ppermute | solution.py:42
  140.8 16.2 %copy-start.6 = (f32[64,512]{1,0:T(8,128)}, f32[64,512]{1,0:T(8,128)S(1)}, u32[]{:S(2)}) copy-start(f32[64,512]{1,0:T(8,128)S(1)} %fusion.13) | copy-start | bytes 393220
  140.8 6.6 %collective-permute-start.13 = (f32[64,512]{1,0:T(8,128)S(1)}, f32[64,512]{1,0:T(8,128)S(1)}, u32[]{:S(2)}, u32[]{:S(2)}) collective-permute-start(f32[64,512]{1,0:T(8,128)S(1)} %fusion.13), channel_id=1, source_target_pairs={{0,4},{1,5},{2,6},{3,7},{4,0},{5,1},{6,2},{7,3},{8,12},{9,13},{10,... | collective-permute-start | bytes 393224 | tf_op jit(solution)/shard_map/ppermute | solution.py:102
  148.5 8.5 %collective-permute-start.14 = (f32[64,1024]{1,0:T(8,128)S(1)}, f32[64,1024]{1,0:T(8,128)S(1)}, u32[]{:S(2)}, u32[]{:S(2)}) collective-permute-start(f32[64,1024]{1,0:T(8,128)S(1)} %fusion.36), channel_id=1, source_target_pairs={{0,4},{1,5},{2,6},{3,7},{4,0},{5,1},{6,2},{7,3},{8,12},{9,13},{10,... | collective-permute-start | bytes 786440 | tf_op jit(solution)/shard_map/ppermute | solution.py:104
  158.1 5.2 %collective-permute-start.15 = (f32[64,1024]{1,0:T(8,128)S(1)}, f32[64,1024]{1,0:T(8,128)S(1)}, u32[]{:S(2)}, u32[]{:S(2)}) collective-permute-start(f32[64,1024]{1,0:T(8,128)S(1)} %get-tuple-element.20), channel_id=1, source_target_pairs={{0,8},{8,0},{16,24},{24,16},{32,40},{40,32},{48,56},{56,48},{64,72... | collective-permute-start | bytes 786440 | tf_op jit(solution)/shard_map/ppermute | solution.py:42
  164.0 33.9 %all-to-all-start.3 = ((f32[32,8,256]{2,1,0:T(8,128)}), f32[32,8,256]{2,1,0:T(8,128)S(1)}, u32[]{:S(2)}, u32[]{:S(2)}) async-start(f32[32,8,256]{2,1,0:T(8,128)} %bitcast.10), calls=%async_computation.3 | async-start | bytes 524288 | tf_op jit(solution)/shard_map/all_to_all | solution.py:34
  216.8 6.2 %collective-permute-start.16 = (f32[64,1024]{1,0:T(8,128)S(1)}, f32[64,1024]{1,0:T(8,128)S(1)}, u32[]{:S(2)}, u32[]{:S(2)}) collective-permute-start(f32[64,1024]{1,0:T(8,128)S(1)} %bitcast.57), channel_id=1, source_target_pairs={{0,8},{8,0},{16,24},{24,16},{32,40},{40,32},{48,56},{56,48},{64,72... | collective-permute-start | bytes 786440 | tf_op jit(solution)/shard_map/ppermute | solution.py:42
  (5 other events, 12.7 us)

commit v10 on v9

--- a/solution.py
+++ b/solution.py
@@ -1,6 +1,8 @@
 import jax
 import jax.numpy as jnp
 from jax import lax
+from jax.experimental import pallas as pl
+from jax.experimental.pallas import tpu as pltpu
 from jax.sharding import PartitionSpec as P
 
 PLANES, CHIPS, CORES = 8, 4, 2
@@ -28,6 +30,39 @@
 
 def product_transposed(left, right):
     return lax.dot_general(left, right, (((1,), (1,)), ((), ())), precision=lax.Precision.HIGH, preferred_element_type=jnp.float32)
+
+
+def split(value):
+    high = value.astype(jnp.bfloat16)
+    return high, (value - high.astype(jnp.float32)).astype(jnp.bfloat16)
+
+
+def border_kernel(left_ref, border_ref, out_ref):
+    left_high, left_low = split(left_ref[...])
+    high, low = split(border_ref[...])
+
+    def dot(left, right):
+        return lax.dot_general(left, right, (((1,), (1,)), ((), ())), preferred_element_type=jnp.float32)
+
+    out_ref[...] = dot(left_high, high) + (dot(left_high, low) + dot(left_low, high))
+
+
+def border_product(left, border):
+    rows, size = left.shape
+    columns = border.shape[0]
+    tile = columns // 4
+    return pl.pallas_call(
+        border_kernel,
+        out_shape=jax.ShapeDtypeStruct((rows, columns), jnp.float32),
+        grid=(columns // tile,),
+        in_specs=[
+            pl.BlockSpec((rows, size), lambda i: (0, 0)),
+            pl.BlockSpec((tile, size), lambda i: (i, 0)),
+        ],
+        out_specs=pl.BlockSpec((rows, tile), lambda i: (0, i)),
+        compiler_params=pltpu.CompilerParams(vmem_limit_bytes=8 * 2**20),
+        cost_estimate=pl.CostEstimate(flops=6 * rows * size * columns, bytes_accessed=4 * size * columns, transcendentals=0),
+    )(left, pltpu.with_memory_space_constraint(border, pltpu.HBM))
 
 
 def exchanged(pieces, axis, groups=None):
@@ -85,13 +120,13 @@
     own_map = to_all(window[:rows], "rhs", members).reshape(size, size)
     own_map, copies = lax.optimization_barrier((own_map, jnp.broadcast_to(border_factor[None], (ROW,) + border_factor.shape)))
     border_near = exchanged(copies, "rhs", ROW_GROUPS)
-    start = jnp.where(plane == 1, arrived, 0.0)
+    start = arrived
     for step in range(2, PLANES):
         end = product(start, own_map) * scale + own_offset
         arrived = permuted(end, [(device(step - 1, c, 1), device(step, c, 1)) for c in range(CHIPS)])
         if step == PLANES - 1:
             arrived, border_near = lax.optimization_barrier((arrived, border_near))
-        start = jnp.where(plane == step, arrived, start)
+        start = start + arrived
     start = jnp.where(even, permuted(start, TO_EVEN), start)
     solved = product(start, own_map) * scale + own_offset
 
@@ -100,8 +135,8 @@
     per_plane = rows // PLANES
     border_near = border_near.reshape(per_core, size)
     solved_across = lax.ppermute(solved, "rhs", ROW_SWAP)
-    near = product_transposed(solved, border_near)
-    far = lax.ppermute(product_transposed(solved_across, border_near), "rhs", ROW_SWAP)
+    near = border_product(solved, border_near)
+    far = lax.ppermute(border_product(solved_across, border_near), "rhs", ROW_SWAP)
     mine = core == member // ROW
     total = jnp.where(mine, near, far) + permuted(jnp.where(mine, far, near), CORE_SWAP)
     pieces = jnp.transpose(total.reshape(PLANES, per_plane, CHIPS, per_chip), (0, 2, 1, 3))

time: 225 us -> 227 us (level)
  Pallas kernels: 0 us -> 6.51 us
  matrix products: 15.9 us -> 9.96 us
    pallas_call x0 -> x2, Pallas kernels: none -> 6.51 us  [border_product(): pl.pallas_call(border_kernel, out_shape=jax.ShapeDtypeStruct((rows, colum...]
    all_to_all x4, waiting for transfers between devices: 54.9 us -> 60.3 us  [exchanged(): return lax.all_to_all(pieces, axis, 0, 0, axis_index_groups=groups)]
    dot_general x12, matrix products: 11.2 us -> 7.46 us  [product(): lax.dot_general(left, right, (((1,), (0,)), ((), ())), precision=lax.Prec...]
    ppermute x1, waiting for transfers between devices: 5.38 us -> 2.11 us  [body(): lax.ppermute(border_product(solved_across, border_near), 'rhs', ROW_SWAP)]
  transfers between devices with their start and end apart: 21 -> 21, of which waited for: 14 -> 14; matrix products, arithmetic and copies ran while one was open for 4% -> 2% of each run, Pallas kernels for 0% -> 1%
where the time goes in v10:
time: 227 us; the launch traced here: 226 us
  starting transfers between devices  95.6 us (42%)
  waiting for transfers between devices  81.8 us (36%)
  blocking collectives  18.2 us (8%)
  matrix products  9.96 us (4%)
  other arithmetic  6.93 us (3%)
  Pallas kernels  6.51 us (3%)
  local copies, waits for them, and re-layouts  5.43 us (2%)
    all_to_all x4, waiting for transfers between devices, exchanged(): return lax.all_to_all(pieces, axis, 0, 0, axis_index_groups=groups)  60.3 us
    ppermute x15, starting transfers between devices, permuted(): return lax.ppermute(value, 'blk', pairs)  54.3 us
    all_to_all x4, starting transfers between devices, exchanged(): return lax.all_to_all(pieces, axis, 0, 0, axis_index_groups=groups)  35.2 us
    all_to_all x1, blocking collectives, exchanged(): return lax.all_to_all(pieces, axis, 0, 0, axis_index_groups=groups)  18.2 us
    ppermute x15, waiting for transfers between devices, permuted(): return lax.ppermute(value, 'blk', pairs)  15.9 us
    dot_general x12, matrix products, product(): lax.dot_general(left, right, (((1,), (0,)), ((), ())), precision=lax.Prec...  7.46 us
    pallas_call x2, Pallas kernels, border_product(): pl.pallas_call(border_kernel, out_shape=jax.ShapeDtypeStruct((rows, colum...  6.51 us
  transfers between devices with their start and end apart: 21, of which 14 were waited for; matrix products, arithmetic and copies ran while one was open for 2% of the time, Pallas kernels for 1%

profile of v10, /device:TPU:1, one launch (start us, length us, event | category | flops | bytes accessed | tf_op | source)
XLA Modules:
  0.0 225.6 jit_solution(9992976790541233918)
XLA Ops:
  3.3 5.9 %all-to-all-start = ((f32[8,128,512]{2,1,0:T(8,128)}), f32[8,128,512]{2,1,0:T(8,128)S(1)}, u32[]{:S(2)}, u32[]{:S(2)}) async-start(f32[8,128,512]{2,1,0:T(8,128)} %broadcast_in_dim.12), calls=%async_computation | async-start | bytes 4194304 | tf_op jit(solution)/shard_map/all_to_all | solution.py:69
  9.1 25.1 %all-to-all-done = f32[8,128,512]{2,1,0:T(8,128)S(1)} async-done(((f32[8,128,512]{2,1,0:T(8,128)}), f32[8,128,512]{2,1,0:T(8,128)S(1)}, u32[]{:S(2)}, u32[]{:S(2)}) %all-to-all-start) | async-done | bytes 2097184 | tf_op jit(solution)/shard_map/all_to_all | solution.py:69
  38.9 3.7 %collective-permute-start = (f32[576,512]{1,0:T(8,128)}, f32[576,512]{1,0:T(8,128)S(1)}, u32[]{:S(2)}, u32[]{:S(2)}) collective-permute-start(f32[576,512]{1,0:T(8,128)} %pad_maximum_fusion), channel_id=1, source_target_pairs={{0,8},{8,0},{16,24},{24,16},{32,40},{40,32},{48,56},{56,48},{64,72... | collective-permute-start | bytes 3538952 | tf_op jit(solution)/shard_map/ppermute | solution.py:77
  47.7 4.2 %collective-permute-start.1 = (f32[64,512]{1,0:T(8,128)S(1)}, f32[64,512]{1,0:T(8,128)S(1)}, u32[]{:S(2)}, u32[]{:S(2)}) collective-permute-start(f32[64,512]{1,0:T(8,128)S(1)} %get-tuple-element.10), channel_id=1, source_target_pairs={{0,16},{8,24},{16,32},{24,40},{32,48},{40,56},{48,64},{56,72},{64,... | collective-permute-start | bytes 393224 | tf_op jit(solution)/shard_map/ppermute | solution.py:77
  54.9 5.0 %collective-permute-start.2 = (f32[64,512]{1,0:T(8,128)S(1)}, f32[64,512]{1,0:T(8,128)S(1)}, u32[]{:S(2)}, u32[]{:S(2)}) collective-permute-start(f32[64,512]{1,0:T(8,128)S(1)} %fusion.5), channel_id=1, source_target_pairs={{0,16},{8,24},{16,32},{24,40},{32,48},{40,56},{48,64},{56,72},{64,... | collective-permute-start | bytes 393224 | tf_op jit(solution)/shard_map/ppermute | solution.py:77
  62.6 5.5 %collective-permute-start.3 = (f32[64,512]{1,0:T(8,128)S(1)}, f32[64,512]{1,0:T(8,128)S(1)}, u32[]{:S(2)}, u32[]{:S(2)}) collective-permute-start(f32[64,512]{1,0:T(8,128)S(1)} %fusion.6), channel_id=1, source_target_pairs={{0,16},{8,24},{16,32},{24,40},{32,48},{40,56},{48,64},{56,72},{64,... | collective-permute-start | bytes 393224 | tf_op jit(solution)/shard_map/ppermute | solution.py:77
  68.1 4.3 %collective-permute-done.3 = f32[64,512]{1,0:T(8,128)S(1)} collective-permute-done((f32[64,512]{1,0:T(8,128)S(1)}, f32[64,512]{1,0:T(8,128)S(1)}, u32[]{:S(2)}, u32[]{:S(2)}) %collective-permute-start.3) | collective-permute-done | bytes 131104 | tf_op jit(solution)/shard_map/ppermute | solution.py:77
  72.4 6.7 %collective-permute-start.4 = (f32[64,512]{1,0:T(8,128)S(1)}, f32[64,512]{1,0:T(8,128)S(1)}, u32[]{:S(2)}, u32[]{:S(2)}) collective-permute-start(f32[64,512]{1,0:T(8,128)S(1)} %collective-permute-done.3), channel_id=1, source_target_pairs={{0,8},{8,0},{16,24},{24,16},{32,40},{40,32},{48,56},{56,48},{64,72... | collective-permute-start | bytes 393224 | tf_op jit(solution)/shard_map/ppermute | solution.py:77
  82.1 4.1 %all-to-all-start.1 = ((f32[8,64,512]{2,1,0:T(8,128)}), f32[8,64,512]{2,1,0:T(8,128)S(1)}, u32[]{:S(2)}, u32[]{:S(2)}) async-start(f32[8,64,512]{2,1,0:T(8,128)} %broadcast_in_dim.14), calls=%async_computation.1 | async-start | bytes 2097152 | tf_op jit(solution)/shard_map/all_to_all | solution.py:69
  86.2 11.1 %collective-permute-start.5 = (f32[64,512]{1,0:T(8,128)S(1)}, f32[64,512]{1,0:T(8,128)S(1)}, u32[]{:S(2)}, u32[]{:S(2)}) collective-permute-start(f32[64,512]{1,0:T(8,128)S(1)} %get-tuple-element.17), channel_id=1, source_target_pairs={{8,72},{24,88},{40,104},{56,120},{9,73},{25,89},{41,105},{57,121},... | collective-permute-start | bytes 393224 | tf_op jit(solution)/shard_map/ppermute | solution.py:77
  97.3 3.8 %all-to-all-done.1 = f32[8,64,512]{2,1,0:T(8,128)S(1)} async-done(((f32[8,64,512]{2,1,0:T(8,128)}), f32[8,64,512]{2,1,0:T(8,128)S(1)}, u32[]{:S(2)}, u32[]{:S(2)}) %all-to-all-start.1) | async-done | bytes 1048608 | tf_op jit(solution)/shard_map/all_to_all | solution.py:69
  106.3 3.6 %all-to-all-start.2 = ((f32[4,256,512]{2,1,0:T(8,128)}), f32[4,256,512]{2,1,0:T(8,128)S(1)}, u32[]{:S(2)}, u32[]{:S(2)}) async-start(f32[4,256,512]{2,1,0:T(8,128)} %broadcast_in_dim.15), calls=%async_computation.2 | async-start | bytes 4194304 | tf_op jit(solution)/shard_map/all_to_all | solution.py:69
  116.1 19.4 %all-to-all-done.2 = f32[4,256,512]{2,1,0:T(8,128)S(1)} async-done(((f32[4,256,512]{2,1,0:T(8,128)}), f32[4,256,512]{2,1,0:T(8,128)S(1)}, u32[]{:S(2)}, u32[]{:S(2)}) %all-to-all-start.2) | async-done | bytes 2097184 | tf_op jit(solution)/shard_map/all_to_all | solution.py:69
  136.5 3.6 %collective-permute-start.12 = (f32[64,512]{1,0:T(8,128)S(1)}, f32[64,512]{1,0:T(8,128)S(1)}, u32[]{:S(2)}, u32[]{:S(2)}) collective-permute-start(f32[64,512]{1,0:T(8,128)S(1)} %add.97), channel_id=1, source_target_pairs={{8,0},{24,16},{40,32},{56,48},{72,64},{88,80},{104,96},{120,112},{... | collective-permute-start | bytes 393224 | tf_op jit(solution)/shard_map/ppermute | solution.py:77
  141.6 3.1 %collective-permute-start.13 = (f32[64,512]{1,0:T(8,128)S(1)}, f32[64,512]{1,0:T(8,128)S(1)}, u32[]{:S(2)}, u32[]{:S(2)}) collective-permute-start(f32[64,512]{1,0:T(8,128)S(1)} %fusion.13.left_ref), channel_id=1, source_target_pairs={{0,4},{1,5},{2,6},{3,7},{4,0},{5,1},{6,2},{7,3},{8,12},{9,13},{10,... | collective-permute-start | bytes 393224 | tf_op jit(solution)/shard_map/ppermute | solution.py:137
  144.7 3.5 %collective-permute-done.13.left_ref = f32[64,512]{1,0:T(8,128)S(1)} collective-permute-done((f32[64,512]{1,0:T(8,128)S(1)}, f32[64,512]{1,0:T(8,128)S(1)}, u32[]{:S(2)}, u32[]{:S(2)}) %collective-permute-start.13) | collective-permute-done | bytes 131104 | tf_op jit(solution)/shard_map/ppermute | solution.py:137
  148.2 3.3 %shard_map.78 = f32[64,1024]{1,0:T(8,128)S(1)} custom-call(f32[64,512]{1,0:T(8,128)S(1)} %collective-permute-done.13.left_ref, f32[1024,512]{1,0:T(8,128)} %bitcast.52), custom_call_target="tpu_custom_call" | custom-call | flops 201326592 | bytes 2097152 | tf_op jit(solution)/shard_map/pallas_call | solution.py:54
  151.5 3.1 %collective-permute-start.14 = (f32[64,1024]{1,0:T(8,128)S(1)}, f32[64,1024]{1,0:T(8,128)S(1)}, u32[]{:S(2)}, u32[]{:S(2)}) collective-permute-start(f32[64,1024]{1,0:T(8,128)S(1)} %shard_map.78), channel_id=1, source_target_pairs={{0,4},{1,5},{2,6},{3,7},{4,0},{5,1},{6,2},{7,3},{8,12},{9,13},{10,... | collective-permute-start | bytes 786440 | tf_op jit(solution)/shard_map/ppermute | solution.py:139
  154.6 3.3 %shard_map.77 = f32[64,1024]{1,0:T(8,128)S(1)} custom-call(f32[64,512]{1,0:T(8,128)S(1)} %fusion.13.left_ref, f32[1024,512]{1,0:T(8,128)} %bitcast.53), custom_call_target="tpu_custom_call" | custom-call | flops 201326592 | bytes 2097152 | tf_op jit(solution)/shard_map/pallas_call | solution.py:54
  160.0 4.0 %collective-permute-start.15 = (f32[64,1024]{1,0:T(8,128)S(1)}, f32[64,1024]{1,0:T(8,128)S(1)}, u32[]{:S(2)}, u32[]{:S(2)}) collective-permute-start(f32[64,1024]{1,0:T(8,128)S(1)} %broadcast_select_fusion.1), channel_id=1, source_target_pairs={{0,8},{8,0},{16,24},{24,16},{32,40},{40,32},{48,56},{56,48},{64,72... | collective-permute-start | bytes 786440 | tf_op jit(solution)/shard_map/ppermute | solution.py:77
  165.9 21.6 %all-to-all-start.3 = ((f32[32,8,256]{2,1,0:T(8,128)}), f32[32,8,256]{2,1,0:T(8,128)S(1)}, u32[]{:S(2)}, u32[]{:S(2)}) async-start(f32[32,8,256]{2,1,0:T(8,128)} %bitcast.10), calls=%async_computation.3 | async-start | bytes 524288 | tf_op jit(solution)/shard_map/all_to_all | solution.py:69
  187.6 11.9 %all-to-all-done.3 = f32[32,8,256]{2,1,0:T(8,128)S(1)} async-done(((f32[32,8,256]{2,1,0:T(8,128)}), f32[32,8,256]{2,1,0:T(8,128)S(1)}, u32[]{:S(2)}, u32[]{:S(2)}) %all-to-all-start.3) | async-done | bytes 262176 | tf_op jit(solution)/shard_map/all_to_all | solution.py:69
  200.3 18.2 %all_to_all.25 = f32[32,8,256]{2,1,0:T(8,128)S(1)} all-to-all(f32[32,8,256]{2,1,0:T(8,128)S(1)} %broadcast_in_dim.16), channel_id=1, replica_groups={{0,16,32,48,64,80,96,112,128,144,160,176,192,208,224,240,256,272,288,30..., dimensions={0} | all-to-all | bytes 524288 | tf_op jit(solution)/shard_map/all_to_all | solution.py:69
  218.5 5.0 %collective-permute-start.16 = (f32[64,1024]{1,0:T(8,128)S(1)}, f32[64,1024]{1,0:T(8,128)S(1)}, u32[]{:S(2)}, u32[]{:S(2)}) collective-permute-start(f32[64,1024]{1,0:T(8,128)S(1)} %bitcast.57), channel_id=1, source_target_pairs={{0,8},{8,0},{16,24},{24,16},{32,40},{40,32},{48,56},{56,48},{64,72... | collective-permute-start | bytes 786440 | tf_op jit(solution)/shard_map/ppermute | solution.py:77
  (73 shorter events, 41.3 us)
Async XLA Ops:
  0.6 35.8 %copy-start = (f32[64,512]{1,0:T(8,128)S(1)}, f32[64,512]{1,0:T(8,128)}, u32[]{:S(2)}) copy-start(f32[64,512]{1,0:T(8,128)} %param.8) | copy-start | bytes 393220
  3.3 31.0 %all-to-all-start = ((f32[8,128,512]{2,1,0:T(8,128)}), f32[8,128,512]{2,1,0:T(8,128)S(1)}, u32[]{:S(2)}, u32[]{:S(2)}) async-start(f32[8,128,512]{2,1,0:T(8,128)} %broadcast_in_dim.12), calls=%async_computation | async-start | bytes 4194304 | tf_op jit(solution)/shard_map/all_to_all | solution.py:69
  38.9 6.4 %collective-permute-start = (f32[576,512]{1,0:T(8,128)}, f32[576,512]{1,0:T(8,128)S(1)}, u32[]{:S(2)}, u32[]{:S(2)}) collective-permute-start(f32[576,512]{1,0:T(8,128)} %pad_maximum_fusion), channel_id=1, source_target_pairs={{0,8},{8,0},{16,24},{24,16},{32,40},{40,32},{48,56},{56,48},{64,72... | collective-permute-start | bytes 3538952 | tf_op jit(solution)/shard_map/ppermute | solution.py:77
  47.7 6.8 %collective-permute-start.1 = (f32[64,512]{1,0:T(8,128)S(1)}, f32[64,512]{1,0:T(8,128)S(1)}, u32[]{:S(2)}, u32[]{:S(2)}) collective-permute-start(f32[64,512]{1,0:T(8,128)S(1)} %get-tuple-element.10), channel_id=1, source_target_pairs={{0,16},{8,24},{16,32},{24,40},{32,48},{40,56},{48,64},{56,72},{64,... | collective-permute-start | bytes 393224 | tf_op jit(solution)/shard_map/ppermute | solution.py:77
  54.9 7.2 %collective-permute-start.2 = (f32[64,512]{1,0:T(8,128)S(1)}, f32[64,512]{1,0:T(8,128)S(1)}, u32[]{:S(2)}, u32[]{:S(2)}) collective-permute-start(f32[64,512]{1,0:T(8,128)S(1)} %fusion.5), channel_id=1, source_target_pairs={{0,16},{8,24},{16,32},{24,40},{32,48},{40,56},{48,64},{56,72},{64,... | collective-permute-start | bytes 393224 | tf_op jit(solution)/shard_map/ppermute | solution.py:77
  62.6 9.8 %collective-permute-start.3 = (f32[64,512]{1,0:T(8,128)S(1)}, f32[64,512]{1,0:T(8,128)S(1)}, u32[]{:S(2)}, u32[]{:S(2)}) collective-permute-start(f32[64,512]{1,0:T(8,128)S(1)} %fusion.6), channel_id=1, source_target_pairs={{0,16},{8,24},{16,32},{24,40},{32,48},{40,56},{48,64},{56,72},{64,... | collective-permute-start | bytes 393224 | tf_op jit(solution)/shard_map/ppermute | solution.py:77
  72.4 7.7 %collective-permute-start.4 = (f32[64,512]{1,0:T(8,128)S(1)}, f32[64,512]{1,0:T(8,128)S(1)}, u32[]{:S(2)}, u32[]{:S(2)}) collective-permute-start(f32[64,512]{1,0:T(8,128)S(1)} %collective-permute-done.3), channel_id=1, source_target_pairs={{0,8},{8,0},{16,24},{24,16},{32,40},{40,32},{48,56},{56,48},{64,72... | collective-permute-start | bytes 393224 | tf_op jit(solution)/shard_map/ppermute | solution.py:77
  82.1 19.0 %copy-start.5 = (f32[256,512]{1,0:T(8,128)S(1)}, f32[256,512]{1,0:T(8,128)}, u32[]{:S(2)}) copy-start(f32[256,512]{1,0:T(8,128)} %param.10) | copy-start | bytes 1572868
  82.1 19.0 %all-to-all-start.1 = ((f32[8,64,512]{2,1,0:T(8,128)}), f32[8,64,512]{2,1,0:T(8,128)S(1)}, u32[]{:S(2)}, u32[]{:S(2)}) async-start(f32[8,64,512]{2,1,0:T(8,128)} %broadcast_in_dim.14), calls=%async_computation.1 | async-start | bytes 2097152 | tf_op jit(solution)/shard_map/all_to_all | solution.py:69
  86.2 16.6 %collective-permute-start.5 = (f32[64,512]{1,0:T(8,128)S(1)}, f32[64,512]{1,0:T(8,128)S(1)}, u32[]{:S(2)}, u32[]{:S(2)}) collective-permute-start(f32[64,512]{1,0:T(8,128)S(1)} %get-tuple-element.17), channel_id=1, source_target_pairs={{8,72},{24,88},{40,104},{56,120},{9,73},{25,89},{41,105},{57,121},... | collective-permute-start | bytes 393224 | tf_op jit(solution)/shard_map/ppermute | solution.py:77
  103.2 0.7 collective-permute-start.6
  105.0 4.9 %collective-permute-start.7 = (f32[64,512]{1,0:T(8,128)}, f32[64,512]{1,0:T(8,128)}, u32[]{:S(2)}, u32[]{:S(2)}) collective-permute-start(f32[64,512]{1,0:T(8,128)} %fusion.8), channel_id=1, source_target_pairs={{136,200},{152,216},{168,232},{184,248},{137,201},{153,217},{169,2... | collective-permute-start | bytes 393224 | tf_op jit(solution)/shard_map/ppermute | solution.py:77
  106.3 29.2 %all-to-all-start.2 = ((f32[4,256,512]{2,1,0:T(8,128)}), f32[4,256,512]{2,1,0:T(8,128)S(1)}, u32[]{:S(2)}, u32[]{:S(2)}) async-start(f32[4,256,512]{2,1,0:T(8,128)} %broadcast_in_dim.15), calls=%async_computation.2 | async-start | bytes 4194304 | tf_op jit(solution)/shard_map/all_to_all | solution.py:69
  111.3 0.7 collective-permute-start.8
  112.5 0.7 collective-permute-start.9
  113.6 0.7 collective-permute-start.10
  114.8 1.3 collective-permute-start.11
  136.5 4.6 %collective-permute-start.12 = (f32[64,512]{1,0:T(8,128)S(1)}, f32[64,512]{1,0:T(8,128)S(1)}, u32[]{:S(2)}, u32[]{:S(2)}) collective-permute-start(f32[64,512]{1,0:T(8,128)S(1)} %add.97), channel_id=1, source_target_pairs={{8,0},{24,16},{40,32},{56,48},{72,64},{88,80},{104,96},{120,112},{... | collective-permute-start | bytes 393224 | tf_op jit(solution)/shard_map/ppermute | solution.py:77
  141.6 13.0 %copy-start.1 = (f32[64,512]{1,0:T(8,128)}, f32[64,512]{1,0:T(8,128)S(1)}, u32[]{:S(2)}) copy-start(f32[64,512]{1,0:T(8,128)S(1)} %fusion.13.left_ref) | copy-start | bytes 393220
  141.6 6.6 %collective-permute-start.13 = (f32[64,512]{1,0:T(8,128)S(1)}, f32[64,512]{1,0:T(8,128)S(1)}, u32[]{:S(2)}, u32[]{:S(2)}) collective-permute-start(f32[64,512]{1,0:T(8,128)S(1)} %fusion.13.left_ref), channel_id=1, source_target_pairs={{0,4},{1,5},{2,6},{3,7},{4,0},{5,1},{6,2},{7,3},{8,12},{9,13},{10,... | collective-permute-start | bytes 393224 | tf_op jit(solution)/shard_map/ppermute | solution.py:137
  151.5 8.5 %collective-permute-start.14 = (f32[64,1024]{1,0:T(8,128)S(1)}, f32[64,1024]{1,0:T(8,128)S(1)}, u32[]{:S(2)}, u32[]{:S(2)}) collective-permute-start(f32[64,1024]{1,0:T(8,128)S(1)} %shard_map.78), channel_id=1, source_target_pairs={{0,4},{1,5},{2,6},{3,7},{4,0},{5,1},{6,2},{7,3},{8,12},{9,13},{10,... | collective-permute-start | bytes 786440 | tf_op jit(solution)/shard_map/ppermute | solution.py:139
  160.0 5.2 %collective-permute-start.15 = (f32[64,1024]{1,0:T(8,128)S(1)}, f32[64,1024]{1,0:T(8,128)S(1)}, u32[]{:S(2)}, u32[]{:S(2)}) collective-permute-start(f32[64,1024]{1,0:T(8,128)S(1)} %broadcast_select_fusion.1), channel_id=1, source_target_pairs={{0,8},{8,0},{16,24},{24,16},{32,40},{40,32},{48,56},{56,48},{64,72... | collective-permute-start | bytes 786440 | tf_op jit(solution)/shard_map/ppermute | solution.py:77
  165.9 33.6 %all-to-all-start.3 = ((f32[32,8,256]{2,1,0:T(8,128)}), f32[32,8,256]{2,1,0:T(8,128)S(1)}, u32[]{:S(2)}, u32[]{:S(2)}) async-start(f32[32,8,256]{2,1,0:T(8,128)} %bitcast.10), calls=%async_computation.3 | async-start | bytes 524288 | tf_op jit(solution)/shard_map/all_to_all | solution.py:69
  218.5 6.2 %collective-permute-start.16 = (f32[64,1024]{1,0:T(8,128)S(1)}, f32[64,1024]{1,0:T(8,128)S(1)}, u32[]{:S(2)}, u32[]{:S(2)}) collective-permute-start(f32[64,1024]{1,0:T(8,128)S(1)} %bitcast.57), channel_id=1, source_target_pairs={{0,8},{8,0},{16,24},{24,16},{32,40},{40,32},{48,56},{56,48},{64,72... | collective-permute-start | bytes 786440 | tf_op jit(solution)/shard_map/ppermute | solution.py:77
  (4 other events, 22.1 us)

commit v11 on v9

--- a/solution.py
+++ b/solution.py
@@ -13,7 +13,7 @@
 
 
 CORE_SWAP = [(p, p ^ 1) for p in range(BLOCKS)]
-TO_EVEN = [(p + 1, p) for p in range(0, BLOCKS, CORES)]
+TO_EVEN = [(device(z - 1, c, 1), device(z, c, 0)) for z in range(1, PLANES) for c in range(CHIPS)]
 NEXT_CHIP = [(p, p + CORES) for p in range(BLOCKS - CORES)]
 CORE_GROUPS = [[device(z, c, k) for z in range(PLANES) for c in range(CHIPS)] for k in range(CORES)]
 
@@ -54,6 +54,8 @@
 
     share = coupling.shape[1]
     gathered = to_all(jnp.concatenate([coupling[0], diag_inverse[0]], axis=0), "rhs", members)
+    copies = jnp.broadcast_to(border_factor[None], (ROW,) + border_factor.shape)
+    gathered, copies = lax.optimization_barrier((gathered, copies))
     link = gathered[:, :share].reshape(size, size)
     inverse = gathered[:, share:].reshape(size, size)
 
@@ -83,16 +85,16 @@
 
     arrived = permuted(own_offset, [(device(0, c, 1), device(1, c, 1)) for c in range(CHIPS)])
     own_map = to_all(window[:rows], "rhs", members).reshape(size, size)
-    own_map, copies = lax.optimization_barrier((own_map, jnp.broadcast_to(border_factor[None], (ROW,) + border_factor.shape)))
+    own_map, copies = lax.optimization_barrier((own_map, copies))
     border_near = exchanged(copies, "rhs", ROW_GROUPS)
-    start = jnp.where(plane == 1, arrived, 0.0)
+    start = arrived
     for step in range(2, PLANES):
         end = product(start, own_map) * scale + own_offset
         arrived = permuted(end, [(device(step - 1, c, 1), device(step, c, 1)) for c in range(CHIPS)])
         if step == PLANES - 1:
             arrived, border_near = lax.optimization_barrier((arrived, border_near))
-        start = jnp.where(plane == step, arrived, start)
-    start = jnp.where(even, permuted(start, TO_EVEN), start)
+        start = start + arrived
+    start = jnp.where(even, permuted(end, TO_EVEN), start)
     solved = product(start, own_map) * scale + own_offset
 
     border = border_rhs.shape[1]

time: 225 us -> 221 us (0.982)
  waiting for transfers between devices: 79.7 us -> 68.8 us
  starting transfers between devices: 97.1 us -> 106 us
    ppermute x15, starting transfers between devices: 55.5 us -> 65 us  [permuted(): return lax.ppermute(value, 'blk', pairs)]
    all_to_all x4, waiting for transfers between devices: 54.9 us -> 47.2 us  [exchanged(): return lax.all_to_all(pieces, axis, 0, 0, axis_index_groups=groups)]
  transfers between devices with their start and end apart: 21 -> 21, of which waited for: 14 -> 13; matrix products, arithmetic and copies ran while one was open for 4% -> 2% of each run, Pallas kernels for 0% -> 0%
where the time goes in v11:
time: 221 us; the launch traced here: 220 us
  starting transfers between devices  106 us (48%)
  waiting for transfers between devices  68.8 us (31%)
  blocking collectives  18.2 us (8%)
  matrix products  13.7 us (6%)
  local copies, waits for them, and re-layouts  6.07 us (3%)
  other arithmetic  5.86 us (3%)
    ppermute x15, starting transfers between devices, permuted(): return lax.ppermute(value, 'blk', pairs)  65 us
    all_to_all x4, waiting for transfers between devices, exchanged(): return lax.all_to_all(pieces, axis, 0, 0, axis_index_groups=groups)  47.2 us
    all_to_all x4, starting transfers between devices, exchanged(): return lax.all_to_all(pieces, axis, 0, 0, axis_index_groups=groups)  35.2 us
    all_to_all x1, blocking collectives, exchanged(): return lax.all_to_all(pieces, axis, 0, 0, axis_index_groups=groups)  18.2 us
    ppermute x15, waiting for transfers between devices, permuted(): return lax.ppermute(value, 'blk', pairs)  15 us
    dot_general x12, matrix products, product(): lax.dot_general(left, right, (((1,), (0,)), ((), ())), precision=lax.Prec...  8.99 us
  transfers between devices with their start and end apart: 21, of which 13 were waited for; matrix products, arithmetic and copies ran while one was open for 2% of the time, Pallas kernels for 0%

profile of v11, /device:TPU:1, one launch (start us, length us, event | category | flops | bytes accessed | tf_op | source)
XLA Modules:
  0.0 220.0 jit_solution(14914236956569705551)
XLA Ops:
  3.3 6.0 %all-to-all-start = ((f32[8,128,512]{2,1,0:T(8,128)}), f32[8,128,512]{2,1,0:T(8,128)S(1)}, u32[]{:S(2)}, u32[]{:S(2)}) async-start(f32[8,128,512]{2,1,0:T(8,128)} %broadcast_in_dim.12), calls=%async_computation | async-start | bytes 4194304 | tf_op jit(solution)/shard_map/all_to_all | solution.py:34
  9.3 25.1 %all-to-all-done = f32[8,128,512]{2,1,0:T(8,128)S(1)} async-done(((f32[8,128,512]{2,1,0:T(8,128)}), f32[8,128,512]{2,1,0:T(8,128)S(1)}, u32[]{:S(2)}, u32[]{:S(2)}) %all-to-all-start) | async-done | bytes 2097184 | tf_op jit(solution)/shard_map/all_to_all | solution.py:34
  40.6 3.7 %collective-permute-start = (f32[576,512]{1,0:T(8,128)}, f32[576,512]{1,0:T(8,128)S(1)}, u32[]{:S(2)}, u32[]{:S(2)}) collective-permute-start(f32[576,512]{1,0:T(8,128)} %pad_maximum_fusion), channel_id=1, source_target_pairs={{0,8},{8,0},{16,24},{24,16},{32,40},{40,32},{48,56},{56,48},{64,72... | collective-permute-start | bytes 3538952 | tf_op jit(solution)/shard_map/ppermute | solution.py:42
  44.4 2.6 %collective-permute-done = f32[576,512]{1,0:T(8,128)S(1)} collective-permute-done((f32[576,512]{1,0:T(8,128)}, f32[576,512]{1,0:T(8,128)S(1)}, u32[]{:S(2)}, u32[]{:S(2)}) %collective-permute-start) | collective-permute-done | bytes 1179680 | tf_op jit(solution)/shard_map/ppermute | solution.py:42
  49.5 4.2 %collective-permute-start.1 = (f32[64,512]{1,0:T(8,128)S(1)}, f32[64,512]{1,0:T(8,128)S(1)}, u32[]{:S(2)}, u32[]{:S(2)}) collective-permute-start(f32[64,512]{1,0:T(8,128)S(1)} %get-tuple-element.14), channel_id=1, source_target_pairs={{0,16},{8,24},{16,32},{24,40},{32,48},{40,56},{48,64},{56,72},{64,... | collective-permute-start | bytes 393224 | tf_op jit(solution)/shard_map/ppermute | solution.py:42
  56.7 5.0 %collective-permute-start.2 = (f32[64,512]{1,0:T(8,128)S(1)}, f32[64,512]{1,0:T(8,128)S(1)}, u32[]{:S(2)}, u32[]{:S(2)}) collective-permute-start(f32[64,512]{1,0:T(8,128)S(1)} %fusion.5), channel_id=1, source_target_pairs={{0,16},{8,24},{16,32},{24,40},{32,48},{40,56},{48,64},{56,72},{64,... | collective-permute-start | bytes 393224 | tf_op jit(solution)/shard_map/ppermute | solution.py:42
  64.3 5.5 %collective-permute-start.3 = (f32[64,512]{1,0:T(8,128)S(1)}, f32[64,512]{1,0:T(8,128)S(1)}, u32[]{:S(2)}, u32[]{:S(2)}) collective-permute-start(f32[64,512]{1,0:T(8,128)S(1)} %fusion.6), channel_id=1, source_target_pairs={{0,16},{8,24},{16,32},{24,40},{32,48},{40,56},{48,64},{56,72},{64,... | collective-permute-start | bytes 393224 | tf_op jit(solution)/shard_map/ppermute | solution.py:42
  69.8 4.3 %collective-permute-done.3 = f32[64,512]{1,0:T(8,128)S(1)} collective-permute-done((f32[64,512]{1,0:T(8,128)S(1)}, f32[64,512]{1,0:T(8,128)S(1)}, u32[]{:S(2)}, u32[]{:S(2)}) %collective-permute-start.3) | collective-permute-done | bytes 131104 | tf_op jit(solution)/shard_map/ppermute | solution.py:42
  74.2 6.7 %collective-permute-start.4 = (f32[64,512]{1,0:T(8,128)S(1)}, f32[64,512]{1,0:T(8,128)S(1)}, u32[]{:S(2)}, u32[]{:S(2)}) collective-permute-start(f32[64,512]{1,0:T(8,128)S(1)} %collective-permute-done.3), channel_id=1, source_target_pairs={{0,8},{8,0},{16,24},{24,16},{32,40},{40,32},{48,56},{56,48},{64,72... | collective-permute-start | bytes 393224 | tf_op jit(solution)/shard_map/ppermute | solution.py:42
  83.9 3.9 %all-to-all-start.1 = ((f32[8,64,512]{2,1,0:T(8,128)}), f32[8,64,512]{2,1,0:T(8,128)S(1)}, u32[]{:S(2)}, u32[]{:S(2)}) async-start(f32[8,64,512]{2,1,0:T(8,128)} %broadcast_in_dim.15), calls=%async_computation.1 | async-start | bytes 2097152 | tf_op jit(solution)/shard_map/all_to_all | solution.py:34
  87.8 11.1 %collective-permute-start.5 = (f32[64,512]{1,0:T(8,128)S(1)}, f32[64,512]{1,0:T(8,128)S(1)}, u32[]{:S(2)}, u32[]{:S(2)}) collective-permute-start(f32[64,512]{1,0:T(8,128)S(1)} %get-tuple-element.21), channel_id=1, source_target_pairs={{8,72},{24,88},{40,104},{56,120},{9,73},{25,89},{41,105},{57,121},... | collective-permute-start | bytes 393224 | tf_op jit(solution)/shard_map/ppermute | solution.py:42
  99.0 3.8 %all-to-all-done.1 = f32[8,64,512]{2,1,0:T(8,128)S(1)} async-done(((f32[8,64,512]{2,1,0:T(8,128)}), f32[8,64,512]{2,1,0:T(8,128)S(1)}, u32[]{:S(2)}, u32[]{:S(2)}) %all-to-all-start.1) | async-done | bytes 1048608 | tf_op jit(solution)/shard_map/all_to_all | solution.py:34
  106.3 3.6 %all-to-all-start.2 = ((f32[4,256,512]{2,1,0:T(8,128)}), f32[4,256,512]{2,1,0:T(8,128)S(1)}, u32[]{:S(2)}, u32[]{:S(2)}) async-start(f32[4,256,512]{2,1,0:T(8,128)} %broadcast_in_dim.13), calls=%async_computation.2 | async-start | bytes 4194304 | tf_op jit(solution)/shard_map/all_to_all | solution.py:34
  116.7 12.5 %collective-permute-start.11 = (f32[64,512]{1,0:T(8,128)}, f32[64,512]{1,0:T(8,128)}, u32[]{:S(2)}, u32[]{:S(2)}) collective-permute-start(f32[64,512]{1,0:T(8,128)} %fusion.12), channel_id=1, source_target_pairs={{8,64},{24,80},{40,96},{56,112},{72,128},{88,144},{104,160},{120,1... | collective-permute-start | bytes 393224 | tf_op jit(solution)/shard_map/ppermute | solution.py:42
  129.2 6.3 %all-to-all-done.2 = f32[4,256,512]{2,1,0:T(8,128)S(1)} async-done(((f32[4,256,512]{2,1,0:T(8,128)}), f32[4,256,512]{2,1,0:T(8,128)S(1)}, u32[]{:S(2)}, u32[]{:S(2)}) %all-to-all-start.2) | async-done | bytes 2097184 | tf_op jit(solution)/shard_map/all_to_all | solution.py:34
  137.5 3.1 %collective-permute-start.13 = (f32[64,512]{1,0:T(8,128)S(1)}, f32[64,512]{1,0:T(8,128)S(1)}, u32[]{:S(2)}, u32[]{:S(2)}) collective-permute-start(f32[64,512]{1,0:T(8,128)S(1)} %fusion.13), channel_id=1, source_target_pairs={{0,4},{1,5},{2,6},{3,7},{4,0},{5,1},{6,2},{7,3},{8,12},{9,13},{10,... | collective-permute-start | bytes 393224 | tf_op jit(solution)/shard_map/ppermute | solution.py:104
  140.6 2.6 %collective-permute-done.13 = f32[64,512]{1,0:T(8,128)S(1)} collective-permute-done((f32[64,512]{1,0:T(8,128)S(1)}, f32[64,512]{1,0:T(8,128)S(1)}, u32[]{:S(2)}, u32[]{:S(2)}) %collective-permute-start.13) | collective-permute-done | bytes 131104 | tf_op jit(solution)/shard_map/ppermute | solution.py:104
  144.3 3.1 %collective-permute-start.14 = (f32[64,1024]{1,0:T(8,128)S(1)}, f32[64,1024]{1,0:T(8,128)S(1)}, u32[]{:S(2)}, u32[]{:S(2)}) collective-permute-start(f32[64,1024]{1,0:T(8,128)S(1)} %fusion.32), channel_id=1, source_target_pairs={{0,4},{1,5},{2,6},{3,7},{4,0},{5,1},{6,2},{7,3},{8,12},{9,13},{10,... | collective-permute-start | bytes 786440 | tf_op jit(solution)/shard_map/ppermute | solution.py:106
  147.4 4.0 %collective-permute-done.14 = f32[64,1024]{1,0:T(8,128)S(1)} collective-permute-done((f32[64,1024]{1,0:T(8,128)S(1)}, f32[64,1024]{1,0:T(8,128)S(1)}, u32[]{:S(2)}, u32[]{:S(2)}) %collective-permute-start.14) | collective-permute-done | bytes 262176 | tf_op jit(solution)/shard_map/ppermute | solution.py:106
  152.5 6.0 %collective-permute-start.15 = (f32[64,1024]{1,0:T(8,128)S(1)}, f32[64,1024]{1,0:T(8,128)S(1)}, u32[]{:S(2)}, u32[]{:S(2)}) collective-permute-start(f32[64,1024]{1,0:T(8,128)S(1)} %get-tuple-element.24), channel_id=1, source_target_pairs={{0,8},{8,0},{16,24},{24,16},{32,40},{40,32},{48,56},{56,48},{64,72... | collective-permute-start | bytes 786440 | tf_op jit(solution)/shard_map/ppermute | solution.py:42
  160.3 21.6 %all-to-all-start.3 = ((f32[32,8,256]{2,1,0:T(8,128)}), f32[32,8,256]{2,1,0:T(8,128)S(1)}, u32[]{:S(2)}, u32[]{:S(2)}) async-start(f32[32,8,256]{2,1,0:T(8,128)} %bitcast.10), calls=%async_computation.3 | async-start | bytes 524288 | tf_op jit(solution)/shard_map/all_to_all | solution.py:34
  182.0 11.9 %all-to-all-done.3 = f32[32,8,256]{2,1,0:T(8,128)S(1)} async-done(((f32[32,8,256]{2,1,0:T(8,128)}), f32[32,8,256]{2,1,0:T(8,128)S(1)}, u32[]{:S(2)}, u32[]{:S(2)}) %all-to-all-start.3) | async-done | bytes 262176 | tf_op jit(solution)/shard_map/all_to_all | solution.py:34
  194.7 18.2 %all_to_all.25 = f32[32,8,256]{2,1,0:T(8,128)S(1)} all-to-all(f32[32,8,256]{2,1,0:T(8,128)S(1)} %broadcast_in_dim.16), channel_id=1, replica_groups={{0,16,32,48,64,80,96,112,128,144,160,176,192,208,224,240,256,272,288,30..., dimensions={0} | all-to-all | bytes 524288 | tf_op jit(solution)/shard_map/all_to_all | solution.py:34
  212.9 5.0 %collective-permute-start.16 = (f32[64,1024]{1,0:T(8,128)S(1)}, f32[64,1024]{1,0:T(8,128)S(1)}, u32[]{:S(2)}, u32[]{:S(2)}) collective-permute-start(f32[64,1024]{1,0:T(8,128)S(1)} %bitcast.61), channel_id=1, source_target_pairs={{0,8},{8,0},{16,24},{24,16},{32,40},{40,32},{48,56},{56,48},{64,72... | collective-permute-start | bytes 786440 | tf_op jit(solution)/shard_map/ppermute | solution.py:42
  (71 shorter events, 38.9 us)
Async XLA Ops:
  0.6 37.5 %copy-start = (f32[64,512]{1,0:T(8,128)S(1)}, f32[64,512]{1,0:T(8,128)}, u32[]{:S(2)}) copy-start(f32[64,512]{1,0:T(8,128)} %param.8) | copy-start | bytes 393220
  3.3 31.1 %copy-start.3 = (f32[256,512]{1,0:T(8,128)S(1)}, f32[256,512]{1,0:T(8,128)}, u32[]{:S(2)}) copy-start(f32[256,512]{1,0:T(8,128)} %param.10) | copy-start | bytes 1572868
  3.3 31.1 %all-to-all-start = ((f32[8,128,512]{2,1,0:T(8,128)}), f32[8,128,512]{2,1,0:T(8,128)S(1)}, u32[]{:S(2)}, u32[]{:S(2)}) async-start(f32[8,128,512]{2,1,0:T(8,128)} %broadcast_in_dim.12), calls=%async_computation | async-start | bytes 4194304 | tf_op jit(solution)/shard_map/all_to_all | solution.py:34
  40.6 6.4 %collective-permute-start = (f32[576,512]{1,0:T(8,128)}, f32[576,512]{1,0:T(8,128)S(1)}, u32[]{:S(2)}, u32[]{:S(2)}) collective-permute-start(f32[576,512]{1,0:T(8,128)} %pad_maximum_fusion), channel_id=1, source_target_pairs={{0,8},{8,0},{16,24},{24,16},{32,40},{40,32},{48,56},{56,48},{64,72... | collective-permute-start | bytes 3538952 | tf_op jit(solution)/shard_map/ppermute | solution.py:42
  49.5 6.8 %collective-permute-start.1 = (f32[64,512]{1,0:T(8,128)S(1)}, f32[64,512]{1,0:T(8,128)S(1)}, u32[]{:S(2)}, u32[]{:S(2)}) collective-permute-start(f32[64,512]{1,0:T(8,128)S(1)} %get-tuple-element.14), channel_id=1, source_target_pairs={{0,16},{8,24},{16,32},{24,40},{32,48},{40,56},{48,64},{56,72},{64,... | collective-permute-start | bytes 393224 | tf_op jit(solution)/shard_map/ppermute | solution.py:42
  56.7 7.2 %collective-permute-start.2 = (f32[64,512]{1,0:T(8,128)S(1)}, f32[64,512]{1,0:T(8,128)S(1)}, u32[]{:S(2)}, u32[]{:S(2)}) collective-permute-start(f32[64,512]{1,0:T(8,128)S(1)} %fusion.5), channel_id=1, source_target_pairs={{0,16},{8,24},{16,32},{24,40},{32,48},{40,56},{48,64},{56,72},{64,... | collective-permute-start | bytes 393224 | tf_op jit(solution)/shard_map/ppermute | solution.py:42
  64.3 9.8 %collective-permute-start.3 = (f32[64,512]{1,0:T(8,128)S(1)}, f32[64,512]{1,0:T(8,128)S(1)}, u32[]{:S(2)}, u32[]{:S(2)}) collective-permute-start(f32[64,512]{1,0:T(8,128)S(1)} %fusion.6), channel_id=1, source_target_pairs={{0,16},{8,24},{16,32},{24,40},{32,48},{40,56},{48,64},{56,72},{64,... | collective-permute-start | bytes 393224 | tf_op jit(solution)/shard_map/ppermute | solution.py:42
  74.2 7.6 %collective-permute-start.4 = (f32[64,512]{1,0:T(8,128)S(1)}, f32[64,512]{1,0:T(8,128)S(1)}, u32[]{:S(2)}, u32[]{:S(2)}) collective-permute-start(f32[64,512]{1,0:T(8,128)S(1)} %collective-permute-done.3), channel_id=1, source_target_pairs={{0,8},{8,0},{16,24},{24,16},{32,40},{40,32},{48,56},{56,48},{64,72... | collective-permute-start | bytes 393224 | tf_op jit(solution)/shard_map/ppermute | solution.py:42
  83.9 18.9 %all-to-all-start.1 = ((f32[8,64,512]{2,1,0:T(8,128)}), f32[8,64,512]{2,1,0:T(8,128)S(1)}, u32[]{:S(2)}, u32[]{:S(2)}) async-start(f32[8,64,512]{2,1,0:T(8,128)} %broadcast_in_dim.15), calls=%async_computation.1 | async-start | bytes 2097152 | tf_op jit(solution)/shard_map/all_to_all | solution.py:34
  87.8 15.0 %collective-permute-start.5 = (f32[64,512]{1,0:T(8,128)S(1)}, f32[64,512]{1,0:T(8,128)S(1)}, u32[]{:S(2)}, u32[]{:S(2)}) collective-permute-start(f32[64,512]{1,0:T(8,128)S(1)} %get-tuple-element.21), channel_id=1, source_target_pairs={{8,72},{24,88},{40,104},{56,120},{9,73},{25,89},{41,105},{57,121},... | collective-permute-start | bytes 393224 | tf_op jit(solution)/shard_map/ppermute | solution.py:42
  103.2 0.7 collective-permute-start.6
  105.0 4.9 %collective-permute-start.7 = (f32[64,512]{1,0:T(8,128)}, f32[64,512]{1,0:T(8,128)}, u32[]{:S(2)}, u32[]{:S(2)}) collective-permute-start(f32[64,512]{1,0:T(8,128)} %fusion.8), channel_id=1, source_target_pairs={{136,200},{152,216},{168,232},{184,248},{137,201},{153,217},{169,2... | collective-permute-start | bytes 393224 | tf_op jit(solution)/shard_map/ppermute | solution.py:42
  106.3 29.2 %all-to-all-start.2 = ((f32[4,256,512]{2,1,0:T(8,128)}), f32[4,256,512]{2,1,0:T(8,128)S(1)}, u32[]{:S(2)}, u32[]{:S(2)}) async-start(f32[4,256,512]{2,1,0:T(8,128)} %broadcast_in_dim.13), calls=%async_computation.2 | async-start | bytes 4194304 | tf_op jit(solution)/shard_map/all_to_all | solution.py:34
  111.3 0.7 collective-permute-start.8
  112.5 0.7 collective-permute-start.9
  113.6 0.7 collective-permute-start.10
  115.4 13.8 %collective-permute-start.12 = (f32[64,512]{1,0:T(8,128)}, f32[64,512]{1,0:T(8,128)}, u32[]{:S(2)}, u32[]{:S(2)}) collective-permute-start(f32[64,512]{1,0:T(8,128)} %fusion.12), channel_id=1, source_target_pairs={{392,456},{408,472},{424,488},{440,504},{393,457},{409,473},{425,4... | collective-permute-start | bytes 393224 | tf_op jit(solution)/shard_map/ppermute | solution.py:42
  116.7 18.8 %collective-permute-start.11 = (f32[64,512]{1,0:T(8,128)}, f32[64,512]{1,0:T(8,128)}, u32[]{:S(2)}, u32[]{:S(2)}) collective-permute-start(f32[64,512]{1,0:T(8,128)} %fusion.12), channel_id=1, source_target_pairs={{8,64},{24,80},{40,96},{56,112},{72,128},{88,144},{104,160},{120,1... | collective-permute-start | bytes 393224 | tf_op jit(solution)/shard_map/ppermute | solution.py:42
  137.5 5.7 %collective-permute-start.13 = (f32[64,512]{1,0:T(8,128)S(1)}, f32[64,512]{1,0:T(8,128)S(1)}, u32[]{:S(2)}, u32[]{:S(2)}) collective-permute-start(f32[64,512]{1,0:T(8,128)S(1)} %fusion.13), channel_id=1, source_target_pairs={{0,4},{1,5},{2,6},{3,7},{4,0},{5,1},{6,2},{7,3},{8,12},{9,13},{10,... | collective-permute-start | bytes 393224 | tf_op jit(solution)/shard_map/ppermute | solution.py:104
  143.2 8.2 %copy-start.5 = (f32[64,512]{1,0:T(8,128)S(1)}, f32[64,512]{1,0:T(8,128)}, u32[]{:S(2)}) copy-start(f32[64,512]{1,0:T(8,128)} %copy-done.4) | copy-start | bytes 393220
  144.3 7.1 %collective-permute-start.14 = (f32[64,1024]{1,0:T(8,128)S(1)}, f32[64,1024]{1,0:T(8,128)S(1)}, u32[]{:S(2)}, u32[]{:S(2)}) collective-permute-start(f32[64,1024]{1,0:T(8,128)S(1)} %fusion.32), channel_id=1, source_target_pairs={{0,4},{1,5},{2,6},{3,7},{4,0},{5,1},{6,2},{7,3},{8,12},{9,13},{10,... | collective-permute-start | bytes 786440 | tf_op jit(solution)/shard_map/ppermute | solution.py:106
  152.5 7.1 %collective-permute-start.15 = (f32[64,1024]{1,0:T(8,128)S(1)}, f32[64,1024]{1,0:T(8,128)S(1)}, u32[]{:S(2)}, u32[]{:S(2)}) collective-permute-start(f32[64,1024]{1,0:T(8,128)S(1)} %get-tuple-element.24), channel_id=1, source_target_pairs={{0,8},{8,0},{16,24},{24,16},{32,40},{40,32},{48,56},{56,48},{64,72... | collective-permute-start | bytes 786440 | tf_op jit(solution)/shard_map/ppermute | solution.py:42
  160.3 33.6 %all-to-all-start.3 = ((f32[32,8,256]{2,1,0:T(8,128)}), f32[32,8,256]{2,1,0:T(8,128)S(1)}, u32[]{:S(2)}, u32[]{:S(2)}) async-start(f32[32,8,256]{2,1,0:T(8,128)} %bitcast.10), calls=%async_computation.3 | async-start | bytes 524288 | tf_op jit(solution)/shard_map/all_to_all | solution.py:34
  212.9 6.2 %collective-permute-start.16 = (f32[64,1024]{1,0:T(8,128)S(1)}, f32[64,1024]{1,0:T(8,128)S(1)}, u32[]{:S(2)}, u32[]{:S(2)}) collective-permute-start(f32[64,1024]{1,0:T(8,128)S(1)} %bitcast.61), channel_id=1, source_target_pairs={{0,8},{8,0},{16,24},{24,16},{32,40},{40,32},{48,56},{56,48},{64,72... | collective-permute-start | bytes 786440 | tf_op jit(solution)/shard_map/ppermute | solution.py:42
  (4 other events, 10.0 us)

commit v12 on v11

--- a/solution.py
+++ b/solution.py
@@ -20,6 +20,16 @@
 ROW = 4
 ROW_GROUPS = [[0, 1, 2, 3], [4, 5, 6, 7]]
 ROW_SWAP = [(j, j ^ ROW) for j in range(2 * ROW)]
+
+
+def across_pairs(core):
+    members = 2 * ROW
+    return [
+        (device(z - 1, c, 1) * members + j, device(z, c, core) * members + (j ^ ROW))
+        for z in range(1, PLANES)
+        for c in range(CHIPS)
+        for j in range(members)
+    ]
 
 
 def product(left, right):
@@ -85,7 +95,8 @@
 
     arrived = permuted(own_offset, [(device(0, c, 1), device(1, c, 1)) for c in range(CHIPS)])
     own_map = to_all(window[:rows], "rhs", members).reshape(size, size)
-    own_map, copies = lax.optimization_barrier((own_map, copies))
+    offset_across = lax.ppermute(own_offset, "rhs", ROW_SWAP)
+    own_map, copies, offset_across = lax.optimization_barrier((own_map, copies, offset_across))
     border_near = exchanged(copies, "rhs", ROW_GROUPS)
     start = arrived
     for step in range(2, PLANES):
@@ -95,13 +106,14 @@
             arrived, border_near = lax.optimization_barrier((arrived, border_near))
         start = start + arrived
     start = jnp.where(even, permuted(end, TO_EVEN), start)
+    start_across = lax.ppermute(end, ("blk", "rhs"), across_pairs(0)) + lax.ppermute(end, ("blk", "rhs"), across_pairs(1))
     solved = product(start, own_map) * scale + own_offset
+    solved_across = product(start_across, own_map) * scale + offset_across
 
     border = border_rhs.shape[1]
     per_core, per_chip = border // CORES, border // CORES // CHIPS
     per_plane = rows // PLANES
     border_near = border_near.reshape(per_core, size)
-    solved_across = lax.ppermute(solved, "rhs", ROW_SWAP)
     near = product_transposed(solved, border_near)
     far = lax.ppermute(product_transposed(solved_across, border_near), "rhs", ROW_SWAP)
     mine = core == member // ROW

time: 221 us -> 220 us (level)
  waiting for transfers between devices: 68.8 us -> 58.5 us
  starting transfers between devices: 106 us -> 113 us
  matrix products: 13.7 us -> 16.7 us
    ppermute x1 -> x3, starting transfers between devices: 3.09 us -> 22.4 us  [the longest x1 16.7 us: body(): lax.ppermute(end, ('blk', 'rhs'), across_pairs(1))]
    ppermute x15, starting transfers between devices: 65 us -> 49.9 us  [permuted(): return lax.ppermute(value, 'blk', pairs)]
    all_to_all x4, waiting for transfers between devices: 47.2 us -> 37.7 us  [exchanged(): return lax.all_to_all(pieces, axis, 0, 0, axis_index_groups=groups)]
    dot_general x12 -> x13, matrix products: 8.99 us -> 11.1 us  [product(): lax.dot_general(left, right, (((1,), (0,)), ((), ())), precision=lax.Prec...]
  transfers between devices with their start and end apart: 21 -> 23, of which waited for: 13 -> 11; matrix products, arithmetic and copies ran while one was open for 2% -> 4% of each run, Pallas kernels for 0% -> 0%
where the time goes in v12:
time: 220 us; the launch traced here: 219 us
  starting transfers between devices  113 us (51%)
  waiting for transfers between devices  58.5 us (27%)
  blocking collectives  18.3 us (8%)
  matrix products  16.7 us (8%)
  other arithmetic  5.87 us (3%)
  local copies, waits for them, and re-layouts  5.45 us (2%)
    ppermute x15, starting transfers between devices, permuted(): return lax.ppermute(value, 'blk', pairs)  49.9 us
    all_to_all x4, waiting for transfers between devices, exchanged(): return lax.all_to_all(pieces, axis, 0, 0, axis_index_groups=groups)  37.7 us
    all_to_all x4, starting transfers between devices, exchanged(): return lax.all_to_all(pieces, axis, 0, 0, axis_index_groups=groups)  37.2 us
    all_to_all x1, blocking collectives, exchanged(): return lax.all_to_all(pieces, axis, 0, 0, axis_index_groups=groups)  18.3 us
    ppermute x1, starting transfers between devices, body(): lax.ppermute(end, ('blk', 'rhs'), across_pairs(1))  16.7 us
    ppermute x15, waiting for transfers between devices, permuted(): return lax.ppermute(value, 'blk', pairs)  15.3 us
    dot_general x13, matrix products, product(): lax.dot_general(left, right, (((1,), (0,)), ((), ())), precision=lax.Prec...  11.1 us
  transfers between devices with their start and end apart: 23, of which 11 were waited for; matrix products, arithmetic and copies ran while one was open for 4% of the time, Pallas kernels for 0%

profile of v12, /device:TPU:1, one launch (start us, length us, event | category | flops | bytes accessed | tf_op | source)
XLA Modules:
  0.0 218.7 jit_solution(15731173704949116540)
XLA Ops:
  3.3 6.0 %all-to-all-start = ((f32[8,128,512]{2,1,0:T(8,128)}), f32[8,128,512]{2,1,0:T(8,128)S(1)}, u32[]{:S(2)}, u32[]{:S(2)}) async-start(f32[8,128,512]{2,1,0:T(8,128)} %broadcast_in_dim.12), calls=%async_computation | async-start | bytes 4194304 | tf_op jit(solution)/shard_map/all_to_all | solution.py:44
  9.3 25.1 %all-to-all-done = f32[8,128,512]{2,1,0:T(8,128)S(1)} async-done(((f32[8,128,512]{2,1,0:T(8,128)}), f32[8,128,512]{2,1,0:T(8,128)S(1)}, u32[]{:S(2)}, u32[]{:S(2)}) %all-to-all-start) | async-done | bytes 2097184 | tf_op jit(solution)/shard_map/all_to_all | solution.py:44
  40.7 3.8 %collective-permute-start = (f32[576,512]{1,0:T(8,128)}, f32[576,512]{1,0:T(8,128)S(1)}, u32[]{:S(2)}, u32[]{:S(2)}) collective-permute-start(f32[576,512]{1,0:T(8,128)} %pad_maximum_fusion), channel_id=1, source_target_pairs={{0,8},{8,0},{16,24},{24,16},{32,40},{40,32},{48,56},{56,48},{64,72... | collective-permute-start | bytes 3538952 | tf_op jit(solution)/shard_map/ppermute | solution.py:52
  44.4 2.6 %collective-permute-done = f32[576,512]{1,0:T(8,128)S(1)} collective-permute-done((f32[576,512]{1,0:T(8,128)}, f32[576,512]{1,0:T(8,128)S(1)}, u32[]{:S(2)}, u32[]{:S(2)}) %collective-permute-start) | collective-permute-done | bytes 1179680 | tf_op jit(solution)/shard_map/ppermute | solution.py:52
  47.3 2.0 fusion
  49.5 4.2 %collective-permute-start.1 = (f32[64,512]{1,0:T(8,128)S(1)}, f32[64,512]{1,0:T(8,128)S(1)}, u32[]{:S(2)}, u32[]{:S(2)}) collective-permute-start(f32[64,512]{1,0:T(8,128)S(1)} %get-tuple-element.16), channel_id=1, source_target_pairs={{0,16},{8,24},{16,32},{24,40},{32,48},{40,56},{48,64},{56,72},{64,... | collective-permute-start | bytes 393224 | tf_op jit(solution)/shard_map/ppermute | solution.py:52
  53.7 2.5 %collective-permute-done.1 = f32[64,512]{1,0:T(8,128)S(1)} collective-permute-done((f32[64,512]{1,0:T(8,128)S(1)}, f32[64,512]{1,0:T(8,128)S(1)}, u32[]{:S(2)}, u32[]{:S(2)}) %collective-permute-start.1) | collective-permute-done | bytes 131104 | tf_op jit(solution)/shard_map/ppermute | solution.py:52
  56.7 5.0 %collective-permute-start.2 = (f32[64,512]{1,0:T(8,128)S(1)}, f32[64,512]{1,0:T(8,128)S(1)}, u32[]{:S(2)}, u32[]{:S(2)}) collective-permute-start(f32[64,512]{1,0:T(8,128)S(1)} %fusion.5), channel_id=1, source_target_pairs={{0,16},{8,24},{16,32},{24,40},{32,48},{40,56},{48,64},{56,72},{64,... | collective-permute-start | bytes 393224 | tf_op jit(solution)/shard_map/ppermute | solution.py:52
  61.7 2.2 %collective-permute-done.2 = f32[64,512]{1,0:T(8,128)S(1)} collective-permute-done((f32[64,512]{1,0:T(8,128)S(1)}, f32[64,512]{1,0:T(8,128)S(1)}, u32[]{:S(2)}, u32[]{:S(2)}) %collective-permute-start.2) | collective-permute-done | bytes 131104 | tf_op jit(solution)/shard_map/ppermute | solution.py:52
  64.3 5.5 %collective-permute-start.3 = (f32[64,512]{1,0:T(8,128)S(1)}, f32[64,512]{1,0:T(8,128)S(1)}, u32[]{:S(2)}, u32[]{:S(2)}) collective-permute-start(f32[64,512]{1,0:T(8,128)S(1)} %fusion.6), channel_id=1, source_target_pairs={{0,16},{8,24},{16,32},{24,40},{32,48},{40,56},{48,64},{56,72},{64,... | collective-permute-start | bytes 393224 | tf_op jit(solution)/shard_map/ppermute | solution.py:52
  69.9 4.3 %collective-permute-done.3 = f32[64,512]{1,0:T(8,128)S(1)} collective-permute-done((f32[64,512]{1,0:T(8,128)S(1)}, f32[64,512]{1,0:T(8,128)S(1)}, u32[]{:S(2)}, u32[]{:S(2)}) %collective-permute-start.3) | collective-permute-done | bytes 131104 | tf_op jit(solution)/shard_map/ppermute | solution.py:52
  74.2 6.7 %collective-permute-start.4 = (f32[64,512]{1,0:T(8,128)S(1)}, f32[64,512]{1,0:T(8,128)S(1)}, u32[]{:S(2)}, u32[]{:S(2)}) collective-permute-start(f32[64,512]{1,0:T(8,128)S(1)} %collective-permute-done.3), channel_id=1, source_target_pairs={{0,8},{8,0},{16,24},{24,16},{32,40},{40,32},{48,56},{56,48},{64,72... | collective-permute-start | bytes 393224 | tf_op jit(solution)/shard_map/ppermute | solution.py:52
  83.9 3.9 %all-to-all-start.1 = ((f32[8,64,512]{2,1,0:T(8,128)}), f32[8,64,512]{2,1,0:T(8,128)S(1)}, u32[]{:S(2)}, u32[]{:S(2)}) async-start(f32[8,64,512]{2,1,0:T(8,128)} %broadcast_in_dim.15), calls=%async_computation.1 | async-start | bytes 2097152 | tf_op jit(solution)/shard_map/all_to_all | solution.py:44
  87.9 3.7 %collective-permute-start.6 = (f32[64,512]{1,0:T(8,128)S(1)}, f32[64,512]{1,0:T(8,128)S(1)}, u32[]{:S(2)}, u32[]{:S(2)}) collective-permute-start(f32[64,512]{1,0:T(8,128)S(1)} %get-tuple-element.23), channel_id=1, source_target_pairs={{0,4},{1,5},{2,6},{3,7},{4,0},{5,1},{6,2},{7,3},{8,12},{9,13},{10,... | collective-permute-start | bytes 393224 | tf_op jit(solution)/shard_map/ppermute | solution.py:98
  91.6 10.8 %collective-permute-start.5 = (f32[64,512]{1,0:T(8,128)S(1)}, f32[64,512]{1,0:T(8,128)S(1)}, u32[]{:S(2)}, u32[]{:S(2)}) collective-permute-start(f32[64,512]{1,0:T(8,128)S(1)} %get-tuple-element.23), channel_id=1, source_target_pairs={{8,72},{24,88},{40,104},{56,120},{9,73},{25,89},{41,105},{57,121},... | collective-permute-start | bytes 393224 | tf_op jit(solution)/shard_map/ppermute | solution.py:52
  108.0 3.8 %all-to-all-start.2 = ((f32[4,256,512]{2,1,0:T(8,128)}), f32[4,256,512]{2,1,0:T(8,128)S(1)}, u32[]{:S(2)}, u32[]{:S(2)}) async-start(f32[4,256,512]{2,1,0:T(8,128)} %broadcast_in_dim.13), calls=%async_computation.2 | async-start | bytes 4194304 | tf_op jit(solution)/shard_map/all_to_all | solution.py:44
  117.3 16.7 %collective-permute-start.15 = (f32[64,512]{1,0:T(8,128)}, f32[64,512]{1,0:T(8,128)}, u32[]{:S(2)}, u32[]{:S(2)}) collective-permute-start(f32[64,512]{1,0:T(8,128)} %fusion.12), channel_id=1, source_target_pairs={{8,76},{9,77},{10,78},{11,79},{12,72},{13,73},{14,74},{15,75},{24,... | collective-permute-start | bytes 393224 | tf_op jit(solution)/shard_map/ppermute | solution.py:109
  139.2 2.1 fusion.14
  143.3 3.3 %collective-permute-start.16 = (f32[64,1024]{1,0:T(8,128)S(1)}, f32[64,1024]{1,0:T(8,128)S(1)}, u32[]{:S(2)}, u32[]{:S(2)}) collective-permute-start(f32[64,1024]{1,0:T(8,128)S(1)} %fusion.34), channel_id=1, source_target_pairs={{0,4},{1,5},{2,6},{3,7},{4,0},{5,1},{6,2},{7,3},{8,12},{9,13},{10,... | collective-permute-start | bytes 786440 | tf_op jit(solution)/shard_map/ppermute | solution.py:118
  148.1 3.4 %collective-permute-done.16 = f32[64,1024]{1,0:T(8,128)S(1)} collective-permute-done((f32[64,1024]{1,0:T(8,128)S(1)}, f32[64,1024]{1,0:T(8,128)S(1)}, u32[]{:S(2)}, u32[]{:S(2)}) %collective-permute-start.16) | collective-permute-done | bytes 262176 | tf_op jit(solution)/shard_map/ppermute | solution.py:118
  156.7 23.4 %all-to-all-start.3 = ((f32[32,8,256]{2,1,0:T(8,128)}), f32[32,8,256]{2,1,0:T(8,128)S(1)}, u32[]{:S(2)}, u32[]{:S(2)}) async-start(f32[32,8,256]{2,1,0:T(8,128)} %bitcast.10), calls=%async_computation.3 | async-start | bytes 524288 | tf_op jit(solution)/shard_map/all_to_all | solution.py:44
  180.2 12.6 %all-to-all-done.3 = f32[32,8,256]{2,1,0:T(8,128)S(1)} async-done(((f32[32,8,256]{2,1,0:T(8,128)}), f32[32,8,256]{2,1,0:T(8,128)S(1)}, u32[]{:S(2)}, u32[]{:S(2)}) %all-to-all-start.3) | async-done | bytes 262176 | tf_op jit(solution)/shard_map/all_to_all | solution.py:44
  193.6 18.3 %all_to_all.25 = f32[32,8,256]{2,1,0:T(8,128)S(1)} all-to-all(f32[32,8,256]{2,1,0:T(8,128)S(1)} %broadcast_in_dim.16), channel_id=1, replica_groups={{0,16,32,48,64,80,96,112,128,144,160,176,192,208,224,240,256,272,288,30..., dimensions={0} | all-to-all | bytes 524288 | tf_op jit(solution)/shard_map/all_to_all | solution.py:44
  211.9 4.8 %collective-permute-start.18 = (f32[64,1024]{1,0:T(8,128)S(1)}, f32[64,1024]{1,0:T(8,128)S(1)}, u32[]{:S(2)}, u32[]{:S(2)}) collective-permute-start(f32[64,1024]{1,0:T(8,128)S(1)} %bitcast.63), channel_id=1, source_target_pairs={{0,8},{8,0},{16,24},{24,16},{32,40},{40,32},{48,56},{56,48},{64,72... | collective-permute-start | bytes 786440 | tf_op jit(solution)/shard_map/ppermute | solution.py:52
  (76 shorter events, 40.6 us)
Async XLA Ops:
  0.6 37.5 %copy-start = (f32[64,512]{1,0:T(8,128)S(1)}, f32[64,512]{1,0:T(8,128)}, u32[]{:S(2)}) copy-start(f32[64,512]{1,0:T(8,128)} %param.8) | copy-start | bytes 393220
  3.3 31.1 %all-to-all-start = ((f32[8,128,512]{2,1,0:T(8,128)}), f32[8,128,512]{2,1,0:T(8,128)S(1)}, u32[]{:S(2)}, u32[]{:S(2)}) async-start(f32[8,128,512]{2,1,0:T(8,128)} %broadcast_in_dim.12), calls=%async_computation | async-start | bytes 4194304 | tf_op jit(solution)/shard_map/all_to_all | solution.py:44
  40.7 6.4 %collective-permute-start = (f32[576,512]{1,0:T(8,128)}, f32[576,512]{1,0:T(8,128)S(1)}, u32[]{:S(2)}, u32[]{:S(2)}) collective-permute-start(f32[576,512]{1,0:T(8,128)} %pad_maximum_fusion), channel_id=1, source_target_pairs={{0,8},{8,0},{16,24},{24,16},{32,40},{40,32},{48,56},{56,48},{64,72... | collective-permute-start | bytes 3538952 | tf_op jit(solution)/shard_map/ppermute | solution.py:52
  49.5 6.7 %collective-permute-start.1 = (f32[64,512]{1,0:T(8,128)S(1)}, f32[64,512]{1,0:T(8,128)S(1)}, u32[]{:S(2)}, u32[]{:S(2)}) collective-permute-start(f32[64,512]{1,0:T(8,128)S(1)} %get-tuple-element.16), channel_id=1, source_target_pairs={{0,16},{8,24},{16,32},{24,40},{32,48},{40,56},{48,64},{56,72},{64,... | collective-permute-start | bytes 393224 | tf_op jit(solution)/shard_map/ppermute | solution.py:52
  56.7 7.2 %collective-permute-start.2 = (f32[64,512]{1,0:T(8,128)S(1)}, f32[64,512]{1,0:T(8,128)S(1)}, u32[]{:S(2)}, u32[]{:S(2)}) collective-permute-start(f32[64,512]{1,0:T(8,128)S(1)} %fusion.5), channel_id=1, source_target_pairs={{0,16},{8,24},{16,32},{24,40},{32,48},{40,56},{48,64},{56,72},{64,... | collective-permute-start | bytes 393224 | tf_op jit(solution)/shard_map/ppermute | solution.py:52
  64.3 9.8 %collective-permute-start.3 = (f32[64,512]{1,0:T(8,128)S(1)}, f32[64,512]{1,0:T(8,128)S(1)}, u32[]{:S(2)}, u32[]{:S(2)}) collective-permute-start(f32[64,512]{1,0:T(8,128)S(1)} %fusion.6), channel_id=1, source_target_pairs={{0,16},{8,24},{16,32},{24,40},{32,48},{40,56},{48,64},{56,72},{64,... | collective-permute-start | bytes 393224 | tf_op jit(solution)/shard_map/ppermute | solution.py:52
  74.2 7.7 %collective-permute-start.4 = (f32[64,512]{1,0:T(8,128)S(1)}, f32[64,512]{1,0:T(8,128)S(1)}, u32[]{:S(2)}, u32[]{:S(2)}) collective-permute-start(f32[64,512]{1,0:T(8,128)S(1)} %collective-permute-done.3), channel_id=1, source_target_pairs={{0,8},{8,0},{16,24},{24,16},{32,40},{40,32},{48,56},{56,48},{64,72... | collective-permute-start | bytes 393224 | tf_op jit(solution)/shard_map/ppermute | solution.py:52
  83.9 20.5 %all-to-all-start.1 = ((f32[8,64,512]{2,1,0:T(8,128)}), f32[8,64,512]{2,1,0:T(8,128)S(1)}, u32[]{:S(2)}, u32[]{:S(2)}) async-start(f32[8,64,512]{2,1,0:T(8,128)} %broadcast_in_dim.15), calls=%async_computation.1 | async-start | bytes 2097152 | tf_op jit(solution)/shard_map/all_to_all | solution.py:44
  87.9 16.6 %collective-permute-start.6 = (f32[64,512]{1,0:T(8,128)S(1)}, f32[64,512]{1,0:T(8,128)S(1)}, u32[]{:S(2)}, u32[]{:S(2)}) collective-permute-start(f32[64,512]{1,0:T(8,128)S(1)} %get-tuple-element.23), channel_id=1, source_target_pairs={{0,4},{1,5},{2,6},{3,7},{4,0},{5,1},{6,2},{7,3},{8,12},{9,13},{10,... | collective-permute-start | bytes 393224 | tf_op jit(solution)/shard_map/ppermute | solution.py:98
  91.6 12.9 %collective-permute-start.5 = (f32[64,512]{1,0:T(8,128)S(1)}, f32[64,512]{1,0:T(8,128)S(1)}, u32[]{:S(2)}, u32[]{:S(2)}) collective-permute-start(f32[64,512]{1,0:T(8,128)S(1)} %get-tuple-element.23), channel_id=1, source_target_pairs={{8,72},{24,88},{40,104},{56,120},{9,73},{25,89},{41,105},{57,121},... | collective-permute-start | bytes 393224 | tf_op jit(solution)/shard_map/ppermute | solution.py:52
  104.9 0.7 collective-permute-start.7
  106.7 5.1 %collective-permute-start.8 = (f32[64,512]{1,0:T(8,128)}, f32[64,512]{1,0:T(8,128)}, u32[]{:S(2)}, u32[]{:S(2)}) collective-permute-start(f32[64,512]{1,0:T(8,128)} %fusion.8), channel_id=1, source_target_pairs={{136,200},{152,216},{168,232},{184,248},{137,201},{153,217},{169,2... | collective-permute-start | bytes 393224 | tf_op jit(solution)/shard_map/ppermute | solution.py:52
  108.0 33.4 %all-to-all-start.2 = ((f32[4,256,512]{2,1,0:T(8,128)}), f32[4,256,512]{2,1,0:T(8,128)S(1)}, u32[]{:S(2)}, u32[]{:S(2)}) async-start(f32[4,256,512]{2,1,0:T(8,128)} %broadcast_in_dim.13), calls=%async_computation.2 | async-start | bytes 4194304 | tf_op jit(solution)/shard_map/all_to_all | solution.py:44
  113.2 0.7 collective-permute-start.9
  114.3 0.7 collective-permute-start.10
  115.5 0.7 collective-permute-start.11
  117.3 21.9 %collective-permute-start.15 = (f32[64,512]{1,0:T(8,128)}, f32[64,512]{1,0:T(8,128)}, u32[]{:S(2)}, u32[]{:S(2)}) collective-permute-start(f32[64,512]{1,0:T(8,128)} %fusion.12), channel_id=1, source_target_pairs={{8,76},{9,77},{10,78},{11,79},{12,72},{13,73},{14,74},{15,75},{24,... | collective-permute-start | bytes 393224 | tf_op jit(solution)/shard_map/ppermute | solution.py:109
  134.0 5.2 %collective-permute-start.14 = (f32[64,512]{1,0:T(8,128)}, f32[64,512]{1,0:T(8,128)}, u32[]{:S(2)}, u32[]{:S(2)}) collective-permute-start(f32[64,512]{1,0:T(8,128)} %fusion.12), channel_id=1, source_target_pairs={{8,68},{9,69},{10,70},{11,71},{12,64},{13,65},{14,66},{15,67},{24,... | collective-permute-start | bytes 393224 | tf_op jit(solution)/shard_map/ppermute | solution.py:109
  136.0 5.4 %collective-permute-start.13 = (f32[64,512]{1,0:T(8,128)}, f32[64,512]{1,0:T(8,128)}, u32[]{:S(2)}, u32[]{:S(2)}) collective-permute-start(f32[64,512]{1,0:T(8,128)} %fusion.12), channel_id=1, source_target_pairs={{392,456},{408,472},{424,488},{440,504},{393,457},{409,473},{425,4... | collective-permute-start | bytes 393224 | tf_op jit(solution)/shard_map/ppermute | solution.py:52
  137.3 9.4 %collective-permute-start.12 = (f32[64,512]{1,0:T(8,128)}, f32[64,512]{1,0:T(8,128)}, u32[]{:S(2)}, u32[]{:S(2)}) collective-permute-start(f32[64,512]{1,0:T(8,128)} %fusion.12), channel_id=1, source_target_pairs={{8,64},{24,80},{40,96},{56,112},{72,128},{88,144},{104,160},{120,1... | collective-permute-start | bytes 393224 | tf_op jit(solution)/shard_map/ppermute | solution.py:52
  143.3 8.1 %collective-permute-start.16 = (f32[64,1024]{1,0:T(8,128)S(1)}, f32[64,1024]{1,0:T(8,128)S(1)}, u32[]{:S(2)}, u32[]{:S(2)}) collective-permute-start(f32[64,1024]{1,0:T(8,128)S(1)} %fusion.34), channel_id=1, source_target_pairs={{0,4},{1,5},{2,6},{3,7},{4,0},{5,1},{6,2},{7,3},{8,12},{9,13},{10,... | collective-permute-start | bytes 786440 | tf_op jit(solution)/shard_map/ppermute | solution.py:118
  152.6 3.4 %collective-permute-start.17 = (f32[64,1024]{1,0:T(8,128)S(1)}, f32[64,1024]{1,0:T(8,128)S(1)}, u32[]{:S(2)}, u32[]{:S(2)}) collective-permute-start(f32[64,1024]{1,0:T(8,128)S(1)} %get-tuple-element.26), channel_id=1, source_target_pairs={{0,8},{8,0},{16,24},{24,16},{32,40},{40,32},{48,56},{56,48},{64,72... | collective-permute-start | bytes 786440 | tf_op jit(solution)/shard_map/ppermute | solution.py:52
  156.7 36.1 %all-to-all-start.3 = ((f32[32,8,256]{2,1,0:T(8,128)}), f32[32,8,256]{2,1,0:T(8,128)S(1)}, u32[]{:S(2)}, u32[]{:S(2)}) async-start(f32[32,8,256]{2,1,0:T(8,128)} %bitcast.10), calls=%async_computation.3 | async-start | bytes 524288 | tf_op jit(solution)/shard_map/all_to_all | solution.py:44
  211.9 5.9 %collective-permute-start.18 = (f32[64,1024]{1,0:T(8,128)S(1)}, f32[64,1024]{1,0:T(8,128)S(1)}, u32[]{:S(2)}, u32[]{:S(2)}) collective-permute-start(f32[64,1024]{1,0:T(8,128)S(1)} %bitcast.63), channel_id=1, source_target_pairs={{0,8},{8,0},{16,24},{24,16},{32,40},{40,32},{48,56},{56,48},{64,72... | collective-permute-start | bytes 786440 | tf_op jit(solution)/shard_map/ppermute | solution.py:52
  (6 other events, 47.3 us)

commit v13 on v12

--- a/solution.py
+++ b/solution.py
@@ -63,7 +63,9 @@
     even = core == 0
 
     share = coupling.shape[1]
-    gathered = to_all(jnp.concatenate([coupling[0], diag_inverse[0]], axis=0), "rhs", members)
+    gathered = exchanged(
+        jnp.concatenate([jnp.broadcast_to(part, (members,) + part.shape[1:]) for part in (coupling, diag_inverse)], axis=1), "rhs"
+    )
     copies = jnp.broadcast_to(border_factor[None], (ROW,) + border_factor.shape)
     gathered, copies = lax.optimization_barrier((gathered, copies))
     link = gathered[:, :share].reshape(size, size)

time: 220 us -> 219 us (level)
  no operation moved by 1% of the time
where the time goes in v13:
time: 219 us; the launch traced here: 218 us
  starting transfers between devices  112 us (51%)
  waiting for transfers between devices  58.7 us (27%)
  blocking collectives  18.3 us (8%)
  matrix products  16.7 us (8%)
  other arithmetic  6.38 us (3%)
  local copies, waits for them, and re-layouts  5.02 us (2%)
    ppermute x15, starting transfers between devices, permuted(): return lax.ppermute(value, 'blk', pairs)  49.9 us
    all_to_all x4, waiting for transfers between devices, exchanged(): return lax.all_to_all(pieces, axis, 0, 0, axis_index_groups=groups)  37.8 us
    all_to_all x4, starting transfers between devices, exchanged(): return lax.all_to_all(pieces, axis, 0, 0, axis_index_groups=groups)  36.8 us
    all_to_all x1, blocking collectives, exchanged(): return lax.all_to_all(pieces, axis, 0, 0, axis_index_groups=groups)  18.3 us
    ppermute x1, starting transfers between devices, body(): lax.ppermute(end, ('blk', 'rhs'), across_pairs(1))  16.5 us
    ppermute x15, waiting for transfers between devices, permuted(): return lax.ppermute(value, 'blk', pairs)  15.3 us
    dot_general x13, matrix products, product(): lax.dot_general(left, right, (((1,), (0,)), ((), ())), precision=lax.Prec...  11.2 us
  transfers between devices with their start and end apart: 23, of which 11 were waited for; matrix products, arithmetic and copies ran while one was open for 4% of the time, Pallas kernels for 0%

profile of v13, /device:TPU:1, one launch (start us, length us, event | category | flops | bytes accessed | tf_op | source)
XLA Modules:
  0.0 218.4 jit_solution(10392464562052297800)
XLA Ops:
  3.4 6.0 %all-to-all-start = ((f32[8,128,512]{2,1,0:T(8,128)}), f32[8,128,512]{2,1,0:T(8,128)S(1)}, u32[]{:S(2)}, u32[]{:S(2)}) async-start(f32[8,128,512]{2,1,0:T(8,128)} %pad_maximum_fusion), calls=%async_computation | async-start | bytes 4194304 | tf_op jit(solution)/shard_map/all_to_all | solution.py:44
  9.4 25.1 %all-to-all-done = f32[8,128,512]{2,1,0:T(8,128)S(1)} async-done(((f32[8,128,512]{2,1,0:T(8,128)}), f32[8,128,512]{2,1,0:T(8,128)S(1)}, u32[]{:S(2)}, u32[]{:S(2)}) %all-to-all-start) | async-done | bytes 2097184 | tf_op jit(solution)/shard_map/all_to_all | solution.py:44
  40.8 3.7 %collective-permute-start = (f32[576,512]{1,0:T(8,128)}, f32[576,512]{1,0:T(8,128)S(1)}, u32[]{:S(2)}, u32[]{:S(2)}) collective-permute-start(f32[576,512]{1,0:T(8,128)} %pad_maximum_fusion.1), channel_id=1, source_target_pairs={{0,8},{8,0},{16,24},{24,16},{32,40},{40,32},{48,56},{56,48},{64,72... | collective-permute-start | bytes 3538952 | tf_op jit(solution)/shard_map/ppermute | solution.py:52
  44.6 2.6 %collective-permute-done = f32[576,512]{1,0:T(8,128)S(1)} collective-permute-done((f32[576,512]{1,0:T(8,128)}, f32[576,512]{1,0:T(8,128)S(1)}, u32[]{:S(2)}, u32[]{:S(2)}) %collective-permute-start) | collective-permute-done | bytes 1179680 | tf_op jit(solution)/shard_map/ppermute | solution.py:52
  47.5 2.1 fusion
  49.6 4.2 %collective-permute-start.1 = (f32[64,512]{1,0:T(8,128)S(1)}, f32[64,512]{1,0:T(8,128)S(1)}, u32[]{:S(2)}, u32[]{:S(2)}) collective-permute-start(f32[64,512]{1,0:T(8,128)S(1)} %get-tuple-element.16), channel_id=1, source_target_pairs={{0,16},{8,24},{16,32},{24,40},{32,48},{40,56},{48,64},{56,72},{64,... | collective-permute-start | bytes 393224 | tf_op jit(solution)/shard_map/ppermute | solution.py:52
  53.9 2.5 %collective-permute-done.1 = f32[64,512]{1,0:T(8,128)S(1)} collective-permute-done((f32[64,512]{1,0:T(8,128)S(1)}, f32[64,512]{1,0:T(8,128)S(1)}, u32[]{:S(2)}, u32[]{:S(2)}) %collective-permute-start.1) | collective-permute-done | bytes 131104 | tf_op jit(solution)/shard_map/ppermute | solution.py:52
  56.8 5.0 %collective-permute-start.2 = (f32[64,512]{1,0:T(8,128)S(1)}, f32[64,512]{1,0:T(8,128)S(1)}, u32[]{:S(2)}, u32[]{:S(2)}) collective-permute-start(f32[64,512]{1,0:T(8,128)S(1)} %fusion.5), channel_id=1, source_target_pairs={{0,16},{8,24},{16,32},{24,40},{32,48},{40,56},{48,64},{56,72},{64,... | collective-permute-start | bytes 393224 | tf_op jit(solution)/shard_map/ppermute | solution.py:52
  61.8 2.3 %collective-permute-done.2 = f32[64,512]{1,0:T(8,128)S(1)} collective-permute-done((f32[64,512]{1,0:T(8,128)S(1)}, f32[64,512]{1,0:T(8,128)S(1)}, u32[]{:S(2)}, u32[]{:S(2)}) %collective-permute-start.2) | collective-permute-done | bytes 131104 | tf_op jit(solution)/shard_map/ppermute | solution.py:52
  64.5 5.4 %collective-permute-start.3 = (f32[64,512]{1,0:T(8,128)S(1)}, f32[64,512]{1,0:T(8,128)S(1)}, u32[]{:S(2)}, u32[]{:S(2)}) collective-permute-start(f32[64,512]{1,0:T(8,128)S(1)} %fusion.6), channel_id=1, source_target_pairs={{0,16},{8,24},{16,32},{24,40},{32,48},{40,56},{48,64},{56,72},{64,... | collective-permute-start | bytes 393224 | tf_op jit(solution)/shard_map/ppermute | solution.py:52
  69.9 4.3 %collective-permute-done.3 = f32[64,512]{1,0:T(8,128)S(1)} collective-permute-done((f32[64,512]{1,0:T(8,128)S(1)}, f32[64,512]{1,0:T(8,128)S(1)}, u32[]{:S(2)}, u32[]{:S(2)}) %collective-permute-start.3) | collective-permute-done | bytes 131104 | tf_op jit(solution)/shard_map/ppermute | solution.py:52
  74.2 6.8 %collective-permute-start.4 = (f32[64,512]{1,0:T(8,128)S(1)}, f32[64,512]{1,0:T(8,128)S(1)}, u32[]{:S(2)}, u32[]{:S(2)}) collective-permute-start(f32[64,512]{1,0:T(8,128)S(1)} %collective-permute-done.3), channel_id=1, source_target_pairs={{0,8},{8,0},{16,24},{24,16},{32,40},{40,32},{48,56},{56,48},{64,72... | collective-permute-start | bytes 393224 | tf_op jit(solution)/shard_map/ppermute | solution.py:52
  84.0 4.0 %all-to-all-start.1 = ((f32[8,64,512]{2,1,0:T(8,128)}), f32[8,64,512]{2,1,0:T(8,128)S(1)}, u32[]{:S(2)}, u32[]{:S(2)}) async-start(f32[8,64,512]{2,1,0:T(8,128)} %broadcast_in_dim.42), calls=%async_computation.1 | async-start | bytes 2097152 | tf_op jit(solution)/shard_map/all_to_all | solution.py:44
  88.0 3.7 %collective-permute-start.6 = (f32[64,512]{1,0:T(8,128)S(1)}, f32[64,512]{1,0:T(8,128)S(1)}, u32[]{:S(2)}, u32[]{:S(2)}) collective-permute-start(f32[64,512]{1,0:T(8,128)S(1)} %get-tuple-element.23), channel_id=1, source_target_pairs={{0,4},{1,5},{2,6},{3,7},{4,0},{5,1},{6,2},{7,3},{8,12},{9,13},{10,... | collective-permute-start | bytes 393224 | tf_op jit(solution)/shard_map/ppermute | solution.py:100
  91.7 10.8 %collective-permute-start.5 = (f32[64,512]{1,0:T(8,128)S(1)}, f32[64,512]{1,0:T(8,128)S(1)}, u32[]{:S(2)}, u32[]{:S(2)}) collective-permute-start(f32[64,512]{1,0:T(8,128)S(1)} %get-tuple-element.23), channel_id=1, source_target_pairs={{8,72},{24,88},{40,104},{56,120},{9,73},{25,89},{41,105},{57,121},... | collective-permute-start | bytes 393224 | tf_op jit(solution)/shard_map/ppermute | solution.py:52
  108.1 3.9 %all-to-all-start.2 = ((f32[4,256,512]{2,1,0:T(8,128)}), f32[4,256,512]{2,1,0:T(8,128)S(1)}, u32[]{:S(2)}, u32[]{:S(2)}) async-start(f32[4,256,512]{2,1,0:T(8,128)} %broadcast_in_dim.40), calls=%async_computation.2 | async-start | bytes 4194304 | tf_op jit(solution)/shard_map/all_to_all | solution.py:44
  117.4 16.5 %collective-permute-start.15 = (f32[64,512]{1,0:T(8,128)}, f32[64,512]{1,0:T(8,128)}, u32[]{:S(2)}, u32[]{:S(2)}) collective-permute-start(f32[64,512]{1,0:T(8,128)} %fusion.12), channel_id=1, source_target_pairs={{8,76},{9,77},{10,78},{11,79},{12,72},{13,73},{14,74},{15,75},{24,... | collective-permute-start | bytes 393224 | tf_op jit(solution)/shard_map/ppermute | solution.py:111
  139.1 2.1 fusion.14
  143.3 3.3 %collective-permute-start.16 = (f32[64,1024]{1,0:T(8,128)S(1)}, f32[64,1024]{1,0:T(8,128)S(1)}, u32[]{:S(2)}, u32[]{:S(2)}) collective-permute-start(f32[64,1024]{1,0:T(8,128)S(1)} %fusion.34), channel_id=1, source_target_pairs={{0,4},{1,5},{2,6},{3,7},{4,0},{5,1},{6,2},{7,3},{8,12},{9,13},{10,... | collective-permute-start | bytes 786440 | tf_op jit(solution)/shard_map/ppermute | solution.py:120
  148.0 3.6 %collective-permute-done.16 = f32[64,1024]{1,0:T(8,128)S(1)} collective-permute-done((f32[64,1024]{1,0:T(8,128)S(1)}, f32[64,1024]{1,0:T(8,128)S(1)}, u32[]{:S(2)}, u32[]{:S(2)}) %collective-permute-start.16) | collective-permute-done | bytes 262176 | tf_op jit(solution)/shard_map/ppermute | solution.py:120
  156.9 22.9 %all-to-all-start.3 = ((f32[32,8,256]{2,1,0:T(8,128)}), f32[32,8,256]{2,1,0:T(8,128)S(1)}, u32[]{:S(2)}, u32[]{:S(2)}) async-start(f32[32,8,256]{2,1,0:T(8,128)} %bitcast.10), calls=%async_computation.3 | async-start | bytes 524288 | tf_op jit(solution)/shard_map/all_to_all | solution.py:44
  179.9 12.6 %all-to-all-done.3 = f32[32,8,256]{2,1,0:T(8,128)S(1)} async-done(((f32[32,8,256]{2,1,0:T(8,128)}), f32[32,8,256]{2,1,0:T(8,128)S(1)}, u32[]{:S(2)}, u32[]{:S(2)}) %all-to-all-start.3) | async-done | bytes 262176 | tf_op jit(solution)/shard_map/all_to_all | solution.py:44
  193.3 18.3 %all_to_all.25 = f32[32,8,256]{2,1,0:T(8,128)S(1)} all-to-all(f32[32,8,256]{2,1,0:T(8,128)S(1)} %broadcast_in_dim.43), channel_id=1, replica_groups={{0,16,32,48,64,80,96,112,128,144,160,176,192,208,224,240,256,272,288,30..., dimensions={0} | all-to-all | bytes 524288 | tf_op jit(solution)/shard_map/all_to_all | solution.py:44
  211.6 4.8 %collective-permute-start.18 = (f32[64,1024]{1,0:T(8,128)S(1)}, f32[64,1024]{1,0:T(8,128)S(1)}, u32[]{:S(2)}, u32[]{:S(2)}) collective-permute-start(f32[64,1024]{1,0:T(8,128)S(1)} %bitcast.63), channel_id=1, source_target_pairs={{0,8},{8,0},{16,24},{24,16},{32,40},{40,32},{48,56},{56,48},{64,72... | collective-permute-start | bytes 786440 | tf_op jit(solution)/shard_map/ppermute | solution.py:52
  (79 shorter events, 40.7 us)
Async XLA Ops:
  0.6 37.7 %copy-start = (f32[64,512]{1,0:T(8,128)S(1)}, f32[64,512]{1,0:T(8,128)}, u32[]{:S(2)}) copy-start(f32[64,512]{1,0:T(8,128)} %param.8) | copy-start | bytes 393220
  3.4 31.1 %all-to-all-start = ((f32[8,128,512]{2,1,0:T(8,128)}), f32[8,128,512]{2,1,0:T(8,128)S(1)}, u32[]{:S(2)}, u32[]{:S(2)}) async-start(f32[8,128,512]{2,1,0:T(8,128)} %pad_maximum_fusion), calls=%async_computation | async-start | bytes 4194304 | tf_op jit(solution)/shard_map/all_to_all | solution.py:44
  40.8 6.4 %collective-permute-start = (f32[576,512]{1,0:T(8,128)}, f32[576,512]{1,0:T(8,128)S(1)}, u32[]{:S(2)}, u32[]{:S(2)}) collective-permute-start(f32[576,512]{1,0:T(8,128)} %pad_maximum_fusion.1), channel_id=1, source_target_pairs={{0,8},{8,0},{16,24},{24,16},{32,40},{40,32},{48,56},{56,48},{64,72... | collective-permute-start | bytes 3538952 | tf_op jit(solution)/shard_map/ppermute | solution.py:52
  49.6 6.8 %collective-permute-start.1 = (f32[64,512]{1,0:T(8,128)S(1)}, f32[64,512]{1,0:T(8,128)S(1)}, u32[]{:S(2)}, u32[]{:S(2)}) collective-permute-start(f32[64,512]{1,0:T(8,128)S(1)} %get-tuple-element.16), channel_id=1, source_target_pairs={{0,16},{8,24},{16,32},{24,40},{32,48},{40,56},{48,64},{56,72},{64,... | collective-permute-start | bytes 393224 | tf_op jit(solution)/shard_map/ppermute | solution.py:52
  56.8 7.3 %collective-permute-start.2 = (f32[64,512]{1,0:T(8,128)S(1)}, f32[64,512]{1,0:T(8,128)S(1)}, u32[]{:S(2)}, u32[]{:S(2)}) collective-permute-start(f32[64,512]{1,0:T(8,128)S(1)} %fusion.5), channel_id=1, source_target_pairs={{0,16},{8,24},{16,32},{24,40},{32,48},{40,56},{48,64},{56,72},{64,... | collective-permute-start | bytes 393224 | tf_op jit(solution)/shard_map/ppermute | solution.py:52
  64.5 9.7 %collective-permute-start.3 = (f32[64,512]{1,0:T(8,128)S(1)}, f32[64,512]{1,0:T(8,128)S(1)}, u32[]{:S(2)}, u32[]{:S(2)}) collective-permute-start(f32[64,512]{1,0:T(8,128)S(1)} %fusion.6), channel_id=1, source_target_pairs={{0,16},{8,24},{16,32},{24,40},{32,48},{40,56},{48,64},{56,72},{64,... | collective-permute-start | bytes 393224 | tf_op jit(solution)/shard_map/ppermute | solution.py:52
  74.2 7.7 %collective-permute-start.4 = (f32[64,512]{1,0:T(8,128)S(1)}, f32[64,512]{1,0:T(8,128)S(1)}, u32[]{:S(2)}, u32[]{:S(2)}) collective-permute-start(f32[64,512]{1,0:T(8,128)S(1)} %collective-permute-done.3), channel_id=1, source_target_pairs={{0,8},{8,0},{16,24},{24,16},{32,40},{40,32},{48,56},{56,48},{64,72... | collective-permute-start | bytes 393224 | tf_op jit(solution)/shard_map/ppermute | solution.py:52
  84.0 20.5 %all-to-all-start.1 = ((f32[8,64,512]{2,1,0:T(8,128)}), f32[8,64,512]{2,1,0:T(8,128)S(1)}, u32[]{:S(2)}, u32[]{:S(2)}) async-start(f32[8,64,512]{2,1,0:T(8,128)} %broadcast_in_dim.42), calls=%async_computation.1 | async-start | bytes 2097152 | tf_op jit(solution)/shard_map/all_to_all | solution.py:44
  88.0 16.5 %collective-permute-start.6 = (f32[64,512]{1,0:T(8,128)S(1)}, f32[64,512]{1,0:T(8,128)S(1)}, u32[]{:S(2)}, u32[]{:S(2)}) collective-permute-start(f32[64,512]{1,0:T(8,128)S(1)} %get-tuple-element.23), channel_id=1, source_target_pairs={{0,4},{1,5},{2,6},{3,7},{4,0},{5,1},{6,2},{7,3},{8,12},{9,13},{10,... | collective-permute-start | bytes 393224 | tf_op jit(solution)/shard_map/ppermute | solution.py:100
  91.7 12.8 %collective-permute-start.5 = (f32[64,512]{1,0:T(8,128)S(1)}, f32[64,512]{1,0:T(8,128)S(1)}, u32[]{:S(2)}, u32[]{:S(2)}) collective-permute-start(f32[64,512]{1,0:T(8,128)S(1)} %get-tuple-element.23), channel_id=1, source_target_pairs={{8,72},{24,88},{40,104},{56,120},{9,73},{25,89},{41,105},{57,121},... | collective-permute-start | bytes 393224 | tf_op jit(solution)/shard_map/ppermute | solution.py:52
  105.0 0.7 collective-permute-start.7
  106.8 5.2 %collective-permute-start.8 = (f32[64,512]{1,0:T(8,128)}, f32[64,512]{1,0:T(8,128)}, u32[]{:S(2)}, u32[]{:S(2)}) collective-permute-start(f32[64,512]{1,0:T(8,128)} %fusion.8), channel_id=1, source_target_pairs={{136,200},{152,216},{168,232},{184,248},{137,201},{153,217},{169,2... | collective-permute-start | bytes 393224 | tf_op jit(solution)/shard_map/ppermute | solution.py:52
  108.1 33.2 %all-to-all-start.2 = ((f32[4,256,512]{2,1,0:T(8,128)}), f32[4,256,512]{2,1,0:T(8,128)S(1)}, u32[]{:S(2)}, u32[]{:S(2)}) async-start(f32[4,256,512]{2,1,0:T(8,128)} %broadcast_in_dim.40), calls=%async_computation.2 | async-start | bytes 4194304 | tf_op jit(solution)/shard_map/all_to_all | solution.py:44
  113.3 0.7 collective-permute-start.9
  114.5 0.7 collective-permute-start.10
  115.6 0.7 collective-permute-start.11
  117.4 21.7 %collective-permute-start.15 = (f32[64,512]{1,0:T(8,128)}, f32[64,512]{1,0:T(8,128)}, u32[]{:S(2)}, u32[]{:S(2)}) collective-permute-start(f32[64,512]{1,0:T(8,128)} %fusion.12), channel_id=1, source_target_pairs={{8,76},{9,77},{10,78},{11,79},{12,72},{13,73},{14,74},{15,75},{24,... | collective-permute-start | bytes 393224 | tf_op jit(solution)/shard_map/ppermute | solution.py:111
  133.9 5.2 %collective-permute-start.14 = (f32[64,512]{1,0:T(8,128)}, f32[64,512]{1,0:T(8,128)}, u32[]{:S(2)}, u32[]{:S(2)}) collective-permute-start(f32[64,512]{1,0:T(8,128)} %fusion.12), channel_id=1, source_target_pairs={{8,68},{9,69},{10,70},{11,71},{12,64},{13,65},{14,66},{15,67},{24,... | collective-permute-start | bytes 393224 | tf_op jit(solution)/shard_map/ppermute | solution.py:111
  135.9 5.4 %collective-permute-start.13 = (f32[64,512]{1,0:T(8,128)}, f32[64,512]{1,0:T(8,128)}, u32[]{:S(2)}, u32[]{:S(2)}) collective-permute-start(f32[64,512]{1,0:T(8,128)} %fusion.12), channel_id=1, source_target_pairs={{392,456},{408,472},{424,488},{440,504},{393,457},{409,473},{425,4... | collective-permute-start | bytes 393224 | tf_op jit(solution)/shard_map/ppermute | solution.py:52
  137.2 9.4 %collective-permute-start.12 = (f32[64,512]{1,0:T(8,128)}, f32[64,512]{1,0:T(8,128)}, u32[]{:S(2)}, u32[]{:S(2)}) collective-permute-start(f32[64,512]{1,0:T(8,128)} %fusion.12), channel_id=1, source_target_pairs={{8,64},{24,80},{40,96},{56,112},{72,128},{88,144},{104,160},{120,1... | collective-permute-start | bytes 393224 | tf_op jit(solution)/shard_map/ppermute | solution.py:52
  143.3 8.3 %collective-permute-start.16 = (f32[64,1024]{1,0:T(8,128)S(1)}, f32[64,1024]{1,0:T(8,128)S(1)}, u32[]{:S(2)}, u32[]{:S(2)}) collective-permute-start(f32[64,1024]{1,0:T(8,128)S(1)} %fusion.34), channel_id=1, source_target_pairs={{0,4},{1,5},{2,6},{3,7},{4,0},{5,1},{6,2},{7,3},{8,12},{9,13},{10,... | collective-permute-start | bytes 786440 | tf_op jit(solution)/shard_map/ppermute | solution.py:120
  152.7 3.4 %collective-permute-start.17 = (f32[64,1024]{1,0:T(8,128)S(1)}, f32[64,1024]{1,0:T(8,128)S(1)}, u32[]{:S(2)}, u32[]{:S(2)}) collective-permute-start(f32[64,1024]{1,0:T(8,128)S(1)} %get-tuple-element.26), channel_id=1, source_target_pairs={{0,8},{8,0},{16,24},{24,16},{32,40},{40,32},{48,56},{56,48},{64,72... | collective-permute-start | bytes 786440 | tf_op jit(solution)/shard_map/ppermute | solution.py:52
  156.9 35.6 %all-to-all-start.3 = ((f32[32,8,256]{2,1,0:T(8,128)}), f32[32,8,256]{2,1,0:T(8,128)S(1)}, u32[]{:S(2)}, u32[]{:S(2)}) async-start(f32[32,8,256]{2,1,0:T(8,128)} %bitcast.10), calls=%async_computation.3 | async-start | bytes 524288 | tf_op jit(solution)/shard_map/all_to_all | solution.py:44
  211.6 5.9 %collective-permute-start.18 = (f32[64,1024]{1,0:T(8,128)S(1)}, f32[64,1024]{1,0:T(8,128)S(1)}, u32[]{:S(2)}, u32[]{:S(2)}) collective-permute-start(f32[64,1024]{1,0:T(8,128)S(1)} %bitcast.63), channel_id=1, source_target_pairs={{0,8},{8,0},{16,24},{24,16},{32,40},{40,32},{48,56},{56,48},{64,72... | collective-permute-start | bytes 786440 | tf_op jit(solution)/shard_map/ppermute | solution.py:52
  (7 other events, 48.6 us)
